TPU v7x, 256 devices: a whole 4x4x8 slice. The times are simulated.
256 devices in a mesh: dp: 32 (over z, x_hi, core), rep: 8 (over x_lo, y).
Axes of the slice: x: 4 (x_hi: 2, x_lo: 2; x = x_hi * 2 + x_lo), y: 4, z: 8, core: 2. Of those that a mesh axis runs over, the one named last changes fastest.
Arguments:
- image_student: float32 [8192, 512], P('dp'), may hold values from -12 to 12
- image_teacher: float32 [8192, 768], P('dp'), may hold values from -12 to 12
- text_features: float32 [8192, 512], P(('dp', 'rep')), may hold values from -12 to 12
- text_teacher: float32 [8192, 768], P(('dp', 'rep')), may hold values from -12 to 12
- head: float32 [512, 512], replicated, may hold values from -0.2 to 1.2
Outputs:
- grad_image: float32 [8192, 512], P('dp')
- grad_head: float32 [512, 512], replicated
All inputs are finite; a program needn't handle non-finite values.
Results may differ from a plain program's by a relative error of at most 0.0004.
Values sent between devices are 32-bit elements; how exact they have to be, the bound alone decides.
No kernel may reach another device: no remote copies, remote signals or barrier semaphores. Data moves between devices by JAX's collectives and lax.ppermute only.
A program may use at most 64 MiB of HBM per device.

v0:
```python
import math

import jax
import jax.numpy as jnp
from jax import lax
from jax.sharding import PartitionSpec as P


def from_behind(shard, axis, by):
    devices = lax.axis_size(axis)
    return lax.ppermute(shard, axis, [(i, (i + by) % devices) for i in range(devices)])


def combined_all(shard, axis, combine):
    everything = jax.tree.map(lambda part: lax.all_gather(part, axis), shard)
    first = jax.tree.map(lambda part: part[0], everything)

    def lap(k, so_far):
        return combine(so_far, jax.tree.map(lambda part: part[k], everything))

    return lax.fori_loop(1, lax.axis_size(axis), lap, first)


def logits(block, queries, scale):
    return scale * lax.dot_general(
        block,
        queries,
        (((1,), (1,)), ((), ())),
        precision=lax.Precision.HIGHEST,
        preferred_element_type=jnp.float32,
    )


def online(top, total, tile):
    new_top = jnp.maximum(top, jnp.max(tile, axis=0))
    total = total * jnp.exp(top - new_top) + jnp.sum(jnp.exp(tile - new_top[None, :]), axis=0)
    return (new_top, total)


def first_move(payload):
    return from_behind(payload, "dp", 1)


def second_move(payload):
    return from_behind(payload, "dp", 1)


def combine_totals(first, second):
    top_s = jnp.maximum(first[0], second[0])
    sum_s = first[1] * jnp.exp(first[0] - top_s) + second[1] * jnp.exp(second[0] - top_s)
    top_t = jnp.maximum(first[2], second[2])
    sum_t = first[3] * jnp.exp(first[2] - top_t) + second[3] * jnp.exp(second[2] - top_t)
    return (top_s, sum_s, top_t, sum_t)


def shards(image_student, image_teacher, text_features, text_teacher, head):
    highest = lax.Precision.HIGHEST
    steps = lax.axis_size("dp")
    rows = image_student.shape[0]
    width_s = image_student.shape[1]
    width_t = image_teacher.shape[1]
    texts = text_features.shape[0]
    scale_s = 4.0 / math.sqrt(width_s)
    scale_t = 4.0 / math.sqrt(width_t)
    text_student = jnp.dot(
        text_features, head, precision=highest, preferred_element_type=jnp.float32
    )
    payload = jnp.concatenate([text_student, text_teacher], axis=1)
    lowest = jnp.full((rows,), -jnp.inf, jnp.float32)
    nothing = jnp.zeros((rows,), jnp.float32)
    stored = ()

    def first_step(index, carry):
        block, top_s, sum_s, top_t, sum_t, kept = carry
        tile_s = logits(block[:, :width_s], image_student, scale_s)
        tile_t = logits(block[:, width_s:], image_teacher, scale_t)
        top_s, sum_s = online(top_s, sum_s, tile_s)
        top_t, sum_t = online(top_t, sum_t, tile_t)
        return (first_move(block), top_s, sum_s, top_t, sum_t, kept)

    payload, top_s, sum_s, top_t, sum_t, stored = lax.fori_loop(
        0, steps, first_step, (payload, lowest, nothing, lowest, nothing, stored)
    )
    top_s, sum_s, top_t, sum_t = combined_all((top_s, sum_s, top_t, sum_t), "rep", combine_totals)
    lse_student = top_s + jnp.log(sum_s)
    lse_teacher = top_t + jnp.log(sum_t)
    blank = jnp.zeros((texts, width_s), jnp.float32)
    moving = jnp.concatenate([payload, blank], axis=1)

    def second_step(index, carry):
        block, rows_grad = carry
        student_block = block[:, :width_s]
        tile_s = logits(student_block, image_student, scale_s)
        tile_t = logits(block[:, width_s : width_s + width_t], image_teacher, scale_t)
        gap = jnp.exp(tile_s - lse_student[None, :]) - jnp.exp(tile_t - lse_teacher[None, :])
        rows_grad = rows_grad + scale_s * lax.dot_general(
            gap,
            student_block,
            (((0,), (0,)), ((), ())),
            precision=highest,
            preferred_element_type=jnp.float32,
        )
        accrued = block[:, -width_s:] + scale_s * jnp.dot(
            gap, image_student, precision=highest, preferred_element_type=jnp.float32
        )
        block = jnp.concatenate([block[:, :-width_s], accrued], axis=1)
        return (second_move(block), rows_grad)

    moving, rows_grad = lax.fori_loop(
        0, steps, second_step, (moving, jnp.zeros((rows, width_s), jnp.float32))
    )
    grad_text = moving[:, -width_s:]
    head_term = lax.dot_general(
        text_features,
        grad_text,
        (((0,), (0,)), ((), ())),
        precision=highest,
        preferred_element_type=jnp.float32,
    )
    grad_image = lax.psum(rows_grad, "rep")
    grad_head = lax.psum(head_term, ("dp", "rep")) / math.sqrt(rows * steps)
    return (grad_image, grad_head)


def solution(mesh):
    in_specs = (P("dp", None), P("dp", None), P(("dp", "rep"), None), P(("dp", "rep"), None), P())
    out_specs = (P("dp", None), P())
    return jax.shard_map(shards, mesh=mesh, in_specs=in_specs, out_specs=out_specs, check_vma=False)
```

profile of v0, /device:TPU:1, one launch (start us, length us, event | category | flops | bytes accessed | tf_op | source)
XLA Modules:
  0.0 1077.1 jit_solution(7093232556288906080)
XLA Ops:
  10.1 266.9 %while.54 = (s32[]{:T(128)}, f32[32,1280]{1,0:T(8,128)S(1)}, f32[256]{0:T(256)S(1)}, f32[256]{0:T(256)S(1)}, f32[256]{0:T(256)S(1)}, /*index=5*/f32[256]{0:T(256...) while((s32[]{:T(128)}, f32[32,1280]{1,0:T(8,128)S(1)}, ...), condition=%wide.region_5.0_spmd.clone, body=%wide.region_0.0_spmd.clone.sunk | while | flops 125897216 | bytes 2615449 | solution.py:81
  277.0 14.7 %all-gather.7 = f32[8,1,256]{2,1,0:T(1,128)S(1)} all-gather(f32[1,1,256]{2,1,0:T(1,128)S(1)} %bitcast.68), channel_id=5, replica_groups=mesh['dp'=32,'rep'=8] {'rep'}, dimensions={0}, use_global_device_ids=true | all-gather | bytes 9216 | tf_op jit(solution)/shard_map/all_gather | solution.py:15
  291.7 11.6 %all-gather.4 = f32[8,1,256]{2,1,0:T(1,128)S(1)} all-gather(f32[1,1,256]{2,1,0:T(1,128)S(1)} %bitcast.59), channel_id=2, replica_groups=mesh['dp'=32,'rep'=8] {'rep'}, dimensions={0}, use_global_device_ids=true | all-gather | bytes 9216 | tf_op jit(solution)/shard_map/all_gather | solution.py:15
  303.3 13.2 %all-gather.5 = f32[8,1,256]{2,1,0:T(1,128)S(1)} all-gather(f32[1,1,256]{2,1,0:T(1,128)S(1)} %bitcast.69), channel_id=3, replica_groups=mesh['dp'=32,'rep'=8] {'rep'}, dimensions={0}, use_global_device_ids=true | all-gather | bytes 9216 | tf_op jit(solution)/shard_map/all_gather | solution.py:15
  316.4 11.6 %all-gather.6 = f32[8,1,256]{2,1,0:T(1,128)S(1)} all-gather(f32[1,1,256]{2,1,0:T(1,128)S(1)} %bitcast.58), channel_id=4, replica_groups=mesh['dp'=32,'rep'=8] {'rep'}, dimensions={0}, use_global_device_ids=true | all-gather | bytes 9216 | tf_op jit(solution)/shard_map/all_gather | solution.py:15
  328.9 399.1 %while.55 = (s32[]{:T(128)}, f32[32,1792]{1,0:T(8,128)S(1)}, f32[256,512]{1,0:T(8,128)S(1)}, f32[256,512]{1,0:T(8,128)S(1)}, f32[256]{0:T(256)S(1)}, /*index=5*/...) while((s32[]{:T(128)}, f32[32,1792]{1,0:T(8,128)S(1)}, f32[256,512]{1,0:T(8,128)S(1)}, ...), condition=%wide.region_9.0_spmd.clone, body=%wide.region_8.0_spmd.clone.sunk | while | flops 227016704 | bytes 5572751 | solution.py:109
  330.8 13.0 %collective-permute-start.1 = (f32[32,1792]{1,0:T(8,128)S(1)}, f32[32,1792]{1,0:T(8,128)}, u32[]{:S(2)}, u32[]{:S(2)}) collective-permute-start(f32[32,1792]{1,0:T(8,128)S(1)} %pad_maximum_fusion.3), channel_id=1, source_target_pairs={{0,8},{8,16},{16,24},{24,32},{32,40},{40,48},{48,56},{56,64},{64,7... | collective-permute-start | bytes 688136 | tf_op jit(solution)/shard_map/while/body/eval_jaxpr/ppermute | solution.py:11
  344.5 9.3 collective-permute-done.1
  357.4 8.5 collective-permute-done.1
  369.4 8.5 collective-permute-done.1
  381.5 8.4 collective-permute-done.1
  393.5 8.5 collective-permute-done.1
  405.5 8.4 collective-permute-done.1
  429.6 8.5 collective-permute-done.1
  441.7 8.4 collective-permute-done.1
  465.7 8.5 collective-permute-done.1
  477.8 8.4 collective-permute-done.1
  501.8 8.5 collective-permute-done.1
  513.9 8.4 collective-permute-done.1
  538.0 8.5 collective-permute-done.1
  550.0 8.4 collective-permute-done.1
  574.1 8.5 collective-permute-done.1
  586.1 8.4 collective-permute-done.1
  610.2 8.5 collective-permute-done.1
  622.2 8.4 collective-permute-done.1
  646.3 8.5 collective-permute-done.1
  658.4 8.4 collective-permute-done.1
  682.4 8.5 collective-permute-done.1
  694.5 8.4 collective-permute-done.1
  718.5 8.5 collective-permute-done.1
  730.7 259.1 %all-reduce.6.cloned.1.call-done = f32[512,512]{0,1:T(8,128)} async-done(((f32[512,512]{0,1:T(8,128)}), f32[512,512]{0,1:T(8,128)}) %all-reduce.6.cloned.1.call-update) | async-done | bytes 1048592 | tf_op jit(solution)/shard_map/psum | solution.py:121
  992.5 75.9 %all-reduce.4.cloned.1.call-done = f32[256,512]{1,0:T(8,128)} async-done(((f32[256,512]{1,0:T(8,128)}), f32[256,512]{1,0:T(8,128)}) %all-reduce.4.cloned.1.call-update) | async-done | bytes 524304 | tf_op jit(solution)/shard_map/psum | solution.py:120
  (721 shorter events, 465.4 us)
Async XLA Ops:
  7.2 982.7 %all-reduce.6.cloned.1.call-start = ((), (), s32[]{:S(2)}) async-start(), calls=%async_computation.1 | async-start | bytes 2097152 | tf_op jit(solution)/shard_map/psum | solution.py:121
  330.8 23.0 %collective-permute-start.1 = (f32[32,1792]{1,0:T(8,128)S(1)}, f32[32,1792]{1,0:T(8,128)}, u32[]{:S(2)}, u32[]{:S(2)}) collective-permute-start(f32[32,1792]{1,0:T(8,128)S(1)} %pad_maximum_fusion.3), channel_id=1, source_target_pairs={{0,8},{8,16},{16,24},{24,32},{32,40},{40,48},{48,56},{56,64},{64,7... | collective-permute-start | bytes 688136 | tf_op jit(solution)/shard_map/while/body/eval_jaxpr/ppermute | solution.py:11
  356.6 9.2 collective-permute-start.1
  368.6 9.2 collective-permute-start.1
  380.7 9.2 collective-permute-start.1
  392.7 9.2 collective-permute-start.1
  404.7 9.2 collective-permute-start.1
  416.8 9.2 collective-permute-start.1
  428.8 9.2 collective-permute-start.1
  440.9 9.2 collective-permute-start.1
  452.9 9.2 collective-permute-start.1
  464.9 9.2 collective-permute-start.1
  477.0 9.2 collective-permute-start.1
  489.0 9.2 collective-permute-start.1
  501.1 9.2 collective-permute-start.1
  513.1 9.2 collective-permute-start.1
  525.1 9.2 collective-permute-start.1
  537.2 9.2 collective-permute-start.1
  549.2 9.2 collective-permute-start.1
  561.3 9.2 collective-permute-start.1
  573.3 9.2 collective-permute-start.1
  597.4 9.2 collective-permute-start.1
  609.4 9.2 collective-permute-start.1
  621.4 9.2 collective-permute-start.1
  633.5 9.2 collective-permute-start.1
  645.5 9.2 collective-permute-start.1
  657.6 9.2 collective-permute-start.1
  669.6 9.2 collective-permute-start.1
  681.6 9.2 collective-permute-start.1
  705.7 9.2 collective-permute-start.1
  717.8 9.2 collective-permute-start.1
  730.0 338.4 %all-reduce.4.cloned.1.call-start = ((), (), s32[]{:S(2)}) async-start(), calls=%async_computation | async-start | bytes 1048576 | tf_op jit(solution)/shard_map/psum | solution.py:120
  (40 other events, 694.6 us)
Sparse Core Ops, SparseCore 0:
  730.1 259.7 all-reduce.5
  993.2 75.0 all-reduce.3
where the time goes:
time: 1080 us
  waiting for transfers between devices  808 us (75%)
  matrix products  128 us (12%)
  blocking collectives  51 us (5%)
  local copies, waits for them, and re-layouts  35.6 us (3%)
  starting transfers between devices  31.3 us (3%)
  between operations  14.2 us (1%)
    ppermute x64, waiting for transfers between devices, from_behind(): lax.ppermute(shard, axis, [(i, (i + by) % devices) for i in range(devices)])  473 us
    psum x1, waiting for transfers between devices, shards(): grad_head = lax.psum(head_term, ('dp', 'rep')) / math.sqrt(rows * steps)  259 us
    dot_general x128, matrix products, logits(): lax.dot_general(block, queries, (((1,), (1,)), ((), ())), precision=lax.P...  89.2 us
    psum x1, waiting for transfers between devices, shards(): grad_image = lax.psum(rows_grad, 'rep')  75.9 us
    all_gather x4, blocking collectives, combined_all(): everything = jax.tree.map(lambda part: lax.all_gather(part, axis), shard)  51 us
    ppermute x64, starting transfers between devices, from_behind(): lax.ppermute(shard, axis, [(i, (i + by) % devices) for i in range(devices)])  31.2 us
    while x128, local copies, waits for them, and re-layouts  30.6 us
    dot_general x32, matrix products, second_step(): lax.dot_general(gap, student_block, (((0,), (0,)), ((), ())), precision=h...  21.9 us
  transfers between devices with their start and end apart: 66, of which 66 were waited for; matrix products, arithmetic and copies ran while one was open for 7% of the time, Pallas kernels for 0%

commit v1 on v0

v1 whole, which is shorter than its diff:
```python
import math

import jax
import jax.numpy as jnp
from jax import lax
from jax.sharding import Mesh, PartitionSpec as P

AXES = ("z", "xh", "core", "xl", "y")
SIZES = (8, 2, 2, 2, 4)
HIGH = lax.Precision.HIGH


def linear(z, xh, core, xl, y):
    return (((z * 2 + xh) * 2 + core) * 2 + xl) * 4 + y


def moves(place):
    pairs = []
    for z in range(8):
        for xh in range(2):
            for core in range(2):
                for xl in range(2):
                    for y in range(4):
                        here = (z, xh, core, xl, y)
                        pairs.append((linear(*here), linear(*place(*here))))
    return pairs


Z_UP = moves(lambda z, xh, core, xl, y: ((z + 1) % 8, xh, core, xl, y))
Z_DOWN = moves(lambda z, xh, core, xl, y: ((z + 7) % 8, xh, core, xl, y))
X_FLIP = moves(lambda z, xh, core, xl, y: (z, 1 - xh, core, 1 - xl, y))
X_FAR = moves(lambda z, xh, core, xl, y: (z, 1 - xh, core, xl, y))
CORE = moves(lambda z, xh, core, xl, y: (z, xh, 1 - core, xl, y))
Z_FOLD = tuple(
    moves(lambda z, xh, core, xl, y, bit=bit: (z ^ bit, xh, core, xl, y)) for bit in (1, 2, 4)
)


def move(array, pairs):
    return lax.ppermute(array, AXES, pairs)


def dot(a, b, dims):
    return lax.dot_general(
        a, b, (dims, ((), ())), precision=HIGH, preferred_element_type=jnp.float32
    )


def part(folded, images, texts, width):
    features = texts[:, :width]
    student = dot(folded, features, ((1,), (1,)))
    teacher = dot(images, texts[:, width:], ((1,), (1,)))
    outs = []
    for tile in (student, teacher):
        top = jnp.max(tile, axis=1, keepdims=True)
        weight = jnp.exp(tile - top)
        total = jnp.sum(weight, axis=1, keepdims=True)
        outs.append((top, total, dot(weight, features, ((1,), (0,)))))
    return outs


def merged(first, second):
    top = jnp.maximum(first[0], second[0])
    a = jnp.exp(first[0] - top)
    b = jnp.exp(second[0] - top)
    return (top, first[1] * a + second[1] * b, first[2] * a + second[2] * b)


def shards(image_student, image_teacher, text_features, text_teacher, head):
    rows, width = image_student.shape
    scale_s = 4.0 / math.sqrt(width)
    scale_t = 4.0 / math.sqrt(image_teacher.shape[1])
    batch = rows * 32
    folded = scale_s * dot(image_student, head, ((1,), (1,)))
    images = scale_t * image_teacher

    own = jnp.concatenate([text_features, text_teacher], axis=1)
    up, down = move(own, Z_UP), move(own, Z_DOWN)
    group1 = jnp.concatenate([own, up, down], axis=0)
    up, down = move(up, Z_UP), move(down, Z_DOWN)
    across1 = move(group1, X_FLIP)
    group2 = jnp.concatenate([up, down], axis=0)
    up, down = move(up, Z_UP), move(down, Z_DOWN)
    across2 = move(group2, X_FLIP)
    group3 = jnp.concatenate([up, down], axis=0)
    up = move(up, Z_UP)
    across3 = move(group3, X_FLIP)
    across4 = move(up, X_FLIP)
    early = [group1, group2, across1]
    late = [group3, up, across2]
    last = [across3, across4]
    state = None
    for blocks in (early, late, last):
        texts = jnp.concatenate(blocks + [move(block, CORE) for block in blocks], axis=0)
        fresh = part(folded, images, texts, width)
        state = fresh if state is None else [merged(a, b) for a, b in zip(state, fresh)]
    (top_s, sum_s, prod_s), (top_t, sum_t, prod_t) = state

    columns = width // 8
    both = jnp.concatenate(
        [prod_s.reshape(rows, 8, columns), prod_t.reshape(rows, 8, columns)], axis=2
    ).transpose(1, 0, 2)
    stats = jnp.concatenate([top_s, sum_s, top_t, sum_t], axis=1).T.reshape(8, 128)
    both = jnp.concatenate([both, jnp.broadcast_to(stats[None], (8, 8, 128))], axis=1)
    both = lax.all_to_all(both, ("xl", "y"), 0, 0, tiled=True)
    stats = both[:, rows:, :].reshape(8, 4, rows)
    both = both[:, :rows, :]
    factors = []
    for k in (0, 2):
        tops = stats[:, k]
        top = jnp.max(tops, axis=0)
        shares = jnp.exp(tops - top[None])
        total = jnp.sum(shares * stats[:, k + 1], axis=0)
        factors.append(shares / total[None])
    summed_s = jnp.sum(both[:, :, :columns] * factors[0][:, :, None], axis=0)
    summed_t = jnp.sum(both[:, :, columns:] * factors[1][:, :, None], axis=0)
    gap_text = summed_s - summed_t

    term = dot(gap_text, image_student, ((0,), (0,)))
    core = lax.axis_index("core")
    half = columns // 2
    mine = lax.dynamic_slice_in_dim(term, core * half, half, 0)
    other = lax.dynamic_slice_in_dim(term, (1 - core) * half, half, 0)
    term = mine + move(other, CORE)
    for pairs in Z_FOLD + (X_FAR,):
        term = term + move(term, pairs)

    payload = jnp.concatenate(
        [
            jnp.concatenate([gap_text[: rows // 2], gap_text[rows // 2 :]], axis=1),
            term.reshape(half, 4, 128).transpose(1, 0, 2).reshape(4 * half, 128),
        ],
        axis=0,
    )
    payload = lax.all_to_all(
        jnp.broadcast_to(payload[None], (8,) + payload.shape), ("xl", "y"), 0, 0, tiled=True
    )
    gap_text = payload[:, : rows // 2].reshape(8, rows // 2, 2, columns)
    gap_text = gap_text.transpose(2, 1, 0, 3).reshape(rows, width)
    grad_image = scale_s * dot(gap_text, head, ((1,), (0,)))
    term = payload[:, rows // 2 :].reshape(8, 4, half, 128).transpose(0, 2, 1, 3).reshape(8, half, width)
    partner = move(term, CORE)
    low = jnp.where(core == 0, term, partner)
    high = jnp.where(core == 0, partner, term)
    grad_head = jnp.stack([low, high], axis=1).reshape(width, width)
    return (grad_image, grad_head * (scale_s / math.sqrt(batch)))


def solution(mesh):
    fine = Mesh(mesh.devices.reshape(SIZES), AXES)
    dp, every = ("z", "xh", "core"), AXES
    in_specs = (P(dp, None), P(dp, None), P(every, None), P(every, None), P())
    out_specs = (P(dp, None), P())
    return jax.shard_map(shards, mesh=fine, in_specs=in_specs, out_specs=out_specs, check_vma=False)
```

time: 1080 us -> 142 us (0.13)
  waiting for transfers between devices: 808 us -> 56.4 us
  matrix products: 128 us -> 13.7 us
  blocking collectives: 51 us -> 13.6 us
  local copies, waits for them, and re-layouts: 35.6 us -> 8.38 us
  between operations: 14.2 us -> 1.32 us
  starting transfers between devices: 31.3 us -> 42.6 us
    ppermute x64 -> x25, waiting for transfers between devices: 473 us -> 41 us  [move(): return lax.ppermute(array, AXES, pairs)]
    psum x2 -> x0, waiting for transfers between devices: 335 us -> none  [the longest x1 259 us: shards(): grad_head = lax.psum(head_term, ('dp', 'rep')) / math.sqrt(rows * steps)]
    dot_general x194 -> x15, matrix products: 128 us -> 13.7 us  [dot(): lax.dot_general(a, b, (dims, ((), ())), precision=HIGH, preferred_element...]
    all_gather x4 -> x0, blocking collectives: 51 us -> none  [combined_all(): everything = jax.tree.map(lambda part: lax.all_gather(part, axis), shard)]
    while x128 -> x0, local copies, waits for them, and re-layouts: 30.6 us -> none
    all_to_all x0 -> x1, waiting for transfers between devices: none -> 15.4 us  [shards(): both = lax.all_to_all(both, ('xl', 'y'), 0, 0, tiled=True)]
    all_to_all x0 -> x1, blocking collectives: none -> 13.6 us  [shards(): lax.all_to_all(jnp.broadcast_to(payload[None], (8,) + payload.shape), ('x...]
    ppermute x64 -> x25, starting transfers between devices: 31.2 us -> 38.2 us  [move(): return lax.ppermute(array, AXES, pairs)]
  transfers between devices with their start and end apart: 66 -> 26, of which waited for: 66 -> 13; matrix products, arithmetic and copies ran while one was open for 7% -> 6% of each run, Pallas kernels for 0% -> 0%
where the time goes in v1:
time: 142 us
  waiting for transfers between devices  56.4 us (40%)
  starting transfers between devices  42.6 us (30%)
  matrix products  13.7 us (10%)
  blocking collectives  13.6 us (10%)
  local copies, waits for them, and re-layouts  8.38 us (6%)
  other arithmetic  5.93 us (4%)
    ppermute x25, waiting for transfers between devices, move(): return lax.ppermute(array, AXES, pairs)  41 us
    ppermute x25, starting transfers between devices, move(): return lax.ppermute(array, AXES, pairs)  38.2 us
    all_to_all x1, waiting for transfers between devices, shards(): both = lax.all_to_all(both, ('xl', 'y'), 0, 0, tiled=True)  15.4 us
    dot_general x15, matrix products, dot(): lax.dot_general(a, b, (dims, ((), ())), precision=HIGH, preferred_element...  13.7 us
    all_to_all x1, blocking collectives, shards(): lax.all_to_all(jnp.broadcast_to(payload[None], (8,) + payload.shape), ('x...  13.6 us
    all_to_all x1, starting transfers between devices, shards(): both = lax.all_to_all(both, ('xl', 'y'), 0, 0, tiled=True)  4.32 us
    reduce_sum x6, other arithmetic, part(): total = jnp.sum(weight, axis=1, keepdims=True)  3.44 us
  transfers between devices with their start and end apart: 26, of which 13 were waited for; matrix products, arithmetic and copies ran while one was open for 6% of the time, Pallas kernels for 0%

profile of v1, /device:TPU:1, one launch (start us, length us, event | category | flops | bytes accessed | tf_op | source)
XLA Modules:
  0.0 141.8 jit_solution(6809667635505734936)
XLA Ops:
  2.5 2.5 %collective-permute-start = (f32[32,1280]{1,0:T(8,128)S(1)}, f32[32,1280]{1,0:T(8,128)S(1)}, u32[]{:S(2)}, u32[]{:S(2)}) collective-permute-start(f32[32,1280]{1,0:T(8,128)S(1)} %get-tuple-element.23), channel_id=1, source_target_pairs={{0,32},{1,33},{2,34},{3,35},{4,36},{5,37},{6,38},{7,39},{8,40},{9,... | collective-permute-start | bytes 491528 | tf_op jit(solution)/shard_map/ppermute | solution.py:40
  5.0 4.0 %collective-permute-start.1 = (f32[32,1280]{1,0:T(8,128)S(1)}, f32[32,1280]{1,0:T(8,128)S(1)}, u32[]{:S(2)}, u32[]{:S(2)}) collective-permute-start(f32[32,1280]{1,0:T(8,128)S(1)} %get-tuple-element.23), channel_id=1, source_target_pairs={{0,224},{1,225},{2,226},{3,227},{4,228},{5,229},{6,230},{7,231},{8... | collective-permute-start | bytes 491528 | tf_op jit(solution)/shard_map/ppermute | solution.py:40
  9.1 1.7 %convolution_multiply_fusion.3 = f32[256,512]{1,0:T(8,128)S(1)} fusion(f32[256,512]{1,0:T(8,128)} %param.5, f32[512,512]{1,0:T(8,128)S(1)} %copy-done), kind=kOutput, calls=%fused_computation.6 | convolution fusion | flops 402784256 | bytes 2097152 | tf_op jit(solution)/shard_map/dot_general | solution.py:44
  10.7 2.2 %collective-permute-done = f32[32,1280]{1,0:T(8,128)S(1)} collective-permute-done((f32[32,1280]{1,0:T(8,128)S(1)}, f32[32,1280]{1,0:T(8,128)S(1)}, u32[]{:S(2)}, u32[]{:S(2)}) %collective-permute-start) | collective-permute-done | bytes 163872 | tf_op jit(solution)/shard_map/ppermute | solution.py:40
  12.9 2.6 %collective-permute-start.4 = (f32[96,1280]{1,0:T(8,128)S(1)}, f32[96,1280]{1,0:T(8,128)S(1)}, u32[]{:S(2)}, u32[]{:S(2)}) collective-permute-start(f32[96,1280]{1,0:T(8,128)S(1)} %pad_maximum_fusion.1), channel_id=1, source_target_pairs={{0,20},{1,21},{2,22},{3,23},{4,16},{5,17},{6,18},{7,19},{8,28},{9,... | collective-permute-start | bytes 1474568 | tf_op jit(solution)/shard_map/ppermute | solution.py:40
  15.5 1.5 %collective-permute-start.5 = (f32[96,1280]{1,0:T(8,128)S(1)}, f32[96,1280]{1,0:T(8,128)S(1)}, u32[]{:S(2)}, u32[]{:S(2)}) collective-permute-start(f32[96,1280]{1,0:T(8,128)S(1)} %pad_maximum_fusion.1), channel_id=1, source_target_pairs={{0,8},{1,9},{2,10},{3,11},{4,12},{5,13},{6,14},{7,15},{8,0},{9,1},... | collective-permute-start | bytes 1474568 | tf_op jit(solution)/shard_map/ppermute | solution.py:40
  17.0 2.8 %collective-permute-start.3 = (f32[32,1280]{1,0:T(8,128)S(1)}, f32[32,1280]{1,0:T(8,128)S(1)}, u32[]{:S(2)}, u32[]{:S(2)}) collective-permute-start(f32[32,1280]{1,0:T(8,128)S(1)} %collective-permute-done.1), channel_id=1, source_target_pairs={{0,224},{1,225},{2,226},{3,227},{4,228},{5,229},{6,230},{7,231},{8... | collective-permute-start | bytes 491528 | tf_op jit(solution)/shard_map/ppermute | solution.py:40
  19.8 4.4 %collective-permute-done.2 = f32[32,1280]{1,0:T(8,128)S(1)} collective-permute-done((f32[32,1280]{1,0:T(8,128)S(1)}, f32[32,1280]{1,0:T(8,128)S(1)}, u32[]{:S(2)}, u32[]{:S(2)}) %collective-permute-start.2) | collective-permute-done | bytes 163872 | tf_op jit(solution)/shard_map/ppermute | solution.py:40
  25.6 4.9 %collective-permute-done.8 = f32[32,1280]{1,0:T(8,128)S(1)} collective-permute-done((f32[32,1280]{1,0:T(8,128)S(1)}, f32[32,1280]{1,0:T(8,128)S(1)}, u32[]{:S(2)}, u32[]{:S(2)}) %collective-permute-start.8) | collective-permute-done | bytes 163872 | tf_op jit(solution)/shard_map/ppermute | solution.py:40
  30.6 4.4 %collective-permute-done.9 = f32[32,1280]{1,0:T(8,128)S(1)} collective-permute-done((f32[32,1280]{1,0:T(8,128)S(1)}, f32[32,1280]{1,0:T(8,128)S(1)}, u32[]{:S(2)}, u32[]{:S(2)}) %collective-permute-start.9) | collective-permute-done | bytes 163872 | tf_op jit(solution)/shard_map/ppermute | solution.py:40
  35.0 2.5 %collective-permute-start.12 = (f32[64,1280]{1,0:T(8,128)S(1)}, f32[64,1280]{1,0:T(8,128)S(1)}, u32[]{:S(2)}, u32[]{:S(2)}) collective-permute-start(f32[64,1280]{1,0:T(8,128)S(1)} %get-tuple-element.15), channel_id=1, source_target_pairs={{0,8},{1,9},{2,10},{3,11},{4,12},{5,13},{6,14},{7,15},{8,0},{9,1},... | collective-permute-start | bytes 983048 | tf_op jit(solution)/shard_map/ppermute | solution.py:40
  37.9 6.6 %collective-permute-done.10 = f32[32,1280]{1,0:T(8,128)S(1)} collective-permute-done((f32[32,1280]{1,0:T(8,128)S(1)}, f32[32,1280]{1,0:T(8,128)S(1)}, u32[]{:S(2)}, u32[]{:S(2)}) %collective-permute-start.10) | collective-permute-done | bytes 163872 | tf_op jit(solution)/shard_map/ppermute | solution.py:40
  46.1 2.1 %collective-permute-done.15 = f32[64,1280]{1,0:T(8,128)S(1)} collective-permute-done((f32[64,1280]{1,0:T(8,128)S(1)}, f32[64,1280]{1,0:T(8,128)S(1)}, u32[]{:S(2)}, u32[]{:S(2)}) %collective-permute-start.15) | collective-permute-done | bytes 327712 | tf_op jit(solution)/shard_map/ppermute | solution.py:40
  48.4 1.4 %collective-permute-start.17 = (f32[64,1280]{1,0:T(8,128)S(1)}, f32[64,1280]{1,0:T(8,128)S(1)}, u32[]{:S(2)}, u32[]{:S(2)}) collective-permute-start(f32[64,1280]{1,0:T(8,128)S(1)} %collective-permute-done.15), channel_id=1, source_target_pairs={{0,8},{1,9},{2,10},{3,11},{4,12},{5,13},{6,14},{7,15},{8,0},{9,1},... | collective-permute-start | bytes 983048 | tf_op jit(solution)/shard_map/ppermute | solution.py:40
  49.8 4.4 %collective-permute-done.16 = f32[32,1280]{1,0:T(8,128)S(1)} collective-permute-done((f32[32,1280]{1,0:T(8,128)S(1)}, f32[32,1280]{1,0:T(8,128)S(1)}, u32[]{:S(2)}, u32[]{:S(2)}) %collective-permute-start.16) | collective-permute-done | bytes 163872 | tf_op jit(solution)/shard_map/ppermute | solution.py:40
  54.2 1.8 %collective-permute-start.18 = (f32[32,1280]{1,0:T(8,128)S(1)}, f32[32,1280]{1,0:T(8,128)S(1)}, u32[]{:S(2)}, u32[]{:S(2)}) collective-permute-start(f32[32,1280]{1,0:T(8,128)S(1)} %collective-permute-done.16), channel_id=1, source_target_pairs={{0,8},{1,9},{2,10},{3,11},{4,12},{5,13},{6,14},{7,15},{8,0},{9,1},... | collective-permute-start | bytes 491528 | tf_op jit(solution)/shard_map/ppermute | solution.py:40
  64.6 1.2 fusion.5
  65.9 2.0 %copy.41 = f32[256,512]{0,1:T(8,128)} copy(f32[256,512]{1,0:T(8,128)} %fusion.5) | data formatting | bytes 1048576 | tf_op jit(solution)/shard_map/add | solution.py:66
  69.6 1.9 %fusion.6 = f32[256,512]{1,0:T(8,128)S(1)} fusion(f32[256,512]{1,0:T(8,128)S(1)} %convolution_multiply_fusion.4, f32[512,1280]{1,0:T(8,128)} %copy-done.1, f32[256,512]{1,0:T(8,128)S(1)} %get-tuple-element.43, f32[256]{0:T(256)S(1)} %get-tuple-element.35, f32[256]{0:T(256)S(1)} %get-tuple-element.38, f32[256]{0:T(256)S(1)} %get-tuple-element.42), kind=kOutput, calls=%fused_computation.15 | convolution fusion | flops 403177472 | bytes 2624512 | tf_op jit(solution)/shard_map/dot_general | solution.py:44
  71.6 1.4 %fusion.4 = f32[256,512]{1,0:T(8,128)S(1)} fusion(f32[256,512]{1,0:T(8,128)S(1)} %fusion.6, f32[192,1280]{1,0:T(8,128)} %copy-done.3, f32[256]{0:T(256)S(1)} %get-tuple-element.34, f32[256,192]{0,1:T(8,128)S(1)} %copy-done.7, f32[256]{0:T(256)S(1)} %copy-done.11), kind=kOutput, calls=%fused_computation.12 | convolution fusion | flops 151306240 | bytes 1640448 | tf_op jit(solution)/shard_map/dot_general | solution.py:44
  73.7 1.5 %copy.44 = f32[8,264,128]{2,1,0:T(8,128)} copy(f32[8,264,128]{1,2,0:T(8,128)S(1)} %pad_maximum_fusion) | data formatting | bytes 2162688 | tf_op jit(solution)/shard_map/concatenate | solution.py:104
  75.2 4.3 %all-to-all-start = ((f32[8,264,128]{2,1,0:T(8,128)}), f32[8,264,128]{2,1,0:T(8,128)S(1)}, u32[]{:S(2)}, u32[]{:S(2)}) async-start(f32[8,264,128]{2,1,0:T(8,128)} %copy.44), calls=%async_computation | async-start | bytes 2162688 | tf_op jit(solution)/shard_map/all_to_all | solution.py:105
  79.5 15.4 %all-to-all-done = f32[8,264,128]{2,1,0:T(8,128)S(1)} async-done(((f32[8,264,128]{2,1,0:T(8,128)}), f32[8,264,128]{2,1,0:T(8,128)S(1)}, u32[]{:S(2)}, u32[]{:S(2)}) %all-to-all-start) | async-done | bytes 1081376 | tf_op jit(solution)/shard_map/all_to_all | solution.py:105
  98.5 2.9 %collective-permute-done.20 = f32[32,512]{1,0:T(8,128)S(1)} collective-permute-done((f32[32,512]{1,0:T(8,128)S(1)}, f32[32,512]{1,0:T(8,128)S(1)}, u32[]{:S(2)}, u32[]{:S(2)}) %collective-permute-start.20) | collective-permute-done | bytes 65568 | tf_op jit(solution)/shard_map/ppermute | solution.py:40
  101.5 2.9 %collective-permute-start.21 = (f32[32,512]{1,0:T(8,128)S(1)}, f32[32,512]{1,0:T(8,128)S(1)}, u32[]{:S(2)}, u32[]{:S(2)}) collective-permute-start(f32[32,512]{1,0:T(8,128)S(1)} %add.88), channel_id=1, source_target_pairs={{0,64},{1,65},{2,66},{3,67},{4,68},{5,69},{6,70},{7,71},{8,72},{9,... | collective-permute-start | bytes 196616 | tf_op jit(solution)/shard_map/ppermute | solution.py:40
  104.4 1.7 %collective-permute-done.21 = f32[32,512]{1,0:T(8,128)S(1)} collective-permute-done((f32[32,512]{1,0:T(8,128)S(1)}, f32[32,512]{1,0:T(8,128)S(1)}, u32[]{:S(2)}, u32[]{:S(2)}) %collective-permute-start.21) | collective-permute-done | bytes 65568 | tf_op jit(solution)/shard_map/ppermute | solution.py:40
  106.1 4.4 %collective-permute-start.22 = (f32[32,512]{1,0:T(8,128)S(1)}, f32[32,512]{1,0:T(8,128)S(1)}, u32[]{:S(2)}, u32[]{:S(2)}) collective-permute-start(f32[32,512]{1,0:T(8,128)S(1)} %add.89), channel_id=1, source_target_pairs={{0,128},{1,129},{2,130},{3,131},{4,132},{5,133},{6,134},{7,135},{8... | collective-permute-start | bytes 196616 | tf_op jit(solution)/shard_map/ppermute | solution.py:40
  110.5 3.0 %collective-permute-done.22 = f32[32,512]{1,0:T(8,128)S(1)} collective-permute-done((f32[32,512]{1,0:T(8,128)S(1)}, f32[32,512]{1,0:T(8,128)S(1)}, u32[]{:S(2)}, u32[]{:S(2)}) %collective-permute-start.22) | collective-permute-done | bytes 65568 | tf_op jit(solution)/shard_map/ppermute | solution.py:40
  114.7 3.5 %collective-permute-done.23 = f32[32,512]{1,0:T(8,128)S(1)} collective-permute-done((f32[32,512]{1,0:T(8,128)S(1)}, f32[32,512]{1,0:T(8,128)S(1)}, u32[]{:S(2)}, u32[]{:S(2)}) %collective-permute-start.23) | collective-permute-done | bytes 65568 | tf_op jit(solution)/shard_map/ppermute | solution.py:40
  118.4 13.6 %all_to_all.10 = f32[8,256,128]{1,2,0:T(8,128)S(1)} all-to-all(f32[8,256,128]{1,2,0:T(8,128)S(1)} %broadcast_in_dim.8), channel_id=1, replica_groups=mesh['z'=8,'xh'=2,'core'=2,'xl'=2,'y'=4] {'xl','y'}, dimensions={0} | all-to-all | bytes 2097152 | tf_op jit(solution)/shard_map/all_to_all | solution.py:135
  132.4 6.3 %collective-permute-start.24 = (f32[8,32,512]{2,1,0:T(8,128)S(1)}, f32[8,32,512]{2,1,0:T(8,128)S(1)}, u32[]{:S(2)}, u32[]{:S(2)}) collective-permute-start(f32[8,32,512]{2,1,0:T(8,128)S(1)} %bitcast.95), channel_id=1, source_target_pairs={{0,8},{1,9},{2,10},{3,11},{4,12},{5,13},{6,14},{7,15},{8,0},{9,1},... | collective-permute-start | bytes 1572872 | tf_op jit(solution)/shard_map/ppermute | solution.py:40
  139.0 1.4 convolution_multiply_fusion
  (140 shorter events, 23.3 us)
Async XLA Ops:
  0.6 8.4 %copy-start = (f32[512,512]{1,0:T(8,128)S(1)}, f32[512,512]{1,0:T(8,128)}, u32[]{:S(2)}) copy-start(f32[512,512]{1,0:T(8,128)} %param.9) | copy-start | bytes 3145732
  2.5 10.4 %collective-permute-start = (f32[32,1280]{1,0:T(8,128)S(1)}, f32[32,1280]{1,0:T(8,128)S(1)}, u32[]{:S(2)}, u32[]{:S(2)}) collective-permute-start(f32[32,1280]{1,0:T(8,128)S(1)} %get-tuple-element.23), channel_id=1, source_target_pairs={{0,32},{1,33},{2,34},{3,35},{4,36},{5,37},{6,38},{7,39},{8,40},{9,... | collective-permute-start | bytes 491528 | tf_op jit(solution)/shard_map/ppermute | solution.py:40
  5.0 7.9 %collective-permute-start.1 = (f32[32,1280]{1,0:T(8,128)S(1)}, f32[32,1280]{1,0:T(8,128)S(1)}, u32[]{:S(2)}, u32[]{:S(2)}) collective-permute-start(f32[32,1280]{1,0:T(8,128)S(1)} %get-tuple-element.23), channel_id=1, source_target_pairs={{0,224},{1,225},{2,226},{3,227},{4,228},{5,229},{6,230},{7,231},{8... | collective-permute-start | bytes 491528 | tf_op jit(solution)/shard_map/ppermute | solution.py:40
  12.9 24.6 %collective-permute-start.4 = (f32[96,1280]{1,0:T(8,128)S(1)}, f32[96,1280]{1,0:T(8,128)S(1)}, u32[]{:S(2)}, u32[]{:S(2)}) collective-permute-start(f32[96,1280]{1,0:T(8,128)S(1)} %pad_maximum_fusion.1), channel_id=1, source_target_pairs={{0,20},{1,21},{2,22},{3,23},{4,16},{5,17},{6,18},{7,19},{8,28},{9,... | collective-permute-start | bytes 1474568 | tf_op jit(solution)/shard_map/ppermute | solution.py:40
  15.5 29.8 %collective-permute-start.5 = (f32[96,1280]{1,0:T(8,128)S(1)}, f32[96,1280]{1,0:T(8,128)S(1)}, u32[]{:S(2)}, u32[]{:S(2)}) collective-permute-start(f32[96,1280]{1,0:T(8,128)S(1)} %pad_maximum_fusion.1), channel_id=1, source_target_pairs={{0,8},{1,9},{2,10},{3,11},{4,12},{5,13},{6,14},{7,15},{8,0},{9,1},... | collective-permute-start | bytes 1474568 | tf_op jit(solution)/shard_map/ppermute | solution.py:40
  17.0 7.2 %collective-permute-start.2 = (f32[32,1280]{1,0:T(8,128)S(1)}, f32[32,1280]{1,0:T(8,128)S(1)}, u32[]{:S(2)}, u32[]{:S(2)}) collective-permute-start(f32[32,1280]{1,0:T(8,128)S(1)} %collective-permute-done), channel_id=1, source_target_pairs={{0,32},{1,33},{2,34},{3,35},{4,36},{5,37},{6,38},{7,39},{8,40},{9,... | collective-permute-start | bytes 491528 | tf_op jit(solution)/shard_map/ppermute | solution.py:40
  17.0 7.2 %collective-permute-start.3 = (f32[32,1280]{1,0:T(8,128)S(1)}, f32[32,1280]{1,0:T(8,128)S(1)}, u32[]{:S(2)}, u32[]{:S(2)}) collective-permute-start(f32[32,1280]{1,0:T(8,128)S(1)} %collective-permute-done.1), channel_id=1, source_target_pairs={{0,224},{1,225},{2,226},{3,227},{4,228},{5,229},{6,230},{7,231},{8... | collective-permute-start | bytes 491528 | tf_op jit(solution)/shard_map/ppermute | solution.py:40
  24.2 6.3 %collective-permute-start.8 = (f32[32,1280]{1,0:T(8,128)S(1)}, f32[32,1280]{1,0:T(8,128)S(1)}, u32[]{:S(2)}, u32[]{:S(2)}) collective-permute-start(f32[32,1280]{1,0:T(8,128)S(1)} %collective-permute-done.2), channel_id=1, source_target_pairs={{0,32},{1,33},{2,34},{3,35},{4,36},{5,37},{6,38},{7,39},{8,40},{9,... | collective-permute-start | bytes 491528 | tf_op jit(solution)/shard_map/ppermute | solution.py:40
  24.3 13.2 %collective-permute-start.11 = (f32[64,1280]{1,0:T(8,128)S(1)}, f32[64,1280]{1,0:T(8,128)S(1)}, u32[]{:S(2)}, u32[]{:S(2)}) collective-permute-start(f32[64,1280]{1,0:T(8,128)S(1)} %get-tuple-element.18), channel_id=1, source_target_pairs={{0,20},{1,21},{2,22},{3,23},{4,16},{5,17},{6,18},{7,19},{8,28},{9,... | collective-permute-start | bytes 983048 | tf_op jit(solution)/shard_map/ppermute | solution.py:40
  24.6 20.8 %collective-permute-start.6 = (f32[64,1280]{1,0:T(8,128)S(1)}, f32[64,1280]{1,0:T(8,128)S(1)}, u32[]{:S(2)}, u32[]{:S(2)}) collective-permute-start(f32[64,1280]{1,0:T(8,128)S(1)} %get-tuple-element.18), channel_id=1, source_target_pairs={{0,8},{1,9},{2,10},{3,11},{4,12},{5,13},{6,14},{7,15},{8,0},{9,1},... | collective-permute-start | bytes 983048 | tf_op jit(solution)/shard_map/ppermute | solution.py:40
  30.5 4.5 %collective-permute-start.9 = (f32[32,1280]{1,0:T(8,128)S(1)}, f32[32,1280]{1,0:T(8,128)S(1)}, u32[]{:S(2)}, u32[]{:S(2)}) collective-permute-start(f32[32,1280]{1,0:T(8,128)S(1)} %collective-permute-done.3), channel_id=1, source_target_pairs={{0,224},{1,225},{2,226},{3,227},{4,228},{5,229},{6,230},{7,231},{8... | collective-permute-start | bytes 491528 | tf_op jit(solution)/shard_map/ppermute | solution.py:40
  35.0 13.4 %collective-permute-start.12 = (f32[64,1280]{1,0:T(8,128)S(1)}, f32[64,1280]{1,0:T(8,128)S(1)}, u32[]{:S(2)}, u32[]{:S(2)}) collective-permute-start(f32[64,1280]{1,0:T(8,128)S(1)} %get-tuple-element.15), channel_id=1, source_target_pairs={{0,8},{1,9},{2,10},{3,11},{4,12},{5,13},{6,14},{7,15},{8,0},{9,1},... | collective-permute-start | bytes 983048 | tf_op jit(solution)/shard_map/ppermute | solution.py:40
  37.5 7.0 %collective-permute-start.10 = (f32[32,1280]{1,0:T(8,128)S(1)}, f32[32,1280]{1,0:T(8,128)S(1)}, u32[]{:S(2)}, u32[]{:S(2)}) collective-permute-start(f32[32,1280]{1,0:T(8,128)S(1)} %collective-permute-done.8), channel_id=1, source_target_pairs={{0,32},{1,33},{2,34},{3,35},{4,36},{5,37},{6,38},{7,39},{8,40},{9,... | collective-permute-start | bytes 491528 | tf_op jit(solution)/shard_map/ppermute | solution.py:40
  37.5 18.6 %copy-start.2 = (f32[256,768]{1,0:T(8,128)S(1)}, f32[256,768]{1,0:T(8,128)}, u32[]{:S(2)}) copy-start(f32[256,768]{1,0:T(8,128)} %param.6) | copy-start | bytes 2359300
  37.6 10.6 %collective-permute-start.15 = (f32[64,1280]{1,0:T(8,128)S(1)}, f32[64,1280]{1,0:T(8,128)S(1)}, u32[]{:S(2)}, u32[]{:S(2)}) collective-permute-start(f32[64,1280]{1,0:T(8,128)S(1)} %get-tuple-element.15), channel_id=1, source_target_pairs={{0,20},{1,21},{2,22},{3,23},{4,16},{5,17},{6,18},{7,19},{8,28},{9,... | collective-permute-start | bytes 983048 | tf_op jit(solution)/shard_map/ppermute | solution.py:40
  44.5 11.6 %collective-permute-start.13 = (f32[32,1280]{1,0:T(8,128)S(1)}, f32[32,1280]{1,0:T(8,128)S(1)}, u32[]{:S(2)}, u32[]{:S(2)}) collective-permute-start(f32[32,1280]{1,0:T(8,128)S(1)} %collective-permute-done.10), channel_id=1, source_target_pairs={{0,8},{1,9},{2,10},{3,11},{4,12},{5,13},{6,14},{7,15},{8,0},{9,1},... | collective-permute-start | bytes 491528 | tf_op jit(solution)/shard_map/ppermute | solution.py:40
  45.3 10.7 %collective-permute-start.14 = (f32[64,1280]{1,0:T(8,128)S(1)}, f32[64,1280]{1,0:T(8,128)S(1)}, u32[]{:S(2)}, u32[]{:S(2)}) collective-permute-start(f32[64,1280]{1,0:T(8,128)S(1)} %collective-permute-done.11), channel_id=1, source_target_pairs={{0,8},{1,9},{2,10},{3,11},{4,12},{5,13},{6,14},{7,15},{8,0},{9,1},... | collective-permute-start | bytes 983048 | tf_op jit(solution)/shard_map/ppermute | solution.py:40
  45.5 15.3 %collective-permute-start.7 = (f32[96,1280]{1,0:T(8,128)S(1)}, f32[96,1280]{1,0:T(8,128)S(1)}, u32[]{:S(2)}, u32[]{:S(2)}) collective-permute-start(f32[96,1280]{1,0:T(8,128)S(1)} %collective-permute-done.4), channel_id=1, source_target_pairs={{0,8},{1,9},{2,10},{3,11},{4,12},{5,13},{6,14},{7,15},{8,0},{9,1},... | collective-permute-start | bytes 1474568 | tf_op jit(solution)/shard_map/ppermute | solution.py:40
  48.1 6.1 %collective-permute-start.16 = (f32[32,1280]{1,0:T(8,128)S(1)}, f32[32,1280]{1,0:T(8,128)S(1)}, u32[]{:S(2)}, u32[]{:S(2)}) collective-permute-start(f32[32,1280]{1,0:T(8,128)S(1)} %collective-permute-done.10), channel_id=1, source_target_pairs={{0,20},{1,21},{2,22},{3,23},{4,16},{5,17},{6,18},{7,19},{8,28},{9,... | collective-permute-start | bytes 491528 | tf_op jit(solution)/shard_map/ppermute | solution.py:40
  48.4 10.0 %collective-permute-start.17 = (f32[64,1280]{1,0:T(8,128)S(1)}, f32[64,1280]{1,0:T(8,128)S(1)}, u32[]{:S(2)}, u32[]{:S(2)}) collective-permute-start(f32[64,1280]{1,0:T(8,128)S(1)} %collective-permute-done.15), channel_id=1, source_target_pairs={{0,8},{1,9},{2,10},{3,11},{4,12},{5,13},{6,14},{7,15},{8,0},{9,1},... | collective-permute-start | bytes 983048 | tf_op jit(solution)/shard_map/ppermute | solution.py:40
  54.2 4.3 %collective-permute-start.18 = (f32[32,1280]{1,0:T(8,128)S(1)}, f32[32,1280]{1,0:T(8,128)S(1)}, u32[]{:S(2)}, u32[]{:S(2)}) collective-permute-start(f32[32,1280]{1,0:T(8,128)S(1)} %collective-permute-done.16), channel_id=1, source_target_pairs={{0,8},{1,9},{2,10},{3,11},{4,12},{5,13},{6,14},{7,15},{8,0},{9,1},... | collective-permute-start | bytes 491528 | tf_op jit(solution)/shard_map/ppermute | solution.py:40
  57.2 5.3 %copy-start.8 = (f32[256]{0:T(256)}, f32[256]{0:T(256)S(1)}, u32[]{:S(2)}) copy-start(f32[256]{0:T(256)S(1)} %get-tuple-element.50) | copy-start | bytes 3076
  58.5 6.1 %copy-start.3 = (f32[192,1280]{1,0:T(8,128)}, f32[192,1280]{1,0:T(8,128)S(1)}, u32[]{:S(2)}) copy-start(f32[192,1280]{1,0:T(8,128)S(1)} %constant_dynamic-update-slice_fusion.23) | copy-start | bytes 2949124
  69.6 3.9 %copy-start.5 = (f32[256,512]{0,1:T(8,128)S(1)}, f32[256,512]{0,1:T(8,128)}, u32[]{:S(2)}) copy-start(f32[256,512]{0,1:T(8,128)} %copy.41) | copy-start | bytes 1572868
  75.2 21.0 %copy-start.4 = (f32[256,512]{1,0:T(8,128)S(1)}, f32[256,512]{1,0:T(8,128)}, u32[]{:S(2)}) copy-start(f32[256,512]{1,0:T(8,128)} %param.5) | copy-start | bytes 1572868
  75.2 19.7 %all-to-all-start = ((f32[8,264,128]{2,1,0:T(8,128)}), f32[8,264,128]{2,1,0:T(8,128)S(1)}, u32[]{:S(2)}, u32[]{:S(2)}) async-start(f32[8,264,128]{2,1,0:T(8,128)} %copy.44), calls=%async_computation | async-start | bytes 2162688 | tf_op jit(solution)/shard_map/all_to_all | solution.py:105
  96.5 1.7 %collective-permute-start.19 = (f32[32,512]{1,0:T(8,128)S(1)}, f32[32,512]{1,0:T(8,128)S(1)}, u32[]{:S(2)}, u32[]{:S(2)}) collective-permute-start(f32[32,512]{1,0:T(8,128)S(1)} %constant_dynamic-slice_fusion), channel_id=1, source_target_pairs={{0,8},{1,9},{2,10},{3,11},{4,12},{5,13},{6,14},{7,15},{8,0},{9,1},... | collective-permute-start | bytes 196616 | tf_op jit(solution)/shard_map/ppermute | solution.py:40
  98.3 3.2 %collective-permute-start.20 = (f32[32,512]{1,0:T(8,128)S(1)}, f32[32,512]{1,0:T(8,128)S(1)}, u32[]{:S(2)}, u32[]{:S(2)}) collective-permute-start(f32[32,512]{1,0:T(8,128)S(1)} %dynamic-slice_add_fusion), channel_id=1, source_target_pairs={{0,32},{1,33},{2,34},{3,35},{4,36},{5,37},{6,38},{7,39},{8,40},{9,... | collective-permute-start | bytes 196616 | tf_op jit(solution)/shard_map/ppermute | solution.py:40
  101.5 4.6 %collective-permute-start.21 = (f32[32,512]{1,0:T(8,128)S(1)}, f32[32,512]{1,0:T(8,128)S(1)}, u32[]{:S(2)}, u32[]{:S(2)}) collective-permute-start(f32[32,512]{1,0:T(8,128)S(1)} %add.88), channel_id=1, source_target_pairs={{0,64},{1,65},{2,66},{3,67},{4,68},{5,69},{6,70},{7,71},{8,72},{9,... | collective-permute-start | bytes 196616 | tf_op jit(solution)/shard_map/ppermute | solution.py:40
  106.1 7.4 %collective-permute-start.22 = (f32[32,512]{1,0:T(8,128)S(1)}, f32[32,512]{1,0:T(8,128)S(1)}, u32[]{:S(2)}, u32[]{:S(2)}) collective-permute-start(f32[32,512]{1,0:T(8,128)S(1)} %add.89), channel_id=1, source_target_pairs={{0,128},{1,129},{2,130},{3,131},{4,132},{5,133},{6,134},{7,135},{8... | collective-permute-start | bytes 196616 | tf_op jit(solution)/shard_map/ppermute | solution.py:40
  113.5 4.7 %collective-permute-start.23 = (f32[32,512]{1,0:T(8,128)S(1)}, f32[32,512]{1,0:T(8,128)S(1)}, u32[]{:S(2)}, u32[]{:S(2)}) collective-permute-start(f32[32,512]{1,0:T(8,128)S(1)} %add.90), channel_id=1, source_target_pairs={{0,16},{1,17},{2,18},{3,19},{4,20},{5,21},{6,22},{7,23},{8,24},{9,... | collective-permute-start | bytes 196616 | tf_op jit(solution)/shard_map/ppermute | solution.py:40
  132.4 8.1 %collective-permute-start.24 = (f32[8,32,512]{2,1,0:T(8,128)S(1)}, f32[8,32,512]{2,1,0:T(8,128)S(1)}, u32[]{:S(2)}, u32[]{:S(2)}) collective-permute-start(f32[8,32,512]{2,1,0:T(8,128)S(1)} %bitcast.95), channel_id=1, source_target_pairs={{0,8},{1,9},{2,10},{3,11},{4,12},{5,13},{6,14},{7,15},{8,0},{9,1},... | collective-permute-start | bytes 1572872 | tf_op jit(solution)/shard_map/ppermute | solution.py:40
  (12 other events, 39.3 us)

commit v2 on v1

v2 whole, which is shorter than its diff:
```python
import math

import jax
import jax.numpy as jnp
from jax import lax
from jax.experimental import pallas as pl
from jax.experimental.pallas import tpu as pltpu
from jax.sharding import Mesh, PartitionSpec as P

AXES = ("z", "xh", "core", "xl", "y")
SIZES = (8, 2, 2, 2, 4)
HIGH = lax.Precision.HIGH
DS, DT = 512, 768
ROWS = 256
SHARD = 32
COLS = DS // 8
VMEM_LIMIT = 14 * 1024 * 1024


def linear(z, xh, core, xl, y):
    return (((z * 2 + xh) * 2 + core) * 2 + xl) * 4 + y


def moves(place):
    pairs = []
    for z in range(8):
        for xh in range(2):
            for core in range(2):
                for xl in range(2):
                    for y in range(4):
                        here = (z, xh, core, xl, y)
                        pairs.append((linear(*here), linear(*place(*here))))
    return pairs


Z_NEXT = moves(lambda z, xh, core, xl, y: ((z + 1 - 2 * core) % 8, xh, core, xl, y))
X_FLIP = moves(lambda z, xh, core, xl, y: (z, 1 - xh, core, 1 - xl, y))
CORE = moves(lambda z, xh, core, xl, y: (z, xh, 1 - core, xl, y))
Z_FOLD = tuple(
    moves(lambda z, xh, core, xl, y, bit=bit: (z ^ bit, xh, core, xl, y)) for bit in (1, 2, 4)
)


def move(array, pairs):
    return lax.ppermute(array, AXES, pairs)


def dot(a, b, dims):
    return lax.dot_general(
        a, b, (dims, ((), ())), precision=HIGH, preferred_element_type=jnp.float32
    )


def split(x):
    high = x.astype(jnp.bfloat16)
    return high, (x - high.astype(jnp.float32)).astype(jnp.bfloat16)


def dot3(a, b, dims):
    def one(p, q):
        return lax.dot_general(p, q, (dims, ((), ())), preferred_element_type=jnp.float32)

    return one(a[0], b[0]) + (one(a[0], b[1]) + one(a[1], b[0]))


NT = ((1,), (1,))
NN = ((1,), (0,))


def texts_kernel(count, first, last, *refs):
    refs = list(refs)
    place = refs.pop(0) if last else None
    folded_ref, images_ref = refs.pop(0), refs.pop(0)
    arrays = [refs.pop(0) for _ in range(count)]
    state = None if first else [refs.pop(0) for _ in range(3)]
    outs = [refs.pop(0) for _ in range(1 if last else 3)]
    t_high, t_low, f_high, f_low = refs
    start = 0
    for array in arrays:
        here = pl.ds(start, array.shape[0])
        start += array.shape[0]
        t_high[here, :], t_low[here, :] = split(array[:, :DT])
        f_high[here, :], f_low[here, :] = split(array[:, DT:])
    texts = (t_high[...], t_low[...])
    features = (f_high[...], f_low[...])
    tiles = (
        dot3(split(folded_ref[...]), features, NT),
        dot3(split(images_ref[...]), texts, NT),
    )
    lane = lax.broadcasted_iota(jnp.int32, (ROWS, 128), 1)
    stats = jnp.zeros((ROWS, 128), jnp.float32)
    products = []
    for k, tile in enumerate(tiles):
        top = jnp.max(tile, axis=1, keepdims=True)
        if not first:
            old_top = state[0][:, 2 * k : 2 * k + 1]
            top = jnp.maximum(top, old_top)
        weight = jnp.exp(tile - top)
        total = jnp.sum(weight, axis=1, keepdims=True)
        product = dot3(split(weight), features, NN)
        if not first:
            shrink = jnp.exp(old_top - top)
            total = total + shrink * state[0][:, 2 * k + 1 : 2 * k + 2]
            product = product + shrink * state[1 + k][...]
        stats = jnp.where(lane == 2 * k, top, stats)
        stats = jnp.where(lane == 2 * k + 1, total, stats)
        products.append(product)
    if not last:
        outs[0][...] = stats
        outs[1][...] = products[0]
        outs[2][...] = products[1]
        return
    out = outs[0]
    turned = stats.T[:8]
    for q in range(4):
        a = products[0][:, 128 * q : 128 * q + 128]
        b = products[1][:, 128 * q : 128 * q + 128]
        out[place[2 * q], 0:ROWS] = jnp.where(lane < COLS, a, pltpu.roll(b, COLS, 1))
        out[place[2 * q + 1], 0:ROWS] = jnp.where(lane < COLS, pltpu.roll(a, COLS, 1), b)
    for k in range(8):
        out[k, ROWS : ROWS + 8] = turned[:, :128]
        out[k, ROWS + 8 : ROWS + 16] = turned[:, 128:]


def add_texts(folded, images, arrays, state=None, place=None):
    first, last = state is None, place is not None
    texts = sum(array.shape[0] for array in arrays)
    operands = [folded, images] + list(arrays) + ([] if first else list(state))
    vmem = pl.BlockSpec(memory_space=pltpu.VMEM)
    in_specs = [vmem] * len(operands)
    scratch = [
        pltpu.VMEM((texts, DT), jnp.bfloat16),
        pltpu.VMEM((texts, DT), jnp.bfloat16),
        pltpu.VMEM((texts, DS), jnp.bfloat16),
        pltpu.VMEM((texts, DS), jnp.bfloat16),
    ]
    if last:
        operands = [place] + operands
        in_specs = [pl.BlockSpec(memory_space=pltpu.SMEM)] + in_specs
        shapes = [jax.ShapeDtypeStruct((8, ROWS + 16, 128), jnp.float32)]
    else:
        shapes = [
            jax.ShapeDtypeStruct((ROWS, 128), jnp.float32),
            jax.ShapeDtypeStruct((ROWS, DS), jnp.float32),
            jax.ShapeDtypeStruct((ROWS, DS), jnp.float32),
        ]
    flops = 2 * 3 * ROWS * texts * (DT + 3 * DS)

    def body(*refs):
        texts_kernel(len(arrays), first, last, *refs)

    return pl.pallas_call(
        body,
        out_shape=shapes,
        in_specs=in_specs,
        out_specs=[vmem] * len(shapes),
        scratch_shapes=scratch,
        compiler_params=pltpu.CompilerParams(vmem_limit_bytes=VMEM_LIMIT),
        cost_estimate=pl.CostEstimate(
            flops=40 * flops, bytes_accessed=4 * 1024 * 1024, transcendentals=2 * ROWS * texts
        ),
        name="add_texts",
    )(*operands)


def halved(array, index, pairs):
    rows = array.shape[0] // 2
    mine = lax.dynamic_slice_in_dim(array, index * rows, rows, 0)
    other = lax.dynamic_slice_in_dim(array, (1 - index) * rows, rows, 0)
    return mine + move(other, pairs)


def to_all(piece, axes):
    count = math.prod(lax.axis_size(axis) for axis in axes)
    pieces = jnp.broadcast_to(piece[None], (count,) + piece.shape)
    return lax.all_to_all(pieces, axes, 0, 0, tiled=True)


def shards(image_student, image_teacher, text_features, text_teacher, head):
    scale_s = 4.0 / math.sqrt(DS)
    scale_t = 4.0 / math.sqrt(DT)
    batch = ROWS * 32
    xh, core = lax.axis_index("xh"), lax.axis_index("core")
    folded = scale_s * dot(image_student, head, NT)
    images = scale_t * image_teacher

    own = jnp.concatenate([text_teacher, text_features], axis=1)
    across = [move(text_teacher, X_FLIP), move(text_features, X_FLIP)]
    one = jnp.concatenate([own, jnp.concatenate(across, axis=1)], axis=0)
    one, two = lax.optimization_barrier((one, move(one, CORE)))
    state = add_texts(folded, images, [one, two])
    for step in range(3):
        one, two = move(one, Z_NEXT), move(two, Z_NEXT)
        state = add_texts(folded, images, [one, move(one, CORE)], state)
        state = add_texts(folded, images, [two, move(two, CORE)], state)
    one = move(one, Z_NEXT)
    place = jnp.arange(8, dtype=jnp.int32) ^ (4 * xh).astype(jnp.int32)
    (both,) = add_texts(folded, images, [one, move(one, CORE)], state, place)

    got = lax.all_to_all(both, ("xl", "y"), 0, 0, tiled=True)
    stats = got[:, ROWS:].reshape(8, 2, 8, 128)[:, :, :4]
    stats = stats.transpose(0, 2, 1, 3).reshape(8, 4, ROWS)
    sums = []
    for k in (0, 2):
        tops = stats[:, k]
        top = jnp.max(tops, axis=0)
        shares = jnp.exp(tops - top[None])
        total = jnp.sum(shares * stats[:, k + 1], axis=0)
        shares = shares / total[None]
        lanes = slice(0, COLS) if k == 0 else slice(COLS, 2 * COLS)
        sums.append(jnp.sum(got[:, :ROWS, lanes] * shares[:, :, None], axis=0))
    gap_text = sums[0] - sums[1]

    term = dot(gap_text, image_student, ((0,), (0,)))
    term = halved(term, core, CORE)
    piece = jnp.concatenate([gap_text[: ROWS // 2], gap_text[ROWS // 2 :]], axis=1)
    term, piece = lax.optimization_barrier((term, piece))
    term = halved(term, xh, X_FLIP)
    for pairs in Z_FOLD:
        term = term + move(term, pairs)

    gaps = to_all(piece, ("xl", "y"))
    gaps = jnp.where(xh == 0, gaps, jnp.concatenate([gaps[4:], gaps[:4]], axis=0))
    gap_text = gaps.reshape(8, ROWS // 2, 2, COLS).transpose(2, 1, 0, 3).reshape(ROWS, DS)
    grad_image = scale_s * dot(gap_text, head, NN)

    terms = to_all(term * (scale_s / math.sqrt(batch)), ("xh", "xl", "y"))
    terms = terms.reshape(2, 2, 4, SHARD // 2, DS)
    terms = jnp.stack([terms[0], terms[1, ::-1]], axis=2).reshape(8, SHARD, DS)
    partner = move(terms, CORE)
    low = jnp.where(core == 0, terms, partner)
    high = jnp.where(core == 0, partner, terms)
    grad_head = jnp.stack([low, high], axis=1).reshape(DS, DS)
    return (grad_image, grad_head)


def solution(mesh):
    fine = Mesh(mesh.devices.reshape(SIZES), AXES)
    dp, every = ("z", "xh", "core"), AXES
    in_specs = (P(dp, None), P(dp, None), P(every, None), P(every, None), P())
    out_specs = (P(dp, None), P())
    return jax.shard_map(shards, mesh=fine, in_specs=in_specs, out_specs=out_specs, check_vma=False)
```

time: 142 us -> 123 us (0.87)
  starting transfers between devices: 42.6 us -> 56.6 us
  waiting for transfers between devices: 56.4 us -> 42.7 us
  blocking collectives: 13.6 us -> 0 us
  Pallas kernels: 0 us -> 13.4 us
  matrix products: 13.7 us -> 2.34 us
  local copies, waits for them, and re-layouts: 8.38 us -> 2.36 us
    ppermute x25 -> x23, waiting for transfers between devices: 41 us -> 18.1 us  [move(): return lax.ppermute(array, AXES, pairs)]
    all_to_all x1 -> x0, blocking collectives: 13.6 us -> none  [shards(): lax.all_to_all(jnp.broadcast_to(payload[None], (8,) + payload.shape), ('x...]
    pallas_call x0 -> x8, Pallas kernels: none -> 13.4 us  [add_texts(): pl.pallas_call(body, out_shape=shapes, in_specs=in_specs, out_specs=[vmem...]
    dot_general x15 -> x3, matrix products: 13.7 us -> 2.34 us  [dot(): lax.dot_general(a, b, (dims, ((), ())), precision=HIGH, preferred_element...]
    all_to_all x1 -> x3, waiting for transfers between devices: 15.4 us -> 24.6 us  [the longest x1 15.7 us: shards(): got = lax.all_to_all(both, ('xl', 'y'), 0, 0, tiled=True)]
    all_to_all x1 -> x3, starting transfers between devices: 4.32 us -> 12.9 us  [the longest x2 8.66 us: to_all(): return lax.all_to_all(pieces, axes, 0, 0, tiled=True)]
    ppermute x25 -> x23, starting transfers between devices: 38.2 us -> 43.7 us  [move(): return lax.ppermute(array, AXES, pairs)]
    reduce_sum x7 -> x1, other arithmetic: 4.43 us -> 0.99 us  [shards(): sums.append(jnp.sum(got[:, :ROWS, lanes] * shares[:, :, None], axis=0))]
  transfers between devices with their start and end apart: 26 -> 26, of which waited for: 13 -> 12; matrix products, arithmetic and copies ran while one was open for 6% -> 4% of each run, Pallas kernels for 0% -> 8%
where the time goes in v2:
time: 123 us
  starting transfers between devices  56.6 us (46%)
  waiting for transfers between devices  42.7 us (35%)
  Pallas kernels  13.4 us (11%)
  other arithmetic  4.62 us (4%)
  local copies, waits for them, and re-layouts  2.36 us (2%)
  matrix products  2.34 us (2%)
    ppermute x23, starting transfers between devices, move(): return lax.ppermute(array, AXES, pairs)  43.7 us
    ppermute x23, waiting for transfers between devices, move(): return lax.ppermute(array, AXES, pairs)  18.1 us
    all_to_all x1, waiting for transfers between devices, shards(): got = lax.all_to_all(both, ('xl', 'y'), 0, 0, tiled=True)  15.7 us
    pallas_call x8, Pallas kernels, add_texts(): pl.pallas_call(body, out_shape=shapes, in_specs=in_specs, out_specs=[vmem...  13.4 us
    all_to_all x2, waiting for transfers between devices, to_all(): return lax.all_to_all(pieces, axes, 0, 0, tiled=True)  8.91 us
    all_to_all x2, starting transfers between devices, to_all(): return lax.all_to_all(pieces, axes, 0, 0, tiled=True)  8.66 us
    all_to_all x1, starting transfers between devices, shards(): got = lax.all_to_all(both, ('xl', 'y'), 0, 0, tiled=True)  4.21 us
  transfers between devices with their start and end apart: 26, of which 12 were waited for; matrix products, arithmetic and copies ran while one was open for 4% of the time, Pallas kernels for 8%

profile of v2, /device:TPU:1, one launch (start us, length us, event | category | flops | bytes accessed | tf_op | source)
XLA Modules:
  0.0 122.9 jit_solution(1050932259144070828)
XLA Ops:
  0.7 3.4 %collective-permute-start = (f32[32,768]{1,0:T(8,128)}, f32[32,768]{1,0:T(8,128)S(1)}, u32[]{:S(2)}, u32[]{:S(2)}) collective-permute-start(f32[32,768]{1,0:T(8,128)} %param.8), channel_id=1, source_target_pairs={{0,20},{1,21},{2,22},{3,23},{4,16},{5,17},{6,18},{7,19},{8,28},{9,... | collective-permute-start | bytes 294920 | tf_op jit(solution)/shard_map/ppermute | solution.py:45
  4.2 5.1 %collective-permute-done.1 = f32[32,512]{1,0:T(8,128)S(1)} collective-permute-done((f32[32,512]{1,0:T(8,128)}, f32[32,512]{1,0:T(8,128)S(1)}, u32[]{:S(2)}, u32[]{:S(2)}) %collective-permute-start.1) | collective-permute-done | bytes 65568 | tf_op jit(solution)/shard_map/ppermute | solution.py:45
  10.2 1.8 %collective-permute-start.2 = (f32[64,1280]{1,0:T(8,128)S(1)}, f32[64,1280]{1,0:T(8,128)S(1)}, u32[]{:S(2)}, u32[]{:S(2)}) collective-permute-start(f32[64,1280]{1,0:T(8,128)S(1)} %maximum_maximum_fusion.refs_2_), channel_id=1, source_target_pairs={{0,8},{1,9},{2,10},{3,11},{4,12},{5,13},{6,14},{7,15},{8,0},{9,1},... | collective-permute-start | bytes 983048 | tf_op jit(solution)/shard_map/ppermute | solution.py:45
  13.3 5.3 %collective-permute-start.3 = (f32[64,1280]{1,0:T(8,128)S(1)}, f32[64,1280]{1,0:T(8,128)S(1)}, u32[]{:S(2)}, u32[]{:S(2)}) collective-permute-start(f32[64,1280]{1,0:T(8,128)S(1)} %maximum_maximum_fusion.refs_2_), channel_id=1, source_target_pairs={{0,32},{1,33},{2,34},{3,35},{4,36},{5,37},{6,38},{7,39},{8,232},{9... | collective-permute-start | bytes 983048 | tf_op jit(solution)/shard_map/ppermute | solution.py:45
  20.0 2.6 %collective-permute-done.3.refs_2_ = f32[64,1280]{1,0:T(8,128)S(1)} collective-permute-done((f32[64,1280]{1,0:T(8,128)S(1)}, f32[64,1280]{1,0:T(8,128)S(1)}, u32[]{:S(2)}, u32[]{:S(2)}) %collective-permute-start.3) | collective-permute-done | bytes 327712 | tf_op jit(solution)/shard_map/ppermute | solution.py:45
  22.6 1.6 %collective-permute-start.16 = (f32[64,1280]{1,0:T(8,128)S(1)}, f32[64,1280]{1,0:T(8,128)S(1)}, u32[]{:S(2)}, u32[]{:S(2)}) collective-permute-start(f32[64,1280]{1,0:T(8,128)S(1)} %collective-permute-done.3.refs_2_), channel_id=1, source_target_pairs={{0,8},{1,9},{2,10},{3,11},{4,12},{5,13},{6,14},{7,15},{8,0},{9,1},... | collective-permute-start | bytes 983048 | tf_op jit(solution)/shard_map/ppermute | solution.py:45
  24.3 1.7 %collective-permute-start.4 = (f32[64,1280]{1,0:T(8,128)S(1)}, f32[64,1280]{1,0:T(8,128)S(1)}, u32[]{:S(2)}, u32[]{:S(2)}) collective-permute-start(f32[64,1280]{1,0:T(8,128)S(1)} %collective-permute-done.3.refs_2_), channel_id=1, source_target_pairs={{0,32},{1,33},{2,34},{3,35},{4,36},{5,37},{6,38},{7,39},{8,232},{9... | collective-permute-start | bytes 983048 | tf_op jit(solution)/shard_map/ppermute | solution.py:45
  26.1 3.1 %collective-permute-start.9 = (f32[64,1280]{1,0:T(8,128)S(1)}, f32[64,1280]{1,0:T(8,128)S(1)}, u32[]{:S(2)}, u32[]{:S(2)}) collective-permute-start(f32[64,1280]{1,0:T(8,128)S(1)} %collective-permute-done.8.refs_2_), channel_id=1, source_target_pairs={{0,32},{1,33},{2,34},{3,35},{4,36},{5,37},{6,38},{7,39},{8,232},{9... | collective-permute-start | bytes 983048 | tf_op jit(solution)/shard_map/ppermute | solution.py:45
  29.3 1.3 %add_texts.8 = (f32[256,128]{1,0:T(8,128)S(1)}, f32[256,512]{1,0:T(8,128)S(1)}, f32[256,512]{1,0:T(8,128)S(1)}) custom-call(f32[256,512]{1,0:T(8,128)S(1)} %convolution_multiply_fusion.1.refs_0_.refs_1_, f32[256,768]{1,0:T(8,128)S(1)} %broadcast_multiply_fusion.refs_1_.refs_2_, f32[64,1280]{1,0:T(8,128)S(1)} %maximum_maximum_fusion.refs_2_, ...), custom_call_target="tpu_custom_call" | custom-call | flops 18119393280 | bytes 4194304 | tf_op jit(solution)/shard_map/add_texts/pallas_call | solution.py:152
  30.7 1.9 %collective-permute-start.14 = (f32[64,1280]{1,0:T(8,128)S(1)}, f32[64,1280]{1,0:T(8,128)S(1)}, u32[]{:S(2)}, u32[]{:S(2)}) collective-permute-start(f32[64,1280]{1,0:T(8,128)S(1)} %collective-permute-done.4.refs_2_), channel_id=1, source_target_pairs={{0,8},{1,9},{2,10},{3,11},{4,12},{5,13},{6,14},{7,15},{8,0},{9,1},... | collective-permute-start | bytes 983048 | tf_op jit(solution)/shard_map/ppermute | solution.py:45
  34.0 2.1 %collective-permute-start.13 = (f32[64,1280]{1,0:T(8,128)S(1)}, f32[64,1280]{1,0:T(8,128)S(1)}, u32[]{:S(2)}, u32[]{:S(2)}) collective-permute-start(f32[64,1280]{1,0:T(8,128)S(1)} %collective-permute-done.9.refs_2_), channel_id=1, source_target_pairs={{0,8},{1,9},{2,10},{3,11},{4,12},{5,13},{6,14},{7,15},{8,0},{9,1},... | collective-permute-start | bytes 983048 | tf_op jit(solution)/shard_map/ppermute | solution.py:45
  36.9 1.5 %add_texts.9 = (f32[256,128]{1,0:T(8,128)S(1)}, f32[256,512]{1,0:T(8,128)S(1)}, f32[256,512]{1,0:T(8,128)S(1)}) custom-call(f32[256,512]{1,0:T(8,128)S(1)} %convolution_multiply_fusion.1.refs_0_.refs_1_, f32[256,768]{1,0:T(8,128)S(1)} %broadcast_multiply_fusion.refs_1_.refs_2_, f32[64,1280]{1,0:T(8,128)S(1)} %collective-permute-done.3.refs_2_, ...), custom_call_target="tpu_custom_call" | custom-call | flops 18119393280 | bytes 4194304 | tf_op jit(solution)/shard_map/add_texts/pallas_call | solution.py:152
  38.3 1.5 %add_texts.10 = (f32[256,128]{1,0:T(8,128)S(1)}, f32[256,512]{1,0:T(8,128)S(1)}, f32[256,512]{1,0:T(8,128)S(1)}) custom-call(f32[256,512]{1,0:T(8,128)S(1)} %convolution_multiply_fusion.1.refs_0_.refs_1_, f32[256,768]{1,0:T(8,128)S(1)} %broadcast_multiply_fusion.refs_1_.refs_2_, f32[64,1280]{1,0:T(8,128)S(1)} %collective-permute-done.8.refs_2_, ...), custom_call_target="tpu_custom_call" | custom-call | flops 18119393280 | bytes 4194304 | tf_op jit(solution)/shard_map/add_texts/pallas_call | solution.py:152
  42.3 2.1 %collective-permute-start.11 = (f32[64,1280]{1,0:T(8,128)S(1)}, f32[64,1280]{1,0:T(8,128)S(1)}, u32[]{:S(2)}, u32[]{:S(2)}) collective-permute-start(f32[64,1280]{1,0:T(8,128)S(1)} %collective-permute-done.10.refs_2_), channel_id=1, source_target_pairs={{0,8},{1,9},{2,10},{3,11},{4,12},{5,13},{6,14},{7,15},{8,0},{9,1},... | collective-permute-start | bytes 983048 | tf_op jit(solution)/shard_map/ppermute | solution.py:45
  44.4 1.5 %add_texts.11 = (f32[256,128]{1,0:T(8,128)S(1)}, f32[256,512]{1,0:T(8,128)S(1)}, f32[256,512]{1,0:T(8,128)S(1)}) custom-call(f32[256,512]{1,0:T(8,128)S(1)} %convolution_multiply_fusion.1.refs_0_.refs_1_, f32[256,768]{1,0:T(8,128)S(1)} %broadcast_multiply_fusion.refs_1_.refs_2_, f32[64,1280]{1,0:T(8,128)S(1)} %collective-permute-done.4.refs_2_, ...), custom_call_target="tpu_custom_call" | custom-call | flops 18119393280 | bytes 4194304 | tf_op jit(solution)/shard_map/add_texts/pallas_call | solution.py:152
  45.9 1.5 %add_texts.12 = (f32[256,128]{1,0:T(8,128)S(1)}, f32[256,512]{1,0:T(8,128)S(1)}, f32[256,512]{1,0:T(8,128)S(1)}) custom-call(f32[256,512]{1,0:T(8,128)S(1)} %convolution_multiply_fusion.1.refs_0_.refs_1_, f32[256,768]{1,0:T(8,128)S(1)} %broadcast_multiply_fusion.refs_1_.refs_2_, f32[64,1280]{1,0:T(8,128)S(1)} %collective-permute-done.9.refs_2_, ...), custom_call_target="tpu_custom_call" | custom-call | flops 18119393280 | bytes 4194304 | tf_op jit(solution)/shard_map/add_texts/pallas_call | solution.py:152
  47.3 1.8 %collective-permute-start.7 = (f32[64,1280]{1,0:T(8,128)S(1)}, f32[64,1280]{1,0:T(8,128)S(1)}, u32[]{:S(2)}, u32[]{:S(2)}) collective-permute-start(f32[64,1280]{1,0:T(8,128)S(1)} %collective-permute-done.6.refs_3_), channel_id=1, source_target_pairs={{0,8},{1,9},{2,10},{3,11},{4,12},{5,13},{6,14},{7,15},{8,0},{9,1},... | collective-permute-start | bytes 983048 | tf_op jit(solution)/shard_map/ppermute | solution.py:45
  49.2 1.5 %add_texts.13 = (f32[256,128]{1,0:T(8,128)S(1)}, f32[256,512]{1,0:T(8,128)S(1)}, f32[256,512]{1,0:T(8,128)S(1)}) custom-call(f32[256,512]{1,0:T(8,128)S(1)} %convolution_multiply_fusion.1.refs_0_.refs_1_, f32[256,768]{1,0:T(8,128)S(1)} %broadcast_multiply_fusion.refs_1_.refs_2_, f32[64,1280]{1,0:T(8,128)S(1)} %collective-permute-done.5.refs_2_, ...), custom_call_target="tpu_custom_call" | custom-call | flops 18119393280 | bytes 4194304 | tf_op jit(solution)/shard_map/add_texts/pallas_call | solution.py:152
  50.6 1.5 %add_texts.14 = (f32[256,128]{1,0:T(8,128)S(1)}, f32[256,512]{1,0:T(8,128)S(1)}, f32[256,512]{1,0:T(8,128)S(1)}) custom-call(f32[256,512]{1,0:T(8,128)S(1)} %convolution_multiply_fusion.1.refs_0_.refs_1_, f32[256,768]{1,0:T(8,128)S(1)} %broadcast_multiply_fusion.refs_1_.refs_2_, f32[64,1280]{1,0:T(8,128)S(1)} %collective-permute-done.10.refs_2_, ...), custom_call_target="tpu_custom_call" | custom-call | flops 18119393280 | bytes 4194304 | tf_op jit(solution)/shard_map/add_texts/pallas_call | solution.py:152
  52.1 3.3 %add_texts.15 = f32[8,272,128]{2,1,0:T(8,128)} custom-call(s32[8]{0:T(128)S(1)} %iota_xor_fusion.refs_0_, f32[256,512]{1,0:T(8,128)S(1)} %convolution_multiply_fusion.1.refs_0_.refs_1_, f32[256,768]{1,0:T(8,128)S(1)} %broadcast_multiply_fusion.refs_1_.refs_2_, f32[64,1280]{1,0:T(8,128)S(1)} %collective-permute-done.6.refs_3_, ...), custom_call_target="tpu_custom_call" | custom-call | flops 18119393280 | bytes 4194304 | tf_op jit(solution)/shard_map/add_texts/pallas_call | solution.py:152
  55.4 4.2 %all-to-all-start = ((f32[8,272,128]{2,1,0:T(8,128)}), f32[8,272,128]{2,1,0:T(8,128)S(1)}, u32[]{:S(2)}, u32[]{:S(2)}) async-start(f32[8,272,128]{2,1,0:T(8,128)} %add_texts.15), calls=%async_computation | async-start | bytes 2228224 | tf_op jit(solution)/shard_map/all_to_all | solution.py:200
  59.6 15.7 %all-to-all-done = f32[8,272,128]{2,1,0:T(8,128)S(1)} async-done(((f32[8,272,128]{2,1,0:T(8,128)}), f32[8,272,128]{2,1,0:T(8,128)S(1)}, u32[]{:S(2)}, u32[]{:S(2)}) %all-to-all-start) | async-done | bytes 1114144 | tf_op jit(solution)/shard_map/all_to_all | solution.py:200
  78.8 2.4 %collective-permute-start.18 = (f32[16,512]{1,0:T(8,128)S(1)}, f32[16,512]{1,0:T(8,128)S(1)}, u32[]{:S(2)}, u32[]{:S(2)}) collective-permute-start(f32[16,512]{1,0:T(8,128)S(1)} %constant_dynamic-slice_fusion), channel_id=1, source_target_pairs={{0,20},{1,21},{2,22},{3,23},{4,16},{5,17},{6,18},{7,19},{8,28},{9,... | collective-permute-start | bytes 98312 | tf_op jit(solution)/shard_map/ppermute | solution.py:45
  82.1 3.5 %all-to-all-start.1 = ((f32[8,128,128]{1,2,0:T(8,128)}), f32[8,128,128]{1,2,0:T(8,128)S(1)}, u32[]{:S(2)}, u32[]{:S(2)}) async-start(f32[8,128,128]{1,2,0:T(8,128)} %broadcast_in_dim.4), calls=%async_computation.1 | async-start | bytes 1048576 | tf_op jit(solution)/shard_map/all_to_all | solution.py:176
  85.8 2.8 %collective-permute-done.19 = f32[16,512]{1,0:T(8,128)S(1)} collective-permute-done((f32[16,512]{1,0:T(8,128)S(1)}, f32[16,512]{1,0:T(8,128)S(1)}, u32[]{:S(2)}, u32[]{:S(2)}) %collective-permute-start.19) | collective-permute-done | bytes 32800 | tf_op jit(solution)/shard_map/ppermute | solution.py:45
  89.4 3.2 %collective-permute-done.20 = f32[16,512]{1,0:T(8,128)S(1)} collective-permute-done((f32[16,512]{1,0:T(8,128)S(1)}, f32[16,512]{1,0:T(8,128)S(1)}, u32[]{:S(2)}, u32[]{:S(2)}) %collective-permute-start.20) | collective-permute-done | bytes 32800 | tf_op jit(solution)/shard_map/ppermute | solution.py:45
  92.6 4.3 %collective-permute-start.21 = (f32[16,512]{1,0:T(8,128)S(1)}, f32[16,512]{1,0:T(8,128)S(1)}, u32[]{:S(2)}, u32[]{:S(2)}) collective-permute-start(f32[16,512]{1,0:T(8,128)S(1)} %add.34), channel_id=1, source_target_pairs={{0,128},{1,129},{2,130},{3,131},{4,132},{5,133},{6,134},{7,135},{8... | collective-permute-start | bytes 98312 | tf_op jit(solution)/shard_map/ppermute | solution.py:45
  96.9 2.4 %collective-permute-done.21 = f32[16,512]{1,0:T(8,128)S(1)} collective-permute-done((f32[16,512]{1,0:T(8,128)S(1)}, f32[16,512]{1,0:T(8,128)S(1)}, u32[]{:S(2)}, u32[]{:S(2)}) %collective-permute-start.21) | collective-permute-done | bytes 32800 | tf_op jit(solution)/shard_map/ppermute | solution.py:45
  100.1 5.2 %all-to-all-start.2 = ((f32[16,16,512]{2,1,0:T(8,128)}), f32[16,16,512]{2,1,0:T(8,128)S(1)}, u32[]{:S(2)}, u32[]{:S(2)}) async-start(f32[16,16,512]{2,1,0:T(8,128)} %broadcast_in_dim.5), calls=%async_computation.2 | async-start | bytes 1048576 | tf_op jit(solution)/shard_map/all_to_all | solution.py:176
  105.4 8.9 %all-to-all-done.2 = f32[16,16,512]{2,1,0:T(8,128)S(1)} async-done(((f32[16,16,512]{2,1,0:T(8,128)}), f32[16,16,512]{2,1,0:T(8,128)S(1)}, u32[]{:S(2)}, u32[]{:S(2)}) %all-to-all-start.2) | async-done | bytes 524320 | tf_op jit(solution)/shard_map/all_to_all | solution.py:176
  114.4 5.5 %collective-permute-start.22 = (f32[8,32,512]{2,1,0:T(8,128)S(1)}, f32[8,32,512]{2,1,0:T(8,128)S(1)}, u32[]{:S(2)}, u32[]{:S(2)}) collective-permute-start(f32[8,32,512]{2,1,0:T(8,128)S(1)} %bitcast.62), channel_id=1, source_target_pairs={{0,8},{1,9},{2,10},{3,11},{4,12},{5,13},{6,14},{7,15},{8,0},{9,1},... | collective-permute-start | bytes 1572872 | tf_op jit(solution)/shard_map/ppermute | solution.py:45
  120.3 1.4 %convolution_multiply_fusion = f32[256,512]{1,0:T(8,128)} fusion(f32[512,512]{1,0:T(8,128)S(1)} %copy-done, f32[64,8,2,128]{3,2,1,0:T(2,128)S(1)} %bitcast.65), kind=kOutput, calls=%fused_computation | convolution fusion | flops 402784256 | bytes 2097152 | tf_op jit(solution)/shard_map/dot_general | solution.py:49
  (68 shorter events, 16.5 us)
Async XLA Ops:
  0.6 18.7 %copy-start = (f32[512,512]{1,0:T(8,128)S(1)}, f32[512,512]{1,0:T(8,128)}, u32[]{:S(2)}) copy-start(f32[512,512]{1,0:T(8,128)} %param.9) | copy-start | bytes 3145732
  0.6 18.7 %copy-start.1 = (f32[256,512]{1,0:T(8,128)S(1)}, f32[256,512]{1,0:T(8,128)}, u32[]{:S(2)}) copy-start(f32[256,512]{1,0:T(8,128)} %param.5) | copy-start | bytes 1572868
  0.7 8.6 %collective-permute-start = (f32[32,768]{1,0:T(8,128)}, f32[32,768]{1,0:T(8,128)S(1)}, u32[]{:S(2)}, u32[]{:S(2)}) collective-permute-start(f32[32,768]{1,0:T(8,128)} %param.8), channel_id=1, source_target_pairs={{0,20},{1,21},{2,22},{3,23},{4,16},{5,17},{6,18},{7,19},{8,28},{9,... | collective-permute-start | bytes 294920 | tf_op jit(solution)/shard_map/ppermute | solution.py:45
  4.1 5.2 %collective-permute-start.1 = (f32[32,512]{1,0:T(8,128)}, f32[32,512]{1,0:T(8,128)S(1)}, u32[]{:S(2)}, u32[]{:S(2)}) collective-permute-start(f32[32,512]{1,0:T(8,128)} %param.7), channel_id=1, source_target_pairs={{0,20},{1,21},{2,22},{3,23},{4,16},{5,17},{6,18},{7,19},{8,28},{9,... | collective-permute-start | bytes 196616 | tf_op jit(solution)/shard_map/ppermute | solution.py:45
  10.2 3.1 %collective-permute-start.2 = (f32[64,1280]{1,0:T(8,128)S(1)}, f32[64,1280]{1,0:T(8,128)S(1)}, u32[]{:S(2)}, u32[]{:S(2)}) collective-permute-start(f32[64,1280]{1,0:T(8,128)S(1)} %maximum_maximum_fusion.refs_2_), channel_id=1, source_target_pairs={{0,8},{1,9},{2,10},{3,11},{4,12},{5,13},{6,14},{7,15},{8,0},{9,1},... | collective-permute-start | bytes 983048 | tf_op jit(solution)/shard_map/ppermute | solution.py:45
  13.3 9.3 %collective-permute-start.3 = (f32[64,1280]{1,0:T(8,128)S(1)}, f32[64,1280]{1,0:T(8,128)S(1)}, u32[]{:S(2)}, u32[]{:S(2)}) collective-permute-start(f32[64,1280]{1,0:T(8,128)S(1)} %maximum_maximum_fusion.refs_2_), channel_id=1, source_target_pairs={{0,32},{1,33},{2,34},{3,35},{4,36},{5,37},{6,38},{7,39},{8,232},{9... | collective-permute-start | bytes 983048 | tf_op jit(solution)/shard_map/ppermute | solution.py:45
  18.6 7.5 %collective-permute-start.8 = (f32[64,1280]{1,0:T(8,128)S(1)}, f32[64,1280]{1,0:T(8,128)S(1)}, u32[]{:S(2)}, u32[]{:S(2)}) collective-permute-start(f32[64,1280]{1,0:T(8,128)S(1)} %collective-permute-done.2.refs_3_), channel_id=1, source_target_pairs={{0,32},{1,33},{2,34},{3,35},{4,36},{5,37},{6,38},{7,39},{8,232},{9... | collective-permute-start | bytes 983048 | tf_op jit(solution)/shard_map/ppermute | solution.py:45
  22.6 13.5 %collective-permute-start.16 = (f32[64,1280]{1,0:T(8,128)S(1)}, f32[64,1280]{1,0:T(8,128)S(1)}, u32[]{:S(2)}, u32[]{:S(2)}) collective-permute-start(f32[64,1280]{1,0:T(8,128)S(1)} %collective-permute-done.3.refs_2_), channel_id=1, source_target_pairs={{0,8},{1,9},{2,10},{3,11},{4,12},{5,13},{6,14},{7,15},{8,0},{9,1},... | collective-permute-start | bytes 983048 | tf_op jit(solution)/shard_map/ppermute | solution.py:45
  24.3 6.4 %collective-permute-start.4 = (f32[64,1280]{1,0:T(8,128)S(1)}, f32[64,1280]{1,0:T(8,128)S(1)}, u32[]{:S(2)}, u32[]{:S(2)}) collective-permute-start(f32[64,1280]{1,0:T(8,128)S(1)} %collective-permute-done.3.refs_2_), channel_id=1, source_target_pairs={{0,32},{1,33},{2,34},{3,35},{4,36},{5,37},{6,38},{7,39},{8,232},{9... | collective-permute-start | bytes 983048 | tf_op jit(solution)/shard_map/ppermute | solution.py:45
  26.1 7.9 %collective-permute-start.9 = (f32[64,1280]{1,0:T(8,128)S(1)}, f32[64,1280]{1,0:T(8,128)S(1)}, u32[]{:S(2)}, u32[]{:S(2)}) collective-permute-start(f32[64,1280]{1,0:T(8,128)S(1)} %collective-permute-done.8.refs_2_), channel_id=1, source_target_pairs={{0,32},{1,33},{2,34},{3,35},{4,36},{5,37},{6,38},{7,39},{8,232},{9... | collective-permute-start | bytes 983048 | tf_op jit(solution)/shard_map/ppermute | solution.py:45
  30.6 7.8 %collective-permute-start.15 = (f32[64,1280]{1,0:T(8,128)S(1)}, f32[64,1280]{1,0:T(8,128)S(1)}, u32[]{:S(2)}, u32[]{:S(2)}) collective-permute-start(f32[64,1280]{1,0:T(8,128)S(1)} %collective-permute-done.8.refs_2_), channel_id=1, source_target_pairs={{0,8},{1,9},{2,10},{3,11},{4,12},{5,13},{6,14},{7,15},{8,0},{9,1},... | collective-permute-start | bytes 983048 | tf_op jit(solution)/shard_map/ppermute | solution.py:45
  30.7 13.7 %collective-permute-start.14 = (f32[64,1280]{1,0:T(8,128)S(1)}, f32[64,1280]{1,0:T(8,128)S(1)}, u32[]{:S(2)}, u32[]{:S(2)}) collective-permute-start(f32[64,1280]{1,0:T(8,128)S(1)} %collective-permute-done.4.refs_2_), channel_id=1, source_target_pairs={{0,8},{1,9},{2,10},{3,11},{4,12},{5,13},{6,14},{7,15},{8,0},{9,1},... | collective-permute-start | bytes 983048 | tf_op jit(solution)/shard_map/ppermute | solution.py:45
  32.6 7.2 %collective-permute-start.5 = (f32[64,1280]{1,0:T(8,128)S(1)}, f32[64,1280]{1,0:T(8,128)S(1)}, u32[]{:S(2)}, u32[]{:S(2)}) collective-permute-start(f32[64,1280]{1,0:T(8,128)S(1)} %collective-permute-done.4.refs_2_), channel_id=1, source_target_pairs={{0,32},{1,33},{2,34},{3,35},{4,36},{5,37},{6,38},{7,39},{8,232},{9... | collective-permute-start | bytes 983048 | tf_op jit(solution)/shard_map/ppermute | solution.py:45
  34.0 11.8 %collective-permute-start.13 = (f32[64,1280]{1,0:T(8,128)S(1)}, f32[64,1280]{1,0:T(8,128)S(1)}, u32[]{:S(2)}, u32[]{:S(2)}) collective-permute-start(f32[64,1280]{1,0:T(8,128)S(1)} %collective-permute-done.9.refs_2_), channel_id=1, source_target_pairs={{0,8},{1,9},{2,10},{3,11},{4,12},{5,13},{6,14},{7,15},{8,0},{9,1},... | collective-permute-start | bytes 983048 | tf_op jit(solution)/shard_map/ppermute | solution.py:45
  36.1 6.2 %collective-permute-start.10 = (f32[64,1280]{1,0:T(8,128)S(1)}, f32[64,1280]{1,0:T(8,128)S(1)}, u32[]{:S(2)}, u32[]{:S(2)}) collective-permute-start(f32[64,1280]{1,0:T(8,128)S(1)} %collective-permute-done.9.refs_2_), channel_id=1, source_target_pairs={{0,32},{1,33},{2,34},{3,35},{4,36},{5,37},{6,38},{7,39},{8,232},{9... | collective-permute-start | bytes 983048 | tf_op jit(solution)/shard_map/ppermute | solution.py:45
  39.8 9.3 %collective-permute-start.12 = (f32[64,1280]{1,0:T(8,128)S(1)}, f32[64,1280]{1,0:T(8,128)S(1)}, u32[]{:S(2)}, u32[]{:S(2)}) collective-permute-start(f32[64,1280]{1,0:T(8,128)S(1)} %collective-permute-done.5.refs_2_), channel_id=1, source_target_pairs={{0,8},{1,9},{2,10},{3,11},{4,12},{5,13},{6,14},{7,15},{8,0},{9,1},... | collective-permute-start | bytes 983048 | tf_op jit(solution)/shard_map/ppermute | solution.py:45
  40.9 6.5 %collective-permute-start.6 = (f32[64,1280]{1,0:T(8,128)S(1)}, f32[64,1280]{1,0:T(8,128)S(1)}, u32[]{:S(2)}, u32[]{:S(2)}) collective-permute-start(f32[64,1280]{1,0:T(8,128)S(1)} %collective-permute-done.5.refs_2_), channel_id=1, source_target_pairs={{0,32},{1,33},{2,34},{3,35},{4,36},{5,37},{6,38},{7,39},{8,232},{9... | collective-permute-start | bytes 983048 | tf_op jit(solution)/shard_map/ppermute | solution.py:45
  42.3 8.3 %collective-permute-start.11 = (f32[64,1280]{1,0:T(8,128)S(1)}, f32[64,1280]{1,0:T(8,128)S(1)}, u32[]{:S(2)}, u32[]{:S(2)}) collective-permute-start(f32[64,1280]{1,0:T(8,128)S(1)} %collective-permute-done.10.refs_2_), channel_id=1, source_target_pairs={{0,8},{1,9},{2,10},{3,11},{4,12},{5,13},{6,14},{7,15},{8,0},{9,1},... | collective-permute-start | bytes 983048 | tf_op jit(solution)/shard_map/ppermute | solution.py:45
  47.3 4.8 %collective-permute-start.7 = (f32[64,1280]{1,0:T(8,128)S(1)}, f32[64,1280]{1,0:T(8,128)S(1)}, u32[]{:S(2)}, u32[]{:S(2)}) collective-permute-start(f32[64,1280]{1,0:T(8,128)S(1)} %collective-permute-done.6.refs_3_), channel_id=1, source_target_pairs={{0,8},{1,9},{2,10},{3,11},{4,12},{5,13},{6,14},{7,15},{8,0},{9,1},... | collective-permute-start | bytes 983048 | tf_op jit(solution)/shard_map/ppermute | solution.py:45
  55.4 19.9 %all-to-all-start = ((f32[8,272,128]{2,1,0:T(8,128)}), f32[8,272,128]{2,1,0:T(8,128)S(1)}, u32[]{:S(2)}, u32[]{:S(2)}) async-start(f32[8,272,128]{2,1,0:T(8,128)} %add_texts.15), calls=%async_computation | async-start | bytes 2228224 | tf_op jit(solution)/shard_map/all_to_all | solution.py:200
  75.5 1.1 copy-start.2
  76.8 2.0 %collective-permute-start.17 = (f32[32,512]{1,0:T(8,128)S(1)}, f32[32,512]{1,0:T(8,128)S(1)}, u32[]{:S(2)}, u32[]{:S(2)}) collective-permute-start(f32[32,512]{1,0:T(8,128)S(1)} %constant_dynamic-slice_fusion.1), channel_id=1, source_target_pairs={{0,8},{1,9},{2,10},{3,11},{4,12},{5,13},{6,14},{7,15},{8,0},{9,1},... | collective-permute-start | bytes 196616 | tf_op jit(solution)/shard_map/ppermute | solution.py:45
  78.8 6.8 %collective-permute-start.18 = (f32[16,512]{1,0:T(8,128)S(1)}, f32[16,512]{1,0:T(8,128)S(1)}, u32[]{:S(2)}, u32[]{:S(2)}) collective-permute-start(f32[16,512]{1,0:T(8,128)S(1)} %constant_dynamic-slice_fusion), channel_id=1, source_target_pairs={{0,20},{1,21},{2,22},{3,23},{4,16},{5,17},{6,18},{7,19},{8,28},{9,... | collective-permute-start | bytes 98312 | tf_op jit(solution)/shard_map/ppermute | solution.py:45
  82.1 17.1 %all-to-all-start.1 = ((f32[8,128,128]{1,2,0:T(8,128)}), f32[8,128,128]{1,2,0:T(8,128)S(1)}, u32[]{:S(2)}, u32[]{:S(2)}) async-start(f32[8,128,128]{1,2,0:T(8,128)} %broadcast_in_dim.4), calls=%async_computation.1 | async-start | bytes 1048576 | tf_op jit(solution)/shard_map/all_to_all | solution.py:176
  85.7 2.9 %collective-permute-start.19 = (f32[16,512]{1,0:T(8,128)S(1)}, f32[16,512]{1,0:T(8,128)S(1)}, u32[]{:S(2)}, u32[]{:S(2)}) collective-permute-start(f32[16,512]{1,0:T(8,128)S(1)} %dynamic-slice_add_fusion.1), channel_id=1, source_target_pairs={{0,32},{1,33},{2,34},{3,35},{4,36},{5,37},{6,38},{7,39},{8,40},{9,... | collective-permute-start | bytes 98312 | tf_op jit(solution)/shard_map/ppermute | solution.py:45
  88.5 4.0 %collective-permute-start.20 = (f32[16,512]{1,0:T(8,128)S(1)}, f32[16,512]{1,0:T(8,128)S(1)}, u32[]{:S(2)}, u32[]{:S(2)}) collective-permute-start(f32[16,512]{1,0:T(8,128)S(1)} %add.33), channel_id=1, source_target_pairs={{0,64},{1,65},{2,66},{3,67},{4,68},{5,69},{6,70},{7,71},{8,72},{9,... | collective-permute-start | bytes 98312 | tf_op jit(solution)/shard_map/ppermute | solution.py:45
  92.6 6.7 %collective-permute-start.21 = (f32[16,512]{1,0:T(8,128)S(1)}, f32[16,512]{1,0:T(8,128)S(1)}, u32[]{:S(2)}, u32[]{:S(2)}) collective-permute-start(f32[16,512]{1,0:T(8,128)S(1)} %add.34), channel_id=1, source_target_pairs={{0,128},{1,129},{2,130},{3,131},{4,132},{5,133},{6,134},{7,135},{8... | collective-permute-start | bytes 98312 | tf_op jit(solution)/shard_map/ppermute | solution.py:45
  100.1 14.1 %all-to-all-start.2 = ((f32[16,16,512]{2,1,0:T(8,128)}), f32[16,16,512]{2,1,0:T(8,128)S(1)}, u32[]{:S(2)}, u32[]{:S(2)}) async-start(f32[16,16,512]{2,1,0:T(8,128)} %broadcast_in_dim.5), calls=%async_computation.2 | async-start | bytes 1048576 | tf_op jit(solution)/shard_map/all_to_all | solution.py:176
  114.4 7.4 %collective-permute-start.22 = (f32[8,32,512]{2,1,0:T(8,128)S(1)}, f32[8,32,512]{2,1,0:T(8,128)S(1)}, u32[]{:S(2)}, u32[]{:S(2)}) collective-permute-start(f32[8,32,512]{2,1,0:T(8,128)S(1)} %bitcast.62), channel_id=1, source_target_pairs={{0,8},{1,9},{2,10},{3,11},{4,12},{5,13},{6,14},{7,15},{8,0},{9,1},... | collective-permute-start | bytes 1572872 | tf_op jit(solution)/shard_map/ppermute | solution.py:45

commit v3 on v2

--- a/solution.py
+++ b/solution.py
@@ -37,7 +37,7 @@
 X_FLIP = moves(lambda z, xh, core, xl, y: (z, 1 - xh, core, 1 - xl, y))
 CORE = moves(lambda z, xh, core, xl, y: (z, xh, 1 - core, xl, y))
 Z_FOLD = tuple(
-    moves(lambda z, xh, core, xl, y, bit=bit: (z ^ bit, xh, core, xl, y)) for bit in (1, 2, 4)
+    moves(lambda z, xh, core, xl, y, bit=bit: (z ^ bit, xh, core, xl, y)) for bit in (1, 2, 6)
 )
 
 
@@ -184,18 +184,23 @@
     folded = scale_s * dot(image_student, head, NT)
     images = scale_t * image_teacher
 
-    own = jnp.concatenate([text_teacher, text_features], axis=1)
-    across = [move(text_teacher, X_FLIP), move(text_features, X_FLIP)]
-    one = jnp.concatenate([own, jnp.concatenate(across, axis=1)], axis=0)
-    one, two = lax.optimization_barrier((one, move(one, CORE)))
+    own = [text_teacher, text_features]
+    near = [move(array, CORE) for array in own]
+    far = [move(array, X_FLIP) for array in own]
+    one = jnp.concatenate([jnp.concatenate(part, axis=1) for part in (own, near)], axis=0)
+    *far, _ = lax.optimization_barrier((*far, one))
+    last = [move(array, CORE) for array in far]
+    two = jnp.concatenate([jnp.concatenate(part, axis=1) for part in (far, last)], axis=0)
     state = add_texts(folded, images, [one, two])
     for step in range(3):
         one, two = move(one, Z_NEXT), move(two, Z_NEXT)
         state = add_texts(folded, images, [one, move(one, CORE)], state)
         state = add_texts(folded, images, [two, move(two, CORE)], state)
-    one = move(one, Z_NEXT)
+    one, two = move(one[:SHARD], Z_NEXT), move(two[:SHARD], Z_NEXT)
+    two, *state = lax.optimization_barrier((two, *state))
+    state = add_texts(folded, images, [one, move(one, CORE)], state)
     place = jnp.arange(8, dtype=jnp.int32) ^ (4 * xh).astype(jnp.int32)
-    (both,) = add_texts(folded, images, [one, move(one, CORE)], state, place)
+    (both,) = add_texts(folded, images, [two, move(two, CORE)], state, place)
 
     got = lax.all_to_all(both, ("xl", "y"), 0, 0, tiled=True)
     stats = got[:, ROWS:].reshape(8, 2, 8, 128)[:, :, :4]

time: 123 us -> 119 us (0.967)
  waiting for transfers between devices: 42.7 us -> 35.9 us
  other arithmetic: 4.62 us -> 2.58 us
  Pallas kernels: 13.4 us -> 14.8 us
    ppermute x23 -> x28, waiting for transfers between devices: 18.1 us -> 11.2 us  [move(): return lax.ppermute(array, AXES, pairs)]
    pallas_call x8 -> x9, Pallas kernels: 13.4 us -> 14.8 us  [add_texts(): pl.pallas_call(body, out_shape=shapes, in_specs=in_specs, out_specs=[vmem...]
    ppermute x23 -> x28, starting transfers between devices: 43.7 us -> 44.9 us  [move(): return lax.ppermute(array, AXES, pairs)]
  transfers between devices with their start and end apart: 26 -> 31, of which waited for: 12 -> 9; matrix products, arithmetic and copies ran while one was open for 4% -> 4% of each run, Pallas kernels for 8% -> 10%
where the time goes in v3:
time: 119 us
  starting transfers between devices  57.7 us (48%)
  waiting for transfers between devices  35.9 us (30%)
  Pallas kernels  14.8 us (12%)
  matrix products  3.37 us (3%)
  local copies, waits for them, and re-layouts  3.16 us (3%)
  other arithmetic  2.58 us (2%)
    ppermute x28, starting transfers between devices, move(): return lax.ppermute(array, AXES, pairs)  44.9 us
    all_to_all x1, waiting for transfers between devices, shards(): got = lax.all_to_all(both, ('xl', 'y'), 0, 0, tiled=True)  15.7 us
    pallas_call x9, Pallas kernels, add_texts(): pl.pallas_call(body, out_shape=shapes, in_specs=in_specs, out_specs=[vmem...  14.8 us
    ppermute x28, waiting for transfers between devices, move(): return lax.ppermute(array, AXES, pairs)  11.2 us
    all_to_all x2, waiting for transfers between devices, to_all(): return lax.all_to_all(pieces, axes, 0, 0, tiled=True)  9 us
    all_to_all x2, starting transfers between devices, to_all(): return lax.all_to_all(pieces, axes, 0, 0, tiled=True)  8.66 us
    all_to_all x1, starting transfers between devices, shards(): got = lax.all_to_all(both, ('xl', 'y'), 0, 0, tiled=True)  4.19 us
    dot_general x3, matrix products, dot(): lax.dot_general(a, b, (dims, ((), ())), precision=HIGH, preferred_element...  3.37 us
  transfers between devices with their start and end apart: 31, of which 9 were waited for; matrix products, arithmetic and copies ran while one was open for 4% of the time, Pallas kernels for 10%

profile of v3, /device:TPU:1, one launch (start us, length us, event | category | flops | bytes accessed | tf_op | source)
XLA Modules:
  0.0 118.6 jit_solution(17321107965681310423)
XLA Ops:
  0.7 3.3 %collective-permute-start.2 = (f32[32,768]{1,0:T(8,128)}, f32[32,768]{1,0:T(8,128)S(1)}, u32[]{:S(2)}, u32[]{:S(2)}) collective-permute-start(f32[32,768]{1,0:T(8,128)} %param.8), channel_id=1, source_target_pairs={{0,8},{1,9},{2,10},{3,11},{4,12},{5,13},{6,14},{7,15},{8,0},{9,1},... | collective-permute-start | bytes 294920 | tf_op jit(solution)/shard_map/ppermute | solution.py:45
  5.1 1.9 %collective-permute-start.1 = (f32[32,512]{1,0:T(8,128)}, f32[32,512]{1,0:T(8,128)S(1)}, u32[]{:S(2)}, u32[]{:S(2)}) collective-permute-start(f32[32,512]{1,0:T(8,128)} %param.7), channel_id=1, source_target_pairs={{0,20},{1,21},{2,22},{3,23},{4,16},{5,17},{6,18},{7,19},{8,28},{9,... | collective-permute-start | bytes 196616 | tf_op jit(solution)/shard_map/ppermute | solution.py:45
  7.0 1.7 %convolution_multiply_fusion.1.refs_0_.refs_1_ = f32[256,512]{1,0:T(8,128)S(1)} fusion(f32[256,512]{1,0:T(8,128)} %param.5, f32[512,512]{1,0:T(8,128)S(1)} %copy-done), kind=kOutput, calls=%fused_computation.1 | convolution fusion | flops 402784256 | bytes 2097152 | tf_op jit(solution)/shard_map/dot_general | solution.py:49
  9.6 3.9 %collective-permute-start.11 = (f32[64,1280]{1,0:T(8,128)S(1)}, f32[64,1280]{1,0:T(8,128)S(1)}, u32[]{:S(2)}, u32[]{:S(2)}) collective-permute-start(f32[64,1280]{1,0:T(8,128)S(1)} %maximum_maximum_fusion.refs_2_), channel_id=1, source_target_pairs={{0,32},{1,33},{2,34},{3,35},{4,36},{5,37},{6,38},{7,39},{8,232},{9... | collective-permute-start | bytes 983048 | tf_op jit(solution)/shard_map/ppermute | solution.py:45
  15.0 3.0 %collective-permute-start.6 = (f32[64,1280]{1,0:T(8,128)S(1)}, f32[64,1280]{1,0:T(8,128)S(1)}, u32[]{:S(2)}, u32[]{:S(2)}) collective-permute-start(f32[64,1280]{1,0:T(8,128)S(1)} %maximum_maximum_fusion.1.refs_3_), channel_id=1, source_target_pairs={{0,32},{1,33},{2,34},{3,35},{4,36},{5,37},{6,38},{7,39},{8,232},{9... | collective-permute-start | bytes 983048 | tf_op jit(solution)/shard_map/ppermute | solution.py:45
  19.3 1.7 %collective-permute-start.12 = (f32[64,1280]{1,0:T(8,128)S(1)}, f32[64,1280]{1,0:T(8,128)S(1)}, u32[]{:S(2)}, u32[]{:S(2)}) collective-permute-start(f32[64,1280]{1,0:T(8,128)S(1)} %collective-permute-done.11.refs_2_), channel_id=1, source_target_pairs={{0,32},{1,33},{2,34},{3,35},{4,36},{5,37},{6,38},{7,39},{8,232},{9... | collective-permute-start | bytes 983048 | tf_op jit(solution)/shard_map/ppermute | solution.py:45
  23.7 1.5 %collective-permute-start.7 = (f32[64,1280]{1,0:T(8,128)S(1)}, f32[64,1280]{1,0:T(8,128)S(1)}, u32[]{:S(2)}, u32[]{:S(2)}) collective-permute-start(f32[64,1280]{1,0:T(8,128)S(1)} %collective-permute-done.6.refs_2_), channel_id=1, source_target_pairs={{0,32},{1,33},{2,34},{3,35},{4,36},{5,37},{6,38},{7,39},{8,232},{9... | collective-permute-start | bytes 983048 | tf_op jit(solution)/shard_map/ppermute | solution.py:45
  25.6 2.1 %collective-permute-start.16 = (f32[64,1280]{1,0:T(8,128)S(1)}, f32[64,1280]{1,0:T(8,128)S(1)}, u32[]{:S(2)}, u32[]{:S(2)}) collective-permute-start(f32[64,1280]{1,0:T(8,128)S(1)} %collective-permute-done.12.refs_2_), channel_id=1, source_target_pairs={{0,8},{1,9},{2,10},{3,11},{4,12},{5,13},{6,14},{7,15},{8,0},{9,1},... | collective-permute-start | bytes 983048 | tf_op jit(solution)/shard_map/ppermute | solution.py:45
  28.7 1.5 %add_texts.10 = (f32[256,128]{1,0:T(8,128)S(1)}, f32[256,512]{1,0:T(8,128)S(1)}, f32[256,512]{1,0:T(8,128)S(1)}) custom-call(f32[256,512]{1,0:T(8,128)S(1)} %convolution_multiply_fusion.1.refs_0_.refs_1_, f32[256,768]{1,0:T(8,128)S(1)} %broadcast_multiply_fusion.refs_1_.refs_2_, f32[64,1280]{1,0:T(8,128)S(1)} %collective-permute-done.11.refs_2_, ...), custom_call_target="tpu_custom_call" | custom-call | flops 18119393280 | bytes 4194304 | tf_op jit(solution)/shard_map/add_texts/pallas_call | solution.py:152
  30.2 1.8 %collective-permute-start.15 = (f32[64,1280]{1,0:T(8,128)S(1)}, f32[64,1280]{1,0:T(8,128)S(1)}, u32[]{:S(2)}, u32[]{:S(2)}) collective-permute-start(f32[64,1280]{1,0:T(8,128)S(1)} %collective-permute-done.7.refs_2_), channel_id=1, source_target_pairs={{0,8},{1,9},{2,10},{3,11},{4,12},{5,13},{6,14},{7,15},{8,0},{9,1},... | collective-permute-start | bytes 983048 | tf_op jit(solution)/shard_map/ppermute | solution.py:45
  32.7 1.5 %add_texts.11 = (f32[256,128]{1,0:T(8,128)S(1)}, f32[256,512]{1,0:T(8,128)S(1)}, f32[256,512]{1,0:T(8,128)S(1)}) custom-call(f32[256,512]{1,0:T(8,128)S(1)} %convolution_multiply_fusion.1.refs_0_.refs_1_, f32[256,768]{1,0:T(8,128)S(1)} %broadcast_multiply_fusion.refs_1_.refs_2_, f32[64,1280]{1,0:T(8,128)S(1)} %collective-permute-done.6.refs_2_, ...), custom_call_target="tpu_custom_call" | custom-call | flops 18119393280 | bytes 4194304 | tf_op jit(solution)/shard_map/add_texts/pallas_call | solution.py:152
  34.2 1.8 %collective-permute-start.20 = (f32[32,1280]{1,0:T(8,128)S(1)}, f32[32,1280]{1,0:T(8,128)S(1)}, u32[]{:S(2)}, u32[]{:S(2)}) collective-permute-start(f32[32,1280]{1,0:T(8,128)S(1)} %slice.70), channel_id=1, source_target_pairs={{0,32},{1,33},{2,34},{3,35},{4,36},{5,37},{6,38},{7,39},{8,232},{9... | collective-permute-start | bytes 491528 | tf_op jit(solution)/shard_map/ppermute | solution.py:45
  36.1 1.5 %add_texts.12 = (f32[256,128]{1,0:T(8,128)S(1)}, f32[256,512]{1,0:T(8,128)S(1)}, f32[256,512]{1,0:T(8,128)S(1)}) custom-call(f32[256,512]{1,0:T(8,128)S(1)} %convolution_multiply_fusion.1.refs_0_.refs_1_, f32[256,768]{1,0:T(8,128)S(1)} %broadcast_multiply_fusion.refs_1_.refs_2_, f32[64,1280]{1,0:T(8,128)S(1)} %collective-permute-done.12.refs_2_, ...), custom_call_target="tpu_custom_call" | custom-call | flops 18119393280 | bytes 4194304 | tf_op jit(solution)/shard_map/add_texts/pallas_call | solution.py:152
  38.3 2.3 %collective-permute-start.9 = (f32[32,1280]{1,0:T(8,128)S(1)}, f32[32,1280]{1,0:T(8,128)S(1)}, u32[]{:S(2)}, u32[]{:S(2)}) collective-permute-start(f32[32,1280]{1,0:T(8,128)S(1)} %slice.69), channel_id=1, source_target_pairs={{0,32},{1,33},{2,34},{3,35},{4,36},{5,37},{6,38},{7,39},{8,232},{9... | collective-permute-start | bytes 491528 | tf_op jit(solution)/shard_map/ppermute | solution.py:45
  40.6 1.5 %add_texts.13 = (f32[256,128]{1,0:T(8,128)S(1)}, f32[256,512]{1,0:T(8,128)S(1)}, f32[256,512]{1,0:T(8,128)S(1)}) custom-call(f32[256,512]{1,0:T(8,128)S(1)} %convolution_multiply_fusion.1.refs_0_.refs_1_, f32[256,768]{1,0:T(8,128)S(1)} %broadcast_multiply_fusion.refs_1_.refs_2_, f32[64,1280]{1,0:T(8,128)S(1)} %collective-permute-done.7.refs_2_, ...), custom_call_target="tpu_custom_call" | custom-call | flops 18119393280 | bytes 4194304 | tf_op jit(solution)/shard_map/add_texts/pallas_call | solution.py:152
  42.6 1.5 %add_texts.14 = (f32[256,128]{1,0:T(8,128)S(1)}, f32[256,512]{1,0:T(8,128)S(1)}, f32[256,512]{1,0:T(8,128)S(1)}) custom-call(f32[256,512]{1,0:T(8,128)S(1)} %convolution_multiply_fusion.1.refs_0_.refs_1_, f32[256,768]{1,0:T(8,128)S(1)} %broadcast_multiply_fusion.refs_1_.refs_2_, f32[64,1280]{1,0:T(8,128)S(1)} %collective-permute-done.13.refs_2_, ...), custom_call_target="tpu_custom_call" | custom-call | flops 18119393280 | bytes 4194304 | tf_op jit(solution)/shard_map/add_texts/pallas_call | solution.py:152
  44.1 1.5 %add_texts.15 = (f32[256,128]{1,0:T(8,128)S(1)}, f32[256,512]{1,0:T(8,128)S(1)}, f32[256,512]{1,0:T(8,128)S(1)}) custom-call(f32[256,512]{1,0:T(8,128)S(1)} %convolution_multiply_fusion.1.refs_0_.refs_1_, f32[256,768]{1,0:T(8,128)S(1)} %broadcast_multiply_fusion.refs_1_.refs_2_, f32[64,1280]{1,0:T(8,128)S(1)} %collective-permute-done.8.refs_2_, ...), custom_call_target="tpu_custom_call" | custom-call | flops 18119393280 | bytes 4194304 | tf_op jit(solution)/shard_map/add_texts/pallas_call | solution.py:152
  46.9 1.5 %add_texts.16 = (f32[256,128]{1,0:T(8,128)S(1)}, f32[256,512]{1,0:T(8,128)S(1)}, f32[256,512]{1,0:T(8,128)S(1)}) custom-call(f32[256,512]{1,0:T(8,128)S(1)} %convolution_multiply_fusion.1.refs_0_.refs_1_, f32[256,768]{1,0:T(8,128)S(1)} %broadcast_multiply_fusion.refs_1_.refs_2_, f32[32,1280]{1,0:T(8,128)S(1)} %collective-permute-done.20.refs_2_, ...), custom_call_target="tpu_custom_call" | custom-call | flops 9059696640 | bytes 4194304 | tf_op jit(solution)/shard_map/add_texts/pallas_call | solution.py:152
  48.4 3.3 %add_texts.17 = f32[8,272,128]{2,1,0:T(8,128)} custom-call(s32[8]{0:T(128)S(1)} %iota_xor_fusion.refs_0_, f32[256,512]{1,0:T(8,128)S(1)} %convolution_multiply_fusion.1.refs_0_.refs_1_, f32[256,768]{1,0:T(8,128)S(1)} %broadcast_multiply_fusion.refs_1_.refs_2_, f32[32,1280]{1,0:T(8,128)S(1)} %collective-permute-done.9.refs_3_, ...), custom_call_target="tpu_custom_call" | custom-call | flops 9059696640 | bytes 4194304 | tf_op jit(solution)/shard_map/add_texts/pallas_call | solution.py:152
  51.7 4.2 %all-to-all-start = ((f32[8,272,128]{2,1,0:T(8,128)}), f32[8,272,128]{2,1,0:T(8,128)S(1)}, u32[]{:S(2)}, u32[]{:S(2)}) async-start(f32[8,272,128]{2,1,0:T(8,128)} %add_texts.17), calls=%async_computation | async-start | bytes 2228224 | tf_op jit(solution)/shard_map/all_to_all | solution.py:205
  55.9 15.7 %all-to-all-done = f32[8,272,128]{2,1,0:T(8,128)S(1)} async-done(((f32[8,272,128]{2,1,0:T(8,128)}), f32[8,272,128]{2,1,0:T(8,128)S(1)}, u32[]{:S(2)}, u32[]{:S(2)}) %all-to-all-start) | async-done | bytes 1114144 | tf_op jit(solution)/shard_map/all_to_all | solution.py:205
  74.9 3.5 %collective-permute-start.23 = (f32[16,512]{1,0:T(8,128)S(1)}, f32[16,512]{1,0:T(8,128)S(1)}, u32[]{:S(2)}, u32[]{:S(2)}) collective-permute-start(f32[16,512]{1,0:T(8,128)S(1)} %constant_dynamic-slice_fusion), channel_id=1, source_target_pairs={{0,20},{1,21},{2,22},{3,23},{4,16},{5,17},{6,18},{7,19},{8,28},{9,... | collective-permute-start | bytes 98312 | tf_op jit(solution)/shard_map/ppermute | solution.py:45
  79.3 3.5 %all-to-all-start.1 = ((f32[8,128,128]{1,2,0:T(8,128)}), f32[8,128,128]{1,2,0:T(8,128)S(1)}, u32[]{:S(2)}, u32[]{:S(2)}) async-start(f32[8,128,128]{1,2,0:T(8,128)} %broadcast_in_dim.4), calls=%async_computation.1 | async-start | bytes 1048576 | tf_op jit(solution)/shard_map/all_to_all | solution.py:176
  82.9 2.8 %collective-permute-done.24 = f32[16,512]{1,0:T(8,128)S(1)} collective-permute-done((f32[16,512]{1,0:T(8,128)S(1)}, f32[16,512]{1,0:T(8,128)S(1)}, u32[]{:S(2)}, u32[]{:S(2)}) %collective-permute-start.24) | collective-permute-done | bytes 32800 | tf_op jit(solution)/shard_map/ppermute | solution.py:45
  85.7 1.6 %collective-permute-start.25 = (f32[16,512]{1,0:T(8,128)S(1)}, f32[16,512]{1,0:T(8,128)S(1)}, u32[]{:S(2)}, u32[]{:S(2)}) collective-permute-start(f32[16,512]{1,0:T(8,128)S(1)} %add.33), channel_id=1, source_target_pairs={{0,64},{1,65},{2,66},{3,67},{4,68},{5,69},{6,70},{7,71},{8,72},{9,... | collective-permute-start | bytes 98312 | tf_op jit(solution)/shard_map/ppermute | solution.py:45
  87.3 2.3 %collective-permute-done.25 = f32[16,512]{1,0:T(8,128)S(1)} collective-permute-done((f32[16,512]{1,0:T(8,128)S(1)}, f32[16,512]{1,0:T(8,128)S(1)}, u32[]{:S(2)}, u32[]{:S(2)}) %collective-permute-start.25) | collective-permute-done | bytes 32800 | tf_op jit(solution)/shard_map/ppermute | solution.py:45
  89.7 1.5 %collective-permute-start.26 = (f32[16,512]{1,0:T(8,128)S(1)}, f32[16,512]{1,0:T(8,128)S(1)}, u32[]{:S(2)}, u32[]{:S(2)}) collective-permute-start(f32[16,512]{1,0:T(8,128)S(1)} %add.34), channel_id=1, source_target_pairs={{0,192},{1,193},{2,194},{3,195},{4,196},{5,197},{6,198},{7,199},{8... | collective-permute-start | bytes 98312 | tf_op jit(solution)/shard_map/ppermute | solution.py:45
  91.2 3.4 %collective-permute-done.26 = f32[16,512]{1,0:T(8,128)S(1)} collective-permute-done((f32[16,512]{1,0:T(8,128)S(1)}, f32[16,512]{1,0:T(8,128)S(1)}, u32[]{:S(2)}, u32[]{:S(2)}) %collective-permute-start.26) | collective-permute-done | bytes 32800 | tf_op jit(solution)/shard_map/ppermute | solution.py:45
  95.4 5.2 %all-to-all-start.2 = ((f32[16,16,512]{2,1,0:T(8,128)}), f32[16,16,512]{2,1,0:T(8,128)S(1)}, u32[]{:S(2)}, u32[]{:S(2)}) async-start(f32[16,16,512]{2,1,0:T(8,128)} %broadcast_in_dim.5), calls=%async_computation.2 | async-start | bytes 1048576 | tf_op jit(solution)/shard_map/all_to_all | solution.py:176
  100.6 9.0 %all-to-all-done.2 = f32[16,16,512]{2,1,0:T(8,128)S(1)} async-done(((f32[16,16,512]{2,1,0:T(8,128)}), f32[16,16,512]{2,1,0:T(8,128)S(1)}, u32[]{:S(2)}, u32[]{:S(2)}) %all-to-all-start.2) | async-done | bytes 524320 | tf_op jit(solution)/shard_map/all_to_all | solution.py:176
  109.7 5.8 %collective-permute-start.27 = (f32[8,32,512]{2,1,0:T(8,128)S(1)}, f32[8,32,512]{2,1,0:T(8,128)S(1)}, u32[]{:S(2)}, u32[]{:S(2)}) collective-permute-start(f32[8,32,512]{2,1,0:T(8,128)S(1)} %bitcast.62), channel_id=1, source_target_pairs={{0,8},{1,9},{2,10},{3,11},{4,12},{5,13},{6,14},{7,15},{8,0},{9,1},... | collective-permute-start | bytes 1572872 | tf_op jit(solution)/shard_map/ppermute | solution.py:45
  116.0 1.4 %convolution_multiply_fusion = f32[256,512]{1,0:T(8,128)} fusion(f32[512,512]{1,0:T(8,128)S(1)} %copy-done, f32[64,8,2,128]{3,2,1,0:T(2,128)S(1)} %bitcast.65), kind=kOutput, calls=%fused_computation | convolution fusion | flops 402784256 | bytes 2097152 | tf_op jit(solution)/shard_map/dot_general | solution.py:49
  (86 shorter events, 19.2 us)
Async XLA Ops:
  0.6 8.1 %copy-start.2 = (f32[256,768]{1,0:T(8,128)S(1)}, f32[256,768]{1,0:T(8,128)}, u32[]{:S(2)}) copy-start(f32[256,768]{1,0:T(8,128)} %param.6) | copy-start | bytes 2359300
  0.7 8.2 %collective-permute-start.2 = (f32[32,768]{1,0:T(8,128)}, f32[32,768]{1,0:T(8,128)S(1)}, u32[]{:S(2)}, u32[]{:S(2)}) collective-permute-start(f32[32,768]{1,0:T(8,128)} %param.8), channel_id=1, source_target_pairs={{0,8},{1,9},{2,10},{3,11},{4,12},{5,13},{6,14},{7,15},{8,0},{9,1},... | collective-permute-start | bytes 294920 | tf_op jit(solution)/shard_map/ppermute | solution.py:45
  4.0 9.6 %collective-permute-start = (f32[32,768]{1,0:T(8,128)}, f32[32,768]{1,0:T(8,128)S(1)}, u32[]{:S(2)}, u32[]{:S(2)}) collective-permute-start(f32[32,768]{1,0:T(8,128)} %param.8), channel_id=1, source_target_pairs={{0,20},{1,21},{2,22},{3,23},{4,16},{5,17},{6,18},{7,19},{8,28},{9,... | collective-permute-start | bytes 294920 | tf_op jit(solution)/shard_map/ppermute | solution.py:45
  4.7 4.1 %collective-permute-start.3 = (f32[32,512]{1,0:T(8,128)}, f32[32,512]{1,0:T(8,128)S(1)}, u32[]{:S(2)}, u32[]{:S(2)}) collective-permute-start(f32[32,512]{1,0:T(8,128)} %param.7), channel_id=1, source_target_pairs={{0,8},{1,9},{2,10},{3,11},{4,12},{5,13},{6,14},{7,15},{8,0},{9,1},... | collective-permute-start | bytes 196616 | tf_op jit(solution)/shard_map/ppermute | solution.py:45
  5.1 8.5 %collective-permute-start.1 = (f32[32,512]{1,0:T(8,128)}, f32[32,512]{1,0:T(8,128)S(1)}, u32[]{:S(2)}, u32[]{:S(2)}) collective-permute-start(f32[32,512]{1,0:T(8,128)} %param.7), channel_id=1, source_target_pairs={{0,20},{1,21},{2,22},{3,23},{4,16},{5,17},{6,18},{7,19},{8,28},{9,... | collective-permute-start | bytes 196616 | tf_op jit(solution)/shard_map/ppermute | solution.py:45
  9.6 8.3 %collective-permute-start.11 = (f32[64,1280]{1,0:T(8,128)S(1)}, f32[64,1280]{1,0:T(8,128)S(1)}, u32[]{:S(2)}, u32[]{:S(2)}) collective-permute-start(f32[64,1280]{1,0:T(8,128)S(1)} %maximum_maximum_fusion.refs_2_), channel_id=1, source_target_pairs={{0,32},{1,33},{2,34},{3,35},{4,36},{5,37},{6,38},{7,39},{8,232},{9... | collective-permute-start | bytes 983048 | tf_op jit(solution)/shard_map/ppermute | solution.py:45
  13.6 1.4 %collective-permute-start.4 = (f32[32,768]{1,0:T(8,128)S(1)}, f32[32,768]{1,0:T(8,128)S(1)}, u32[]{:S(2)}, u32[]{:S(2)}) collective-permute-start(f32[32,768]{1,0:T(8,128)S(1)} %collective-permute-done), channel_id=1, source_target_pairs={{0,8},{1,9},{2,10},{3,11},{4,12},{5,13},{6,14},{7,15},{8,0},{9,1},... | collective-permute-start | bytes 294920 | tf_op jit(solution)/shard_map/ppermute | solution.py:45
  13.6 1.4 %collective-permute-start.5 = (f32[32,512]{1,0:T(8,128)S(1)}, f32[32,512]{1,0:T(8,128)S(1)}, u32[]{:S(2)}, u32[]{:S(2)}) collective-permute-start(f32[32,512]{1,0:T(8,128)S(1)} %collective-permute-done.1), channel_id=1, source_target_pairs={{0,8},{1,9},{2,10},{3,11},{4,12},{5,13},{6,14},{7,15},{8,0},{9,1},... | collective-permute-start | bytes 196616 | tf_op jit(solution)/shard_map/ppermute | solution.py:45
  15.0 7.4 %collective-permute-start.6 = (f32[64,1280]{1,0:T(8,128)S(1)}, f32[64,1280]{1,0:T(8,128)S(1)}, u32[]{:S(2)}, u32[]{:S(2)}) collective-permute-start(f32[64,1280]{1,0:T(8,128)S(1)} %maximum_maximum_fusion.1.refs_3_), channel_id=1, source_target_pairs={{0,32},{1,33},{2,34},{3,35},{4,36},{5,37},{6,38},{7,39},{8,232},{9... | collective-permute-start | bytes 983048 | tf_op jit(solution)/shard_map/ppermute | solution.py:45
  18.0 10.7 %collective-permute-start.18 = (f32[64,1280]{1,0:T(8,128)S(1)}, f32[64,1280]{1,0:T(8,128)S(1)}, u32[]{:S(2)}, u32[]{:S(2)}) collective-permute-start(f32[64,1280]{1,0:T(8,128)S(1)} %collective-permute-done.11.refs_2_), channel_id=1, source_target_pairs={{0,8},{1,9},{2,10},{3,11},{4,12},{5,13},{6,14},{7,15},{8,0},{9,1},... | collective-permute-start | bytes 983048 | tf_op jit(solution)/shard_map/ppermute | solution.py:45
  19.3 6.2 %collective-permute-start.12 = (f32[64,1280]{1,0:T(8,128)S(1)}, f32[64,1280]{1,0:T(8,128)S(1)}, u32[]{:S(2)}, u32[]{:S(2)}) collective-permute-start(f32[64,1280]{1,0:T(8,128)S(1)} %collective-permute-done.11.refs_2_), channel_id=1, source_target_pairs={{0,32},{1,33},{2,34},{3,35},{4,36},{5,37},{6,38},{7,39},{8,232},{9... | collective-permute-start | bytes 983048 | tf_op jit(solution)/shard_map/ppermute | solution.py:45
  22.4 10.3 %collective-permute-start.17 = (f32[64,1280]{1,0:T(8,128)S(1)}, f32[64,1280]{1,0:T(8,128)S(1)}, u32[]{:S(2)}, u32[]{:S(2)}) collective-permute-start(f32[64,1280]{1,0:T(8,128)S(1)} %collective-permute-done.6.refs_2_), channel_id=1, source_target_pairs={{0,8},{1,9},{2,10},{3,11},{4,12},{5,13},{6,14},{7,15},{8,0},{9,1},... | collective-permute-start | bytes 983048 | tf_op jit(solution)/shard_map/ppermute | solution.py:45
  23.7 6.5 %collective-permute-start.7 = (f32[64,1280]{1,0:T(8,128)S(1)}, f32[64,1280]{1,0:T(8,128)S(1)}, u32[]{:S(2)}, u32[]{:S(2)}) collective-permute-start(f32[64,1280]{1,0:T(8,128)S(1)} %collective-permute-done.6.refs_2_), channel_id=1, source_target_pairs={{0,32},{1,33},{2,34},{3,35},{4,36},{5,37},{6,38},{7,39},{8,232},{9... | collective-permute-start | bytes 983048 | tf_op jit(solution)/shard_map/ppermute | solution.py:45
  25.6 10.6 %collective-permute-start.16 = (f32[64,1280]{1,0:T(8,128)S(1)}, f32[64,1280]{1,0:T(8,128)S(1)}, u32[]{:S(2)}, u32[]{:S(2)}) collective-permute-start(f32[64,1280]{1,0:T(8,128)S(1)} %collective-permute-done.12.refs_2_), channel_id=1, source_target_pairs={{0,8},{1,9},{2,10},{3,11},{4,12},{5,13},{6,14},{7,15},{8,0},{9,1},... | collective-permute-start | bytes 983048 | tf_op jit(solution)/shard_map/ppermute | solution.py:45
  27.6 6.5 %collective-permute-start.13 = (f32[64,1280]{1,0:T(8,128)S(1)}, f32[64,1280]{1,0:T(8,128)S(1)}, u32[]{:S(2)}, u32[]{:S(2)}) collective-permute-start(f32[64,1280]{1,0:T(8,128)S(1)} %collective-permute-done.12.refs_2_), channel_id=1, source_target_pairs={{0,32},{1,33},{2,34},{3,35},{4,36},{5,37},{6,38},{7,39},{8,232},{9... | collective-permute-start | bytes 983048 | tf_op jit(solution)/shard_map/ppermute | solution.py:45
  30.2 10.4 %collective-permute-start.15 = (f32[64,1280]{1,0:T(8,128)S(1)}, f32[64,1280]{1,0:T(8,128)S(1)}, u32[]{:S(2)}, u32[]{:S(2)}) collective-permute-start(f32[64,1280]{1,0:T(8,128)S(1)} %collective-permute-done.7.refs_2_), channel_id=1, source_target_pairs={{0,8},{1,9},{2,10},{3,11},{4,12},{5,13},{6,14},{7,15},{8,0},{9,1},... | collective-permute-start | bytes 983048 | tf_op jit(solution)/shard_map/ppermute | solution.py:45
  32.0 6.2 %collective-permute-start.8 = (f32[64,1280]{1,0:T(8,128)S(1)}, f32[64,1280]{1,0:T(8,128)S(1)}, u32[]{:S(2)}, u32[]{:S(2)}) collective-permute-start(f32[64,1280]{1,0:T(8,128)S(1)} %collective-permute-done.7.refs_2_), channel_id=1, source_target_pairs={{0,32},{1,33},{2,34},{3,35},{4,36},{5,37},{6,38},{7,39},{8,232},{9... | collective-permute-start | bytes 983048 | tf_op jit(solution)/shard_map/ppermute | solution.py:45
  34.2 7.8 %collective-permute-start.20 = (f32[32,1280]{1,0:T(8,128)S(1)}, f32[32,1280]{1,0:T(8,128)S(1)}, u32[]{:S(2)}, u32[]{:S(2)}) collective-permute-start(f32[32,1280]{1,0:T(8,128)S(1)} %slice.70), channel_id=1, source_target_pairs={{0,32},{1,33},{2,34},{3,35},{4,36},{5,37},{6,38},{7,39},{8,232},{9... | collective-permute-start | bytes 491528 | tf_op jit(solution)/shard_map/ppermute | solution.py:45
  36.0 6.7 %collective-permute-start.14 = (f32[64,1280]{1,0:T(8,128)S(1)}, f32[64,1280]{1,0:T(8,128)S(1)}, u32[]{:S(2)}, u32[]{:S(2)}) collective-permute-start(f32[64,1280]{1,0:T(8,128)S(1)} %collective-permute-done.13.refs_2_), channel_id=1, source_target_pairs={{0,8},{1,9},{2,10},{3,11},{4,12},{5,13},{6,14},{7,15},{8,0},{9,1},... | collective-permute-start | bytes 983048 | tf_op jit(solution)/shard_map/ppermute | solution.py:45
  38.3 7.3 %collective-permute-start.9 = (f32[32,1280]{1,0:T(8,128)S(1)}, f32[32,1280]{1,0:T(8,128)S(1)}, u32[]{:S(2)}, u32[]{:S(2)}) collective-permute-start(f32[32,1280]{1,0:T(8,128)S(1)} %slice.69), channel_id=1, source_target_pairs={{0,32},{1,33},{2,34},{3,35},{4,36},{5,37},{6,38},{7,39},{8,232},{9... | collective-permute-start | bytes 491528 | tf_op jit(solution)/shard_map/ppermute | solution.py:45
  40.6 3.6 %collective-permute-start.10 = (f32[64,1280]{1,0:T(8,128)S(1)}, f32[64,1280]{1,0:T(8,128)S(1)}, u32[]{:S(2)}, u32[]{:S(2)}) collective-permute-start(f32[64,1280]{1,0:T(8,128)S(1)} %collective-permute-done.8.refs_2_), channel_id=1, source_target_pairs={{0,8},{1,9},{2,10},{3,11},{4,12},{5,13},{6,14},{7,15},{8,0},{9,1},... | collective-permute-start | bytes 983048 | tf_op jit(solution)/shard_map/ppermute | solution.py:45
  42.0 4.9 %collective-permute-start.21 = (f32[32,1280]{1,0:T(8,128)S(1)}, f32[32,1280]{1,0:T(8,128)S(1)}, u32[]{:S(2)}, u32[]{:S(2)}) collective-permute-start(f32[32,1280]{1,0:T(8,128)S(1)} %collective-permute-done.20.refs_2_), channel_id=1, source_target_pairs={{0,8},{1,9},{2,10},{3,11},{4,12},{5,13},{6,14},{7,15},{8,0},{9,1},... | collective-permute-start | bytes 491528 | tf_op jit(solution)/shard_map/ppermute | solution.py:45
  45.6 2.8 %collective-permute-start.19 = (f32[32,1280]{1,0:T(8,128)S(1)}, f32[32,1280]{1,0:T(8,128)S(1)}, u32[]{:S(2)}, u32[]{:S(2)}) collective-permute-start(f32[32,1280]{1,0:T(8,128)S(1)} %collective-permute-done.9.refs_3_), channel_id=1, source_target_pairs={{0,8},{1,9},{2,10},{3,11},{4,12},{5,13},{6,14},{7,15},{8,0},{9,1},... | collective-permute-start | bytes 491528 | tf_op jit(solution)/shard_map/ppermute | solution.py:45
  51.7 19.9 %all-to-all-start = ((f32[8,272,128]{2,1,0:T(8,128)}), f32[8,272,128]{2,1,0:T(8,128)S(1)}, u32[]{:S(2)}, u32[]{:S(2)}) async-start(f32[8,272,128]{2,1,0:T(8,128)} %add_texts.17), calls=%async_computation | async-start | bytes 2228224 | tf_op jit(solution)/shard_map/all_to_all | solution.py:205
  73.1 1.7 %collective-permute-start.22 = (f32[32,512]{1,0:T(8,128)S(1)}, f32[32,512]{1,0:T(8,128)S(1)}, u32[]{:S(2)}, u32[]{:S(2)}) collective-permute-start(f32[32,512]{1,0:T(8,128)S(1)} %constant_dynamic-slice_fusion.1), channel_id=1, source_target_pairs={{0,8},{1,9},{2,10},{3,11},{4,12},{5,13},{6,14},{7,15},{8,0},{9,1},... | collective-permute-start | bytes 196616 | tf_op jit(solution)/shard_map/ppermute | solution.py:45
  74.9 7.9 %collective-permute-start.23 = (f32[16,512]{1,0:T(8,128)S(1)}, f32[16,512]{1,0:T(8,128)S(1)}, u32[]{:S(2)}, u32[]{:S(2)}) collective-permute-start(f32[16,512]{1,0:T(8,128)S(1)} %constant_dynamic-slice_fusion), channel_id=1, source_target_pairs={{0,20},{1,21},{2,22},{3,23},{4,16},{5,17},{6,18},{7,19},{8,28},{9,... | collective-permute-start | bytes 98312 | tf_op jit(solution)/shard_map/ppermute | solution.py:45
  79.3 15.2 %all-to-all-start.1 = ((f32[8,128,128]{1,2,0:T(8,128)}), f32[8,128,128]{1,2,0:T(8,128)S(1)}, u32[]{:S(2)}, u32[]{:S(2)}) async-start(f32[8,128,128]{1,2,0:T(8,128)} %broadcast_in_dim.4), calls=%async_computation.1 | async-start | bytes 1048576 | tf_op jit(solution)/shard_map/all_to_all | solution.py:176
  82.8 2.9 %collective-permute-start.24 = (f32[16,512]{1,0:T(8,128)S(1)}, f32[16,512]{1,0:T(8,128)S(1)}, u32[]{:S(2)}, u32[]{:S(2)}) collective-permute-start(f32[16,512]{1,0:T(8,128)S(1)} %dynamic-slice_add_fusion.1), channel_id=1, source_target_pairs={{0,32},{1,33},{2,34},{3,35},{4,36},{5,37},{6,38},{7,39},{8,40},{9,... | collective-permute-start | bytes 98312 | tf_op jit(solution)/shard_map/ppermute | solution.py:45
  85.7 4.0 %collective-permute-start.25 = (f32[16,512]{1,0:T(8,128)S(1)}, f32[16,512]{1,0:T(8,128)S(1)}, u32[]{:S(2)}, u32[]{:S(2)}) collective-permute-start(f32[16,512]{1,0:T(8,128)S(1)} %add.33), channel_id=1, source_target_pairs={{0,64},{1,65},{2,66},{3,67},{4,68},{5,69},{6,70},{7,71},{8,72},{9,... | collective-permute-start | bytes 98312 | tf_op jit(solution)/shard_map/ppermute | solution.py:45
  89.7 4.9 %collective-permute-start.26 = (f32[16,512]{1,0:T(8,128)S(1)}, f32[16,512]{1,0:T(8,128)S(1)}, u32[]{:S(2)}, u32[]{:S(2)}) collective-permute-start(f32[16,512]{1,0:T(8,128)S(1)} %add.34), channel_id=1, source_target_pairs={{0,192},{1,193},{2,194},{3,195},{4,196},{5,197},{6,198},{7,199},{8... | collective-permute-start | bytes 98312 | tf_op jit(solution)/shard_map/ppermute | solution.py:45
  95.4 14.2 %all-to-all-start.2 = ((f32[16,16,512]{2,1,0:T(8,128)}), f32[16,16,512]{2,1,0:T(8,128)S(1)}, u32[]{:S(2)}, u32[]{:S(2)}) async-start(f32[16,16,512]{2,1,0:T(8,128)} %broadcast_in_dim.5), calls=%async_computation.2 | async-start | bytes 1048576 | tf_op jit(solution)/shard_map/all_to_all | solution.py:176
  109.7 7.7 %collective-permute-start.27 = (f32[8,32,512]{2,1,0:T(8,128)S(1)}, f32[8,32,512]{2,1,0:T(8,128)S(1)}, u32[]{:S(2)}, u32[]{:S(2)}) collective-permute-start(f32[8,32,512]{2,1,0:T(8,128)S(1)} %bitcast.62), channel_id=1, source_target_pairs={{0,8},{1,9},{2,10},{3,11},{4,12},{5,13},{6,14},{7,15},{8,0},{9,1},... | collective-permute-start | bytes 1572872 | tf_op jit(solution)/shard_map/ppermute | solution.py:45
  (4 other events, 9.3 us)

commit v4 on v3

--- a/solution.py
+++ b/solution.py
@@ -118,8 +118,8 @@
         out[place[2 * q], 0:ROWS] = jnp.where(lane < COLS, a, pltpu.roll(b, COLS, 1))
         out[place[2 * q + 1], 0:ROWS] = jnp.where(lane < COLS, pltpu.roll(a, COLS, 1), b)
     for k in range(8):
-        out[k, ROWS : ROWS + 8] = turned[:, :128]
-        out[k, ROWS + 8 : ROWS + 16] = turned[:, 128:]
+        out[k, ROWS : ROWS + 4] = turned[:4, :128]
+        out[k, ROWS + 4 : ROWS + 8] = turned[:4, 128:]
 
 
 def add_texts(folded, images, arrays, state=None, place=None):
@@ -137,7 +137,7 @@
     if last:
         operands = [place] + operands
         in_specs = [pl.BlockSpec(memory_space=pltpu.SMEM)] + in_specs
-        shapes = [jax.ShapeDtypeStruct((8, ROWS + 16, 128), jnp.float32)]
+        shapes = [jax.ShapeDtypeStruct((8, ROWS + 8, 128), jnp.float32)]
     else:
         shapes = [
             jax.ShapeDtypeStruct((ROWS, 128), jnp.float32),
@@ -170,10 +170,63 @@
     return mine + move(other, pairs)
 
 
-def to_all(piece, axes):
-    count = math.prod(lax.axis_size(axis) for axis in axes)
-    pieces = jnp.broadcast_to(piece[None], (count,) + piece.shape)
-    return lax.all_to_all(pieces, axes, 0, 0, tiled=True)
+def small_call(body, shape, *operands, scalars=0):
+    smem, vmem = pl.BlockSpec(memory_space=pltpu.SMEM), pl.BlockSpec(memory_space=pltpu.VMEM)
+    return pl.pallas_call(
+        body,
+        out_shape=jax.ShapeDtypeStruct(shape, jnp.float32),
+        in_specs=[smem] * scalars + [vmem] * (len(operands) - scalars),
+        out_specs=vmem,
+        compiler_params=pltpu.CompilerParams(vmem_limit_bytes=VMEM_LIMIT),
+        cost_estimate=pl.CostEstimate(flops=1024, bytes_accessed=1024 * 1024, transcendentals=0),
+    )(*operands)
+
+
+def pack(piece, term, received, scale):
+    def body(piece_ref, term_ref, received_ref, out):
+        total = scale * (term_ref[...] + received_ref[...])
+        for k in range(8):
+            out[k, : ROWS // 2] = piece_ref[...]
+            for q in range(4):
+                here = slice(ROWS // 2 + SHARD * q, ROWS // 2 + SHARD * (q + 1))
+                out[k, here] = total[:, 128 * q : 128 * (q + 1)]
+
+    return small_call(body, (8, ROWS, 128), piece, term, received)
+
+
+def unpack_image(where, pieces, head, scale):
+    def body(where_ref, pieces_ref, head_ref, out):
+        lane = lax.broadcasted_iota(jnp.int32, (ROWS // 2, 128), 1)
+        total = jnp.zeros((ROWS, DS), jnp.float32)
+        for half in (0, 1):
+            columns = []
+            for q in (2 * half, 2 * half + 1):
+                a, b = pieces_ref[2 * q, : ROWS // 2], pieces_ref[2 * q + 1, : ROWS // 2]
+                top = jnp.where(lane < COLS, a, pltpu.roll(b, COLS, 1))
+                bottom = jnp.where(lane < COLS, pltpu.roll(a, COLS, 1), b)
+                columns.append(jnp.concatenate([top, bottom], axis=0))
+            gap = jnp.concatenate(columns, axis=1)
+            start = pl.multiple_of((DS // 2) * lax.rem(where_ref[0] + half, 2), DS // 2)
+            total += dot3(split(gap), split(head_ref[pl.ds(start, DS // 2), :]), NN)
+        out[...] = scale * total
+
+    return small_call(body, (ROWS, DS), where, pieces, head, scalars=1)
+
+
+def unpack_head(where, pieces, partner):
+    def body(where_ref, pieces_ref, partner_ref, out):
+        core = where_ref[1]
+        for k in range(8):
+            block = lax.rem(k + 4 * where_ref[0], 8) * COLS
+            mine = pl.multiple_of(block + core * SHARD, SHARD)
+            other = pl.multiple_of(block + (1 - core) * SHARD, SHARD)
+            for q in range(4):
+                lanes = slice(128 * q, 128 * (q + 1))
+                here = slice(ROWS // 2 + SHARD * q, ROWS // 2 + SHARD * (q + 1))
+                out[pl.ds(mine, SHARD), lanes] = pieces_ref[k, here]
+                out[pl.ds(other, SHARD), lanes] = partner_ref[k, SHARD * q : SHARD * (q + 1)]
+
+    return small_call(body, (DS, DS), where, pieces, partner, scalars=1)
 
 
 def shards(image_student, image_teacher, text_features, text_teacher, head):
@@ -203,7 +256,7 @@
     (both,) = add_texts(folded, images, [two, move(two, CORE)], state, place)
 
     got = lax.all_to_all(both, ("xl", "y"), 0, 0, tiled=True)
-    stats = got[:, ROWS:].reshape(8, 2, 8, 128)[:, :, :4]
+    stats = got[:, ROWS:].reshape(8, 2, 4, 128)
     stats = stats.transpose(0, 2, 1, 3).reshape(8, 4, ROWS)
     sums = []
     for k in (0, 2):
@@ -216,27 +269,16 @@
         sums.append(jnp.sum(got[:, :ROWS, lanes] * shares[:, :, None], axis=0))
     gap_text = sums[0] - sums[1]
 
-    term = dot(gap_text, image_student, ((0,), (0,)))
-    term = halved(term, core, CORE)
     piece = jnp.concatenate([gap_text[: ROWS // 2], gap_text[ROWS // 2 :]], axis=1)
-    term, piece = lax.optimization_barrier((term, piece))
-    term = halved(term, xh, X_FLIP)
-    for pairs in Z_FOLD:
+    term = halved(dot(gap_text, image_student, ((0,), (0,))), core, CORE)
+    for pairs in (X_FLIP,) + Z_FOLD[:-1]:
         term = term + move(term, pairs)
-
-    gaps = to_all(piece, ("xl", "y"))
-    gaps = jnp.where(xh == 0, gaps, jnp.concatenate([gaps[4:], gaps[:4]], axis=0))
-    gap_text = gaps.reshape(8, ROWS // 2, 2, COLS).transpose(2, 1, 0, 3).reshape(ROWS, DS)
-    grad_image = scale_s * dot(gap_text, head, NN)
-
-    terms = to_all(term * (scale_s / math.sqrt(batch)), ("xh", "xl", "y"))
-    terms = terms.reshape(2, 2, 4, SHARD // 2, DS)
-    terms = jnp.stack([terms[0], terms[1, ::-1]], axis=2).reshape(8, SHARD, DS)
-    partner = move(terms, CORE)
-    low = jnp.where(core == 0, terms, partner)
-    high = jnp.where(core == 0, partner, terms)
-    grad_head = jnp.stack([low, high], axis=1).reshape(DS, DS)
-    return (grad_image, grad_head)
+    packed = pack(piece, term, move(term, Z_FOLD[-1]), scale_s / math.sqrt(batch))
+
+    pieces = lax.all_to_all(packed, ("xl", "y"), 0, 0, tiled=True)
+    partner = move(pieces[:, ROWS // 2 :], CORE)
+    where = jnp.stack([xh, core]).astype(jnp.int32)
+    return unpack_image(where, pieces, head, scale_s), unpack_head(where, pieces, partner)
 
 
 def solution(mesh):

time: 119 us -> 117 us (0.983)
  blocking collectives: 0 us -> 13.2 us
  starting transfers between devices: 57.7 us -> 48.6 us
  waiting for transfers between devices: 35.9 us -> 31.1 us
  Pallas kernels: 14.8 us -> 18.5 us
  local copies, waits for them, and re-layouts: 3.16 us -> 0.89 us
  matrix products: 3.37 us -> 2.12 us
  other arithmetic: 2.58 us -> 1.39 us
    all_to_all x0 -> x1, blocking collectives: none -> 13.2 us  [shards(): pieces = lax.all_to_all(packed, ('xl', 'y'), 0, 0, tiled=True)]
    all_to_all x2 -> x0, waiting for transfers between devices: 9 us -> none  [to_all(): return lax.all_to_all(pieces, axes, 0, 0, tiled=True)]
    all_to_all x2 -> x0, starting transfers between devices: 8.66 us -> none  [to_all(): return lax.all_to_all(pieces, axes, 0, 0, tiled=True)]
    ppermute x28, waiting for transfers between devices: 11.2 us -> 15.7 us  [move(): return lax.ppermute(array, AXES, pairs)]
    pallas_call x0 -> x3, Pallas kernels: none -> 3.66 us  [small_call(): pl.pallas_call(body, out_shape=jax.ShapeDtypeStruct(shape, jnp.float32),...]
    broadcast_in_dim x2 -> x0, local copies, waits for them, and re-layouts: 1.69 us -> none  [to_all(): pieces = jnp.broadcast_to(piece[None], (count,) + piece.shape)]
    dot_general x3 -> x2, matrix products: 3.37 us -> 2.12 us  [dot(): lax.dot_general(a, b, (dims, ((), ())), precision=HIGH, preferred_element...]
  transfers between devices with their start and end apart: 31 -> 29, of which waited for: 9 -> 9; matrix products, arithmetic and copies ran while one was open for 4% -> 2% of each run, Pallas kernels for 10% -> 12%
where the time goes in v4:
time: 117 us
  starting transfers between devices  48.6 us (42%)
  waiting for transfers between devices  31.1 us (27%)
  Pallas kernels  18.5 us (16%)
  blocking collectives  13.2 us (11%)
  matrix products  2.12 us (2%)
  other arithmetic  1.39 us (1%)
    ppermute x28, starting transfers between devices, move(): return lax.ppermute(array, AXES, pairs)  44.4 us
    ppermute x28, waiting for transfers between devices, move(): return lax.ppermute(array, AXES, pairs)  15.7 us
    all_to_all x1, waiting for transfers between devices, shards(): got = lax.all_to_all(both, ('xl', 'y'), 0, 0, tiled=True)  15.4 us
    pallas_call x9, Pallas kernels, add_texts(): pl.pallas_call(body, out_shape=shapes, in_specs=in_specs, out_specs=[vmem...  14.8 us
    all_to_all x1, blocking collectives, shards(): pieces = lax.all_to_all(packed, ('xl', 'y'), 0, 0, tiled=True)  13.2 us
    all_to_all x1, starting transfers between devices, shards(): got = lax.all_to_all(both, ('xl', 'y'), 0, 0, tiled=True)  4.19 us
    pallas_call x3, Pallas kernels, small_call(): pl.pallas_call(body, out_shape=jax.ShapeDtypeStruct(shape, jnp.float32),...  3.66 us
  transfers between devices with their start and end apart: 29, of which 9 were waited for; matrix products, arithmetic and copies ran while one was open for 2% of the time, Pallas kernels for 12%

profile of v4, /device:TPU:1, one launch (start us, length us, event | category | flops | bytes accessed | tf_op | source)
XLA Modules:
  0.0 116.7 jit_solution(9041256516356360233)
XLA Ops:
  0.7 3.3 %collective-permute-start.2 = (f32[32,768]{1,0:T(8,128)}, f32[32,768]{1,0:T(8,128)S(1)}, u32[]{:S(2)}, u32[]{:S(2)}) collective-permute-start(f32[32,768]{1,0:T(8,128)} %param.8), channel_id=1, source_target_pairs={{0,8},{1,9},{2,10},{3,11},{4,12},{5,13},{6,14},{7,15},{8,0},{9,1},... | collective-permute-start | bytes 294920 | tf_op jit(solution)/shard_map/ppermute | solution.py:45
  5.1 1.9 %collective-permute-start.1 = (f32[32,512]{1,0:T(8,128)}, f32[32,512]{1,0:T(8,128)S(1)}, u32[]{:S(2)}, u32[]{:S(2)}) collective-permute-start(f32[32,512]{1,0:T(8,128)} %param.7), channel_id=1, source_target_pairs={{0,20},{1,21},{2,22},{3,23},{4,16},{5,17},{6,18},{7,19},{8,28},{9,... | collective-permute-start | bytes 196616 | tf_op jit(solution)/shard_map/ppermute | solution.py:45
  7.0 1.8 %convolution_multiply_fusion.refs_0_.refs_1_ = f32[256,512]{1,0:T(8,128)S(1)} fusion(f32[256,512]{1,0:T(8,128)S(1)} %copy-done, f32[512,512]{1,0:T(8,128)} %head_ref.1), kind=kOutput, calls=%fused_computation | convolution fusion | flops 402784256 | bytes 2097152 | tf_op jit(solution)/shard_map/dot_general | solution.py:49
  9.8 3.9 %collective-permute-start.11 = (f32[64,1280]{1,0:T(8,128)S(1)}, f32[64,1280]{1,0:T(8,128)S(1)}, u32[]{:S(2)}, u32[]{:S(2)}) collective-permute-start(f32[64,1280]{1,0:T(8,128)S(1)} %maximum_maximum_fusion.refs_2_), channel_id=1, source_target_pairs={{0,32},{1,33},{2,34},{3,35},{4,36},{5,37},{6,38},{7,39},{8,232},{9... | collective-permute-start | bytes 983048 | tf_op jit(solution)/shard_map/ppermute | solution.py:45
  15.2 2.8 %collective-permute-start.6 = (f32[64,1280]{1,0:T(8,128)S(1)}, f32[64,1280]{1,0:T(8,128)S(1)}, u32[]{:S(2)}, u32[]{:S(2)}) collective-permute-start(f32[64,1280]{1,0:T(8,128)S(1)} %maximum_maximum_fusion.1.refs_3_), channel_id=1, source_target_pairs={{0,32},{1,33},{2,34},{3,35},{4,36},{5,37},{6,38},{7,39},{8,232},{9... | collective-permute-start | bytes 983048 | tf_op jit(solution)/shard_map/ppermute | solution.py:45
  18.0 1.5 %collective-permute-start.18 = (f32[64,1280]{1,0:T(8,128)S(1)}, f32[64,1280]{1,0:T(8,128)S(1)}, u32[]{:S(2)}, u32[]{:S(2)}) collective-permute-start(f32[64,1280]{1,0:T(8,128)S(1)} %collective-permute-done.11.refs_2_), channel_id=1, source_target_pairs={{0,8},{1,9},{2,10},{3,11},{4,12},{5,13},{6,14},{7,15},{8,0},{9,1},... | collective-permute-start | bytes 983048 | tf_op jit(solution)/shard_map/ppermute | solution.py:45
  19.5 1.7 %collective-permute-start.12 = (f32[64,1280]{1,0:T(8,128)S(1)}, f32[64,1280]{1,0:T(8,128)S(1)}, u32[]{:S(2)}, u32[]{:S(2)}) collective-permute-start(f32[64,1280]{1,0:T(8,128)S(1)} %collective-permute-done.11.refs_2_), channel_id=1, source_target_pairs={{0,32},{1,33},{2,34},{3,35},{4,36},{5,37},{6,38},{7,39},{8,232},{9... | collective-permute-start | bytes 983048 | tf_op jit(solution)/shard_map/ppermute | solution.py:45
  22.6 1.3 %collective-permute-start.17 = (f32[64,1280]{1,0:T(8,128)S(1)}, f32[64,1280]{1,0:T(8,128)S(1)}, u32[]{:S(2)}, u32[]{:S(2)}) collective-permute-start(f32[64,1280]{1,0:T(8,128)S(1)} %collective-permute-done.6.refs_2_), channel_id=1, source_target_pairs={{0,8},{1,9},{2,10},{3,11},{4,12},{5,13},{6,14},{7,15},{8,0},{9,1},... | collective-permute-start | bytes 983048 | tf_op jit(solution)/shard_map/ppermute | solution.py:45
  25.7 2.1 %collective-permute-start.16 = (f32[64,1280]{1,0:T(8,128)S(1)}, f32[64,1280]{1,0:T(8,128)S(1)}, u32[]{:S(2)}, u32[]{:S(2)}) collective-permute-start(f32[64,1280]{1,0:T(8,128)S(1)} %collective-permute-done.12.refs_2_), channel_id=1, source_target_pairs={{0,8},{1,9},{2,10},{3,11},{4,12},{5,13},{6,14},{7,15},{8,0},{9,1},... | collective-permute-start | bytes 983048 | tf_op jit(solution)/shard_map/ppermute | solution.py:45
  28.7 1.5 %add_texts.10 = (f32[256,128]{1,0:T(8,128)S(1)}, f32[256,512]{1,0:T(8,128)S(1)}, f32[256,512]{1,0:T(8,128)S(1)}) custom-call(f32[256,512]{1,0:T(8,128)S(1)} %convolution_multiply_fusion.refs_0_.refs_1_, f32[256,768]{1,0:T(8,128)S(1)} %broadcast_multiply_fusion.refs_1_.refs_2_, f32[64,1280]{1,0:T(8,128)S(1)} %collective-permute-done.11.refs_2_, ...), custom_call_target="tpu_custom_call" | custom-call | flops 18119393280 | bytes 4194304 | tf_op jit(solution)/shard_map/add_texts/pallas_call | solution.py:152
  30.2 2.0 %collective-permute-start.15 = (f32[64,1280]{1,0:T(8,128)S(1)}, f32[64,1280]{1,0:T(8,128)S(1)}, u32[]{:S(2)}, u32[]{:S(2)}) collective-permute-start(f32[64,1280]{1,0:T(8,128)S(1)} %collective-permute-done.7.refs_2_), channel_id=1, source_target_pairs={{0,8},{1,9},{2,10},{3,11},{4,12},{5,13},{6,14},{7,15},{8,0},{9,1},... | collective-permute-start | bytes 983048 | tf_op jit(solution)/shard_map/ppermute | solution.py:45
  32.7 1.5 %add_texts.11 = (f32[256,128]{1,0:T(8,128)S(1)}, f32[256,512]{1,0:T(8,128)S(1)}, f32[256,512]{1,0:T(8,128)S(1)}) custom-call(f32[256,512]{1,0:T(8,128)S(1)} %convolution_multiply_fusion.refs_0_.refs_1_, f32[256,768]{1,0:T(8,128)S(1)} %broadcast_multiply_fusion.refs_1_.refs_2_, f32[64,1280]{1,0:T(8,128)S(1)} %collective-permute-done.6.refs_2_, ...), custom_call_target="tpu_custom_call" | custom-call | flops 18119393280 | bytes 4194304 | tf_op jit(solution)/shard_map/add_texts/pallas_call | solution.py:152
  34.2 1.7 %collective-permute-start.20 = (f32[32,1280]{1,0:T(8,128)S(1)}, f32[32,1280]{1,0:T(8,128)S(1)}, u32[]{:S(2)}, u32[]{:S(2)}) collective-permute-start(f32[32,1280]{1,0:T(8,128)S(1)} %slice.49), channel_id=1, source_target_pairs={{0,32},{1,33},{2,34},{3,35},{4,36},{5,37},{6,38},{7,39},{8,232},{9... | collective-permute-start | bytes 491528 | tf_op jit(solution)/shard_map/ppermute | solution.py:45
  36.3 1.5 %add_texts.12 = (f32[256,128]{1,0:T(8,128)S(1)}, f32[256,512]{1,0:T(8,128)S(1)}, f32[256,512]{1,0:T(8,128)S(1)}) custom-call(f32[256,512]{1,0:T(8,128)S(1)} %convolution_multiply_fusion.refs_0_.refs_1_, f32[256,768]{1,0:T(8,128)S(1)} %broadcast_multiply_fusion.refs_1_.refs_2_, f32[64,1280]{1,0:T(8,128)S(1)} %collective-permute-done.12.refs_2_, ...), custom_call_target="tpu_custom_call" | custom-call | flops 18119393280 | bytes 4194304 | tf_op jit(solution)/shard_map/add_texts/pallas_call | solution.py:152
  38.4 2.3 %collective-permute-start.9 = (f32[32,1280]{1,0:T(8,128)S(1)}, f32[32,1280]{1,0:T(8,128)S(1)}, u32[]{:S(2)}, u32[]{:S(2)}) collective-permute-start(f32[32,1280]{1,0:T(8,128)S(1)} %slice.48), channel_id=1, source_target_pairs={{0,32},{1,33},{2,34},{3,35},{4,36},{5,37},{6,38},{7,39},{8,232},{9... | collective-permute-start | bytes 491528 | tf_op jit(solution)/shard_map/ppermute | solution.py:45
  40.7 1.5 %add_texts.13 = (f32[256,128]{1,0:T(8,128)S(1)}, f32[256,512]{1,0:T(8,128)S(1)}, f32[256,512]{1,0:T(8,128)S(1)}) custom-call(f32[256,512]{1,0:T(8,128)S(1)} %convolution_multiply_fusion.refs_0_.refs_1_, f32[256,768]{1,0:T(8,128)S(1)} %broadcast_multiply_fusion.refs_1_.refs_2_, f32[64,1280]{1,0:T(8,128)S(1)} %collective-permute-done.7.refs_2_, ...), custom_call_target="tpu_custom_call" | custom-call | flops 18119393280 | bytes 4194304 | tf_op jit(solution)/shard_map/add_texts/pallas_call | solution.py:152
  42.8 1.5 %add_texts.14 = (f32[256,128]{1,0:T(8,128)S(1)}, f32[256,512]{1,0:T(8,128)S(1)}, f32[256,512]{1,0:T(8,128)S(1)}) custom-call(f32[256,512]{1,0:T(8,128)S(1)} %convolution_multiply_fusion.refs_0_.refs_1_, f32[256,768]{1,0:T(8,128)S(1)} %broadcast_multiply_fusion.refs_1_.refs_2_, f32[64,1280]{1,0:T(8,128)S(1)} %collective-permute-done.13.refs_2_, ...), custom_call_target="tpu_custom_call" | custom-call | flops 18119393280 | bytes 4194304 | tf_op jit(solution)/shard_map/add_texts/pallas_call | solution.py:152
  44.3 1.5 %add_texts.15 = (f32[256,128]{1,0:T(8,128)S(1)}, f32[256,512]{1,0:T(8,128)S(1)}, f32[256,512]{1,0:T(8,128)S(1)}) custom-call(f32[256,512]{1,0:T(8,128)S(1)} %convolution_multiply_fusion.refs_0_.refs_1_, f32[256,768]{1,0:T(8,128)S(1)} %broadcast_multiply_fusion.refs_1_.refs_2_, f32[64,1280]{1,0:T(8,128)S(1)} %collective-permute-done.8.refs_2_, ...), custom_call_target="tpu_custom_call" | custom-call | flops 18119393280 | bytes 4194304 | tf_op jit(solution)/shard_map/add_texts/pallas_call | solution.py:152
  47.1 1.5 %add_texts.16 = (f32[256,128]{1,0:T(8,128)S(1)}, f32[256,512]{1,0:T(8,128)S(1)}, f32[256,512]{1,0:T(8,128)S(1)}) custom-call(f32[256,512]{1,0:T(8,128)S(1)} %convolution_multiply_fusion.refs_0_.refs_1_, f32[256,768]{1,0:T(8,128)S(1)} %broadcast_multiply_fusion.refs_1_.refs_2_, f32[32,1280]{1,0:T(8,128)S(1)} %collective-permute-done.20.refs_2_, ...), custom_call_target="tpu_custom_call" | custom-call | flops 9059696640 | bytes 4194304 | tf_op jit(solution)/shard_map/add_texts/pallas_call | solution.py:152
  48.6 3.3 %add_texts.17 = f32[8,264,128]{2,1,0:T(8,128)} custom-call(s32[8]{0:T(128)S(1)} %iota_xor_fusion.refs_0_, f32[256,512]{1,0:T(8,128)S(1)} %convolution_multiply_fusion.refs_0_.refs_1_, f32[256,768]{1,0:T(8,128)S(1)} %broadcast_multiply_fusion.refs_1_.refs_2_, f32[32,1280]{1,0:T(8,128)S(1)} %collective-permute-done.9.refs_3_, ...), custom_call_target="tpu_custom_call" | custom-call | flops 9059696640 | bytes 4194304 | tf_op jit(solution)/shard_map/add_texts/pallas_call | solution.py:152
  51.9 4.2 %all-to-all-start = ((f32[8,264,128]{2,1,0:T(8,128)}), f32[8,264,128]{2,1,0:T(8,128)S(1)}, u32[]{:S(2)}, u32[]{:S(2)}) async-start(f32[8,264,128]{2,1,0:T(8,128)} %add_texts.17), calls=%async_computation | async-start | bytes 2162688 | tf_op jit(solution)/shard_map/all_to_all | solution.py:258
  56.1 15.4 %all-to-all-done = f32[8,264,128]{2,1,0:T(8,128)S(1)} async-done(((f32[8,264,128]{2,1,0:T(8,128)}), f32[8,264,128]{2,1,0:T(8,128)S(1)}, u32[]{:S(2)}, u32[]{:S(2)}) %all-to-all-start) | async-done | bytes 1081376 | tf_op jit(solution)/shard_map/all_to_all | solution.py:258
  74.6 3.5 %collective-permute-start.23 = (f32[32,512]{1,0:T(8,128)S(1)}, f32[32,512]{1,0:T(8,128)S(1)}, u32[]{:S(2)}, u32[]{:S(2)}) collective-permute-start(f32[32,512]{1,0:T(8,128)S(1)} %dynamic-slice_add_fusion), channel_id=1, source_target_pairs={{0,20},{1,21},{2,22},{3,23},{4,16},{5,17},{6,18},{7,19},{8,28},{9,... | collective-permute-start | bytes 196616 | tf_op jit(solution)/shard_map/ppermute | solution.py:45
  78.1 2.2 %collective-permute-done.23 = f32[32,512]{1,0:T(8,128)S(1)} collective-permute-done((f32[32,512]{1,0:T(8,128)S(1)}, f32[32,512]{1,0:T(8,128)S(1)}, u32[]{:S(2)}, u32[]{:S(2)}) %collective-permute-start.23) | collective-permute-done | bytes 65568 | tf_op jit(solution)/shard_map/ppermute | solution.py:45
  80.4 3.1 %collective-permute-done.24 = f32[32,512]{1,0:T(8,128)S(1)} collective-permute-done((f32[32,512]{1,0:T(8,128)S(1)}, f32[32,512]{1,0:T(8,128)S(1)}, u32[]{:S(2)}, u32[]{:S(2)}) %collective-permute-start.24) | collective-permute-done | bytes 65568 | tf_op jit(solution)/shard_map/ppermute | solution.py:45
  83.5 1.7 %collective-permute-start.25 = (f32[32,512]{1,0:T(8,128)S(1)}, f32[32,512]{1,0:T(8,128)S(1)}, u32[]{:S(2)}, u32[]{:S(2)}) collective-permute-start(f32[32,512]{1,0:T(8,128)S(1)} %add.22), channel_id=1, source_target_pairs={{0,64},{1,65},{2,66},{3,67},{4,68},{5,69},{6,70},{7,71},{8,72},{9,... | collective-permute-start | bytes 196616 | tf_op jit(solution)/shard_map/ppermute | solution.py:45
  85.2 3.1 %collective-permute-done.25 = f32[32,512]{1,0:T(8,128)S(1)} collective-permute-done((f32[32,512]{1,0:T(8,128)S(1)}, f32[32,512]{1,0:T(8,128)S(1)}, u32[]{:S(2)}, u32[]{:S(2)}) %collective-permute-start.25) | collective-permute-done | bytes 65568 | tf_op jit(solution)/shard_map/ppermute | solution.py:45
  89.3 4.3 %collective-permute-done.26.received_ref = f32[32,512]{1,0:T(8,128)S(1)} collective-permute-done((f32[32,512]{1,0:T(8,128)S(1)}, f32[32,512]{1,0:T(8,128)S(1)}, u32[]{:S(2)}, u32[]{:S(2)}) %collective-permute-start.26) | collective-permute-done | bytes 65568 | tf_op jit(solution)/shard_map/ppermute | solution.py:45
  93.7 13.2 %all_to_all.10.pieces_ref = f32[8,256,128]{2,1,0:T(8,128)S(1)} all-to-all(f32[8,256,128]{2,1,0:T(8,128)S(1)} %shard_map.68), channel_id=1, replica_groups=mesh['z'=8,'xh'=2,'core'=2,'xl'=2,'y'=4] {'xl','y'}, dimensions={0} | all-to-all | bytes 2097152 | tf_op jit(solution)/shard_map/all_to_all | solution.py:278
  106.9 6.1 %collective-permute-start.27 = (f32[8,128,128]{2,1,0:T(8,128)S(1)}, f32[8,128,128]{2,1,0:T(8,128)S(1)}, u32[]{:S(2)}, u32[]{:S(2)}) collective-permute-start(f32[8,128,128]{2,1,0:T(8,128)S(1)} %slice.59), channel_id=1, source_target_pairs={{0,8},{1,9},{2,10},{3,11},{4,12},{5,13},{6,14},{7,15},{8,0},{9,1},... | collective-permute-start | bytes 1572872 | tf_op jit(solution)/shard_map/ppermute | solution.py:45
  113.1 2.0 %shard_map.69 = f32[256,512]{1,0:T(8,128)} custom-call(s32[2]{0:T(128)S(1)} %pad_add_fusion.where_ref, f32[8,256,128]{2,1,0:T(8,128)S(1)} %all_to_all.10.pieces_ref, f32[512,512]{1,0:T(8,128)S(1)} %copy-done.1), custom_call_target="tpu_custom_call" | custom-call | flops 1024 | bytes 1048576 | tf_op jit(solution)/shard_map/pallas_call | solution.py:175
  115.1 1.6 %shard_map.70 = f32[512,512]{1,0:T(8,128)} custom-call(s32[2]{0:T(128)S(1)} %pad_add_fusion.where_ref, f32[8,256,128]{2,1,0:T(8,128)S(1)} %all_to_all.10.pieces_ref, f32[8,128,128]{2,1,0:T(8,128)S(1)} %collective-permute-done.27.partner_ref), custom_call_target="tpu_custom_call" | custom-call | flops 1024 | bytes 1048576 | tf_op jit(solution)/shard_map/pallas_call | solution.py:175
  (73 shorter events, 15.4 us)
Async XLA Ops:
  0.6 6.4 %copy-start = (f32[256,512]{1,0:T(8,128)S(1)}, f32[256,512]{1,0:T(8,128)}, u32[]{:S(2)}) copy-start(f32[256,512]{1,0:T(8,128)} %param.5) | copy-start | bytes 1572868
  0.6 8.2 %copy-start.2 = (f32[256,768]{1,0:T(8,128)S(1)}, f32[256,768]{1,0:T(8,128)}, u32[]{:S(2)}) copy-start(f32[256,768]{1,0:T(8,128)} %param.6) | copy-start | bytes 2359300
  0.7 8.4 %collective-permute-start.2 = (f32[32,768]{1,0:T(8,128)}, f32[32,768]{1,0:T(8,128)S(1)}, u32[]{:S(2)}, u32[]{:S(2)}) collective-permute-start(f32[32,768]{1,0:T(8,128)} %param.8), channel_id=1, source_target_pairs={{0,8},{1,9},{2,10},{3,11},{4,12},{5,13},{6,14},{7,15},{8,0},{9,1},... | collective-permute-start | bytes 294920 | tf_op jit(solution)/shard_map/ppermute | solution.py:45
  4.0 9.8 %collective-permute-start = (f32[32,768]{1,0:T(8,128)}, f32[32,768]{1,0:T(8,128)S(1)}, u32[]{:S(2)}, u32[]{:S(2)}) collective-permute-start(f32[32,768]{1,0:T(8,128)} %param.8), channel_id=1, source_target_pairs={{0,20},{1,21},{2,22},{3,23},{4,16},{5,17},{6,18},{7,19},{8,28},{9,... | collective-permute-start | bytes 294920 | tf_op jit(solution)/shard_map/ppermute | solution.py:45
  4.7 4.3 %collective-permute-start.3 = (f32[32,512]{1,0:T(8,128)}, f32[32,512]{1,0:T(8,128)S(1)}, u32[]{:S(2)}, u32[]{:S(2)}) collective-permute-start(f32[32,512]{1,0:T(8,128)} %param.7), channel_id=1, source_target_pairs={{0,8},{1,9},{2,10},{3,11},{4,12},{5,13},{6,14},{7,15},{8,0},{9,1},... | collective-permute-start | bytes 196616 | tf_op jit(solution)/shard_map/ppermute | solution.py:45
  5.1 8.6 %collective-permute-start.1 = (f32[32,512]{1,0:T(8,128)}, f32[32,512]{1,0:T(8,128)S(1)}, u32[]{:S(2)}, u32[]{:S(2)}) collective-permute-start(f32[32,512]{1,0:T(8,128)} %param.7), channel_id=1, source_target_pairs={{0,20},{1,21},{2,22},{3,23},{4,16},{5,17},{6,18},{7,19},{8,28},{9,... | collective-permute-start | bytes 196616 | tf_op jit(solution)/shard_map/ppermute | solution.py:45
  9.8 8.2 %collective-permute-start.11 = (f32[64,1280]{1,0:T(8,128)S(1)}, f32[64,1280]{1,0:T(8,128)S(1)}, u32[]{:S(2)}, u32[]{:S(2)}) collective-permute-start(f32[64,1280]{1,0:T(8,128)S(1)} %maximum_maximum_fusion.refs_2_), channel_id=1, source_target_pairs={{0,32},{1,33},{2,34},{3,35},{4,36},{5,37},{6,38},{7,39},{8,232},{9... | collective-permute-start | bytes 983048 | tf_op jit(solution)/shard_map/ppermute | solution.py:45
  13.7 1.4 %collective-permute-start.4 = (f32[32,768]{1,0:T(8,128)S(1)}, f32[32,768]{1,0:T(8,128)S(1)}, u32[]{:S(2)}, u32[]{:S(2)}) collective-permute-start(f32[32,768]{1,0:T(8,128)S(1)} %collective-permute-done), channel_id=1, source_target_pairs={{0,8},{1,9},{2,10},{3,11},{4,12},{5,13},{6,14},{7,15},{8,0},{9,1},... | collective-permute-start | bytes 294920 | tf_op jit(solution)/shard_map/ppermute | solution.py:45
  13.8 1.4 %collective-permute-start.5 = (f32[32,512]{1,0:T(8,128)S(1)}, f32[32,512]{1,0:T(8,128)S(1)}, u32[]{:S(2)}, u32[]{:S(2)}) collective-permute-start(f32[32,512]{1,0:T(8,128)S(1)} %collective-permute-done.1), channel_id=1, source_target_pairs={{0,8},{1,9},{2,10},{3,11},{4,12},{5,13},{6,14},{7,15},{8,0},{9,1},... | collective-permute-start | bytes 196616 | tf_op jit(solution)/shard_map/ppermute | solution.py:45
  15.2 7.4 %collective-permute-start.6 = (f32[64,1280]{1,0:T(8,128)S(1)}, f32[64,1280]{1,0:T(8,128)S(1)}, u32[]{:S(2)}, u32[]{:S(2)}) collective-permute-start(f32[64,1280]{1,0:T(8,128)S(1)} %maximum_maximum_fusion.1.refs_3_), channel_id=1, source_target_pairs={{0,32},{1,33},{2,34},{3,35},{4,36},{5,37},{6,38},{7,39},{8,232},{9... | collective-permute-start | bytes 983048 | tf_op jit(solution)/shard_map/ppermute | solution.py:45
  18.0 10.7 %collective-permute-start.18 = (f32[64,1280]{1,0:T(8,128)S(1)}, f32[64,1280]{1,0:T(8,128)S(1)}, u32[]{:S(2)}, u32[]{:S(2)}) collective-permute-start(f32[64,1280]{1,0:T(8,128)S(1)} %collective-permute-done.11.refs_2_), channel_id=1, source_target_pairs={{0,8},{1,9},{2,10},{3,11},{4,12},{5,13},{6,14},{7,15},{8,0},{9,1},... | collective-permute-start | bytes 983048 | tf_op jit(solution)/shard_map/ppermute | solution.py:45
  19.5 6.2 %collective-permute-start.12 = (f32[64,1280]{1,0:T(8,128)S(1)}, f32[64,1280]{1,0:T(8,128)S(1)}, u32[]{:S(2)}, u32[]{:S(2)}) collective-permute-start(f32[64,1280]{1,0:T(8,128)S(1)} %collective-permute-done.11.refs_2_), channel_id=1, source_target_pairs={{0,32},{1,33},{2,34},{3,35},{4,36},{5,37},{6,38},{7,39},{8,232},{9... | collective-permute-start | bytes 983048 | tf_op jit(solution)/shard_map/ppermute | solution.py:45
  22.6 10.1 %collective-permute-start.17 = (f32[64,1280]{1,0:T(8,128)S(1)}, f32[64,1280]{1,0:T(8,128)S(1)}, u32[]{:S(2)}, u32[]{:S(2)}) collective-permute-start(f32[64,1280]{1,0:T(8,128)S(1)} %collective-permute-done.6.refs_2_), channel_id=1, source_target_pairs={{0,8},{1,9},{2,10},{3,11},{4,12},{5,13},{6,14},{7,15},{8,0},{9,1},... | collective-permute-start | bytes 983048 | tf_op jit(solution)/shard_map/ppermute | solution.py:45
  23.9 6.3 %collective-permute-start.7 = (f32[64,1280]{1,0:T(8,128)S(1)}, f32[64,1280]{1,0:T(8,128)S(1)}, u32[]{:S(2)}, u32[]{:S(2)}) collective-permute-start(f32[64,1280]{1,0:T(8,128)S(1)} %collective-permute-done.6.refs_2_), channel_id=1, source_target_pairs={{0,32},{1,33},{2,34},{3,35},{4,36},{5,37},{6,38},{7,39},{8,232},{9... | collective-permute-start | bytes 983048 | tf_op jit(solution)/shard_map/ppermute | solution.py:45
  25.7 10.6 %collective-permute-start.16 = (f32[64,1280]{1,0:T(8,128)S(1)}, f32[64,1280]{1,0:T(8,128)S(1)}, u32[]{:S(2)}, u32[]{:S(2)}) collective-permute-start(f32[64,1280]{1,0:T(8,128)S(1)} %collective-permute-done.12.refs_2_), channel_id=1, source_target_pairs={{0,8},{1,9},{2,10},{3,11},{4,12},{5,13},{6,14},{7,15},{8,0},{9,1},... | collective-permute-start | bytes 983048 | tf_op jit(solution)/shard_map/ppermute | solution.py:45
  27.8 6.4 %collective-permute-start.13 = (f32[64,1280]{1,0:T(8,128)S(1)}, f32[64,1280]{1,0:T(8,128)S(1)}, u32[]{:S(2)}, u32[]{:S(2)}) collective-permute-start(f32[64,1280]{1,0:T(8,128)S(1)} %collective-permute-done.12.refs_2_), channel_id=1, source_target_pairs={{0,32},{1,33},{2,34},{3,35},{4,36},{5,37},{6,38},{7,39},{8,232},{9... | collective-permute-start | bytes 983048 | tf_op jit(solution)/shard_map/ppermute | solution.py:45
  30.2 10.5 %collective-permute-start.15 = (f32[64,1280]{1,0:T(8,128)S(1)}, f32[64,1280]{1,0:T(8,128)S(1)}, u32[]{:S(2)}, u32[]{:S(2)}) collective-permute-start(f32[64,1280]{1,0:T(8,128)S(1)} %collective-permute-done.7.refs_2_), channel_id=1, source_target_pairs={{0,8},{1,9},{2,10},{3,11},{4,12},{5,13},{6,14},{7,15},{8,0},{9,1},... | collective-permute-start | bytes 983048 | tf_op jit(solution)/shard_map/ppermute | solution.py:45
  32.2 6.2 %collective-permute-start.8 = (f32[64,1280]{1,0:T(8,128)S(1)}, f32[64,1280]{1,0:T(8,128)S(1)}, u32[]{:S(2)}, u32[]{:S(2)}) collective-permute-start(f32[64,1280]{1,0:T(8,128)S(1)} %collective-permute-done.7.refs_2_), channel_id=1, source_target_pairs={{0,32},{1,33},{2,34},{3,35},{4,36},{5,37},{6,38},{7,39},{8,232},{9... | collective-permute-start | bytes 983048 | tf_op jit(solution)/shard_map/ppermute | solution.py:45
  34.2 8.0 %collective-permute-start.20 = (f32[32,1280]{1,0:T(8,128)S(1)}, f32[32,1280]{1,0:T(8,128)S(1)}, u32[]{:S(2)}, u32[]{:S(2)}) collective-permute-start(f32[32,1280]{1,0:T(8,128)S(1)} %slice.49), channel_id=1, source_target_pairs={{0,32},{1,33},{2,34},{3,35},{4,36},{5,37},{6,38},{7,39},{8,232},{9... | collective-permute-start | bytes 491528 | tf_op jit(solution)/shard_map/ppermute | solution.py:45
  36.0 6.9 %collective-permute-start.14 = (f32[64,1280]{1,0:T(8,128)S(1)}, f32[64,1280]{1,0:T(8,128)S(1)}, u32[]{:S(2)}, u32[]{:S(2)}) collective-permute-start(f32[64,1280]{1,0:T(8,128)S(1)} %collective-permute-done.13.refs_2_), channel_id=1, source_target_pairs={{0,8},{1,9},{2,10},{3,11},{4,12},{5,13},{6,14},{7,15},{8,0},{9,1},... | collective-permute-start | bytes 983048 | tf_op jit(solution)/shard_map/ppermute | solution.py:45
  38.4 7.3 %collective-permute-start.9 = (f32[32,1280]{1,0:T(8,128)S(1)}, f32[32,1280]{1,0:T(8,128)S(1)}, u32[]{:S(2)}, u32[]{:S(2)}) collective-permute-start(f32[32,1280]{1,0:T(8,128)S(1)} %slice.48), channel_id=1, source_target_pairs={{0,32},{1,33},{2,34},{3,35},{4,36},{5,37},{6,38},{7,39},{8,232},{9... | collective-permute-start | bytes 491528 | tf_op jit(solution)/shard_map/ppermute | solution.py:45
  40.7 3.6 %collective-permute-start.10 = (f32[64,1280]{1,0:T(8,128)S(1)}, f32[64,1280]{1,0:T(8,128)S(1)}, u32[]{:S(2)}, u32[]{:S(2)}) collective-permute-start(f32[64,1280]{1,0:T(8,128)S(1)} %collective-permute-done.8.refs_2_), channel_id=1, source_target_pairs={{0,8},{1,9},{2,10},{3,11},{4,12},{5,13},{6,14},{7,15},{8,0},{9,1},... | collective-permute-start | bytes 983048 | tf_op jit(solution)/shard_map/ppermute | solution.py:45
  42.2 4.9 %collective-permute-start.21 = (f32[32,1280]{1,0:T(8,128)S(1)}, f32[32,1280]{1,0:T(8,128)S(1)}, u32[]{:S(2)}, u32[]{:S(2)}) collective-permute-start(f32[32,1280]{1,0:T(8,128)S(1)} %collective-permute-done.20.refs_2_), channel_id=1, source_target_pairs={{0,8},{1,9},{2,10},{3,11},{4,12},{5,13},{6,14},{7,15},{8,0},{9,1},... | collective-permute-start | bytes 491528 | tf_op jit(solution)/shard_map/ppermute | solution.py:45
  45.8 2.8 %collective-permute-start.19 = (f32[32,1280]{1,0:T(8,128)S(1)}, f32[32,1280]{1,0:T(8,128)S(1)}, u32[]{:S(2)}, u32[]{:S(2)}) collective-permute-start(f32[32,1280]{1,0:T(8,128)S(1)} %collective-permute-done.9.refs_3_), channel_id=1, source_target_pairs={{0,8},{1,9},{2,10},{3,11},{4,12},{5,13},{6,14},{7,15},{8,0},{9,1},... | collective-permute-start | bytes 491528 | tf_op jit(solution)/shard_map/ppermute | solution.py:45
  51.9 19.5 %all-to-all-start = ((f32[8,264,128]{2,1,0:T(8,128)}), f32[8,264,128]{2,1,0:T(8,128)S(1)}, u32[]{:S(2)}, u32[]{:S(2)}) async-start(f32[8,264,128]{2,1,0:T(8,128)} %add_texts.17), calls=%async_computation | async-start | bytes 2162688 | tf_op jit(solution)/shard_map/all_to_all | solution.py:258
  72.9 1.7 %collective-permute-start.22 = (f32[32,512]{1,0:T(8,128)S(1)}, f32[32,512]{1,0:T(8,128)S(1)}, u32[]{:S(2)}, u32[]{:S(2)}) collective-permute-start(f32[32,512]{1,0:T(8,128)S(1)} %constant_dynamic-slice_fusion), channel_id=1, source_target_pairs={{0,8},{1,9},{2,10},{3,11},{4,12},{5,13},{6,14},{7,15},{8,0},{9,1},... | collective-permute-start | bytes 196616 | tf_op jit(solution)/shard_map/ppermute | solution.py:45
  74.6 5.6 %collective-permute-start.23 = (f32[32,512]{1,0:T(8,128)S(1)}, f32[32,512]{1,0:T(8,128)S(1)}, u32[]{:S(2)}, u32[]{:S(2)}) collective-permute-start(f32[32,512]{1,0:T(8,128)S(1)} %dynamic-slice_add_fusion), channel_id=1, source_target_pairs={{0,20},{1,21},{2,22},{3,23},{4,16},{5,17},{6,18},{7,19},{8,28},{9,... | collective-permute-start | bytes 196616 | tf_op jit(solution)/shard_map/ppermute | solution.py:45
  80.3 3.2 %collective-permute-start.24 = (f32[32,512]{1,0:T(8,128)S(1)}, f32[32,512]{1,0:T(8,128)S(1)}, u32[]{:S(2)}, u32[]{:S(2)}) collective-permute-start(f32[32,512]{1,0:T(8,128)S(1)} %add.21), channel_id=1, source_target_pairs={{0,32},{1,33},{2,34},{3,35},{4,36},{5,37},{6,38},{7,39},{8,40},{9,... | collective-permute-start | bytes 196616 | tf_op jit(solution)/shard_map/ppermute | solution.py:45
  83.5 4.8 %collective-permute-start.25 = (f32[32,512]{1,0:T(8,128)S(1)}, f32[32,512]{1,0:T(8,128)S(1)}, u32[]{:S(2)}, u32[]{:S(2)}) collective-permute-start(f32[32,512]{1,0:T(8,128)S(1)} %add.22), channel_id=1, source_target_pairs={{0,64},{1,65},{2,66},{3,67},{4,68},{5,69},{6,70},{7,71},{8,72},{9,... | collective-permute-start | bytes 196616 | tf_op jit(solution)/shard_map/ppermute | solution.py:45
  88.3 5.3 %collective-permute-start.26 = (f32[32,512]{1,0:T(8,128)S(1)}, f32[32,512]{1,0:T(8,128)S(1)}, u32[]{:S(2)}, u32[]{:S(2)}) collective-permute-start(f32[32,512]{1,0:T(8,128)S(1)} %add.23.term_ref), channel_id=1, source_target_pairs={{0,192},{1,193},{2,194},{3,195},{4,196},{5,197},{6,198},{7,199},{8... | collective-permute-start | bytes 196616 | tf_op jit(solution)/shard_map/ppermute | solution.py:45
  93.7 19.4 %copy-start.1 = (f32[512,512]{1,0:T(8,128)S(1)}, f32[512,512]{1,0:T(8,128)}, u32[]{:S(2)}) copy-start(f32[512,512]{1,0:T(8,128)} %head_ref.1) | copy-start | bytes 3145732
  106.9 8.1 %collective-permute-start.27 = (f32[8,128,128]{2,1,0:T(8,128)S(1)}, f32[8,128,128]{2,1,0:T(8,128)S(1)}, u32[]{:S(2)}, u32[]{:S(2)}) collective-permute-start(f32[8,128,128]{2,1,0:T(8,128)S(1)} %slice.59), channel_id=1, source_target_pairs={{0,8},{1,9},{2,10},{3,11},{4,12},{5,13},{6,14},{7,15},{8,0},{9,1},... | collective-permute-start | bytes 1572872 | tf_op jit(solution)/shard_map/ppermute | solution.py:45
  (2 other events, 1.8 us)

commit v5 on v4

--- a/solution.py
+++ b/solution.py
@@ -163,10 +163,9 @@
     )(*operands)
 
 
-def halved(array, index, pairs):
-    rows = array.shape[0] // 2
-    mine = lax.dynamic_slice_in_dim(array, index * rows, rows, 0)
-    other = lax.dynamic_slice_in_dim(array, (1 - index) * rows, rows, 0)
+def halved(array, starts, pairs):
+    shape = (array.shape[0] // 2, array.shape[1])
+    mine, other = [lax.dynamic_slice(array, (at, jnp.uint32(0)), shape) for at in starts]
     return mine + move(other, pairs)
 
 
@@ -255,6 +254,8 @@
     place = jnp.arange(8, dtype=jnp.int32) ^ (4 * xh).astype(jnp.int32)
     (both,) = add_texts(folded, images, [two, move(two, CORE)], state, place)
 
+    starts = [(core * SHARD).astype(jnp.uint32), ((1 - core) * SHARD).astype(jnp.uint32)]
+    both, *starts = lax.optimization_barrier((both, *starts))
     got = lax.all_to_all(both, ("xl", "y"), 0, 0, tiled=True)
     stats = got[:, ROWS:].reshape(8, 2, 4, 128)
     stats = stats.transpose(0, 2, 1, 3).reshape(8, 4, ROWS)
@@ -270,7 +271,7 @@
     gap_text = sums[0] - sums[1]
 
     piece = jnp.concatenate([gap_text[: ROWS // 2], gap_text[ROWS // 2 :]], axis=1)
-    term = halved(dot(gap_text, image_student, ((0,), (0,))), core, CORE)
+    term = halved(dot(gap_text, image_student, ((0,), (0,))), starts, CORE)
     for pairs in (X_FLIP,) + Z_FOLD[:-1]:
         term = term + move(term, pairs)
     packed = pack(piece, term, move(term, Z_FOLD[-1]), scale_s / math.sqrt(batch))

time: 117 us -> 116 us (level)
  blocking collectives: 13.2 us -> 33.1 us
  waiting for transfers between devices: 31.1 us -> 13.7 us
  starting transfers between devices: 48.6 us -> 45.8 us
    all_to_all x0 -> x1, blocking collectives: none -> 19.8 us  [shards(): got = lax.all_to_all(both, ('xl', 'y'), 0, 0, tiled=True)]
    all_to_all x1 -> x0, waiting for transfers between devices: 15.4 us -> none  [shards(): got = lax.all_to_all(both, ('xl', 'y'), 0, 0, tiled=True)]
    all_to_all x1 -> x0, starting transfers between devices: 4.19 us -> none  [shards(): got = lax.all_to_all(both, ('xl', 'y'), 0, 0, tiled=True)]
    ppermute x28, waiting for transfers between devices: 15.7 us -> 13.7 us  [move(): return lax.ppermute(array, AXES, pairs)]
    ppermute x28, starting transfers between devices: 44.4 us -> 45.8 us  [move(): return lax.ppermute(array, AXES, pairs)]
  transfers between devices with their start and end apart: 29 -> 28, of which waited for: 9 -> 8; matrix products, arithmetic and copies ran while one was open for 2% -> 2% of each run, Pallas kernels for 12% -> 12%
where the time goes in v5:
time: 116 us
  starting transfers between devices  45.8 us (39%)
  blocking collectives  33.1 us (29%)
  Pallas kernels  17.5 us (15%)
  waiting for transfers between devices  13.7 us (12%)
  matrix products  2.13 us (2%)
  other arithmetic  1.39 us (1%)
    ppermute x28, starting transfers between devices, move(): return lax.ppermute(array, AXES, pairs)  45.8 us
    all_to_all x1, blocking collectives, shards(): got = lax.all_to_all(both, ('xl', 'y'), 0, 0, tiled=True)  19.8 us
    pallas_call x9, Pallas kernels, add_texts(): pl.pallas_call(body, out_shape=shapes, in_specs=in_specs, out_specs=[vmem...  13.8 us
    ppermute x28, waiting for transfers between devices, move(): return lax.ppermute(array, AXES, pairs)  13.7 us
    all_to_all x1, blocking collectives, shards(): pieces = lax.all_to_all(packed, ('xl', 'y'), 0, 0, tiled=True)  13.3 us
    pallas_call x3, Pallas kernels, small_call(): pl.pallas_call(body, out_shape=jax.ShapeDtypeStruct(shape, jnp.float32),...  3.66 us
  transfers between devices with their start and end apart: 28, of which 8 were waited for; matrix products, arithmetic and copies ran while one was open for 2% of the time, Pallas kernels for 12%

profile of v5, /device:TPU:1, one launch (start us, length us, event | category | flops | bytes accessed | tf_op | source)
XLA Modules:
  0.0 115.5 jit_solution(3350770673181479342)
XLA Ops:
  0.7 3.3 %collective-permute-start.2 = (f32[32,768]{1,0:T(8,128)}, f32[32,768]{1,0:T(8,128)S(1)}, u32[]{:S(2)}, u32[]{:S(2)}) collective-permute-start(f32[32,768]{1,0:T(8,128)} %param.8), channel_id=1, source_target_pairs={{0,8},{1,9},{2,10},{3,11},{4,12},{5,13},{6,14},{7,15},{8,0},{9,1},... | collective-permute-start | bytes 294920 | tf_op jit(solution)/shard_map/ppermute | solution.py:45
  5.1 1.9 %collective-permute-start.1 = (f32[32,512]{1,0:T(8,128)}, f32[32,512]{1,0:T(8,128)S(1)}, u32[]{:S(2)}, u32[]{:S(2)}) collective-permute-start(f32[32,512]{1,0:T(8,128)} %param.7), channel_id=1, source_target_pairs={{0,20},{1,21},{2,22},{3,23},{4,16},{5,17},{6,18},{7,19},{8,28},{9,... | collective-permute-start | bytes 196616 | tf_op jit(solution)/shard_map/ppermute | solution.py:45
  7.0 1.8 %convolution_multiply_fusion.refs_0_.refs_1_ = f32[256,512]{1,0:T(8,128)S(1)} fusion(f32[256,512]{1,0:T(8,128)S(1)} %copy-done, f32[512,512]{1,0:T(8,128)} %head_ref.1), kind=kOutput, calls=%fused_computation | convolution fusion | flops 402784256 | bytes 2097152 | tf_op jit(solution)/shard_map/dot_general | solution.py:49
  9.8 3.9 %collective-permute-start.11 = (f32[64,1280]{1,0:T(8,128)S(1)}, f32[64,1280]{1,0:T(8,128)S(1)}, u32[]{:S(2)}, u32[]{:S(2)}) collective-permute-start(f32[64,1280]{1,0:T(8,128)S(1)} %maximum_maximum_fusion.refs_2_), channel_id=1, source_target_pairs={{0,32},{1,33},{2,34},{3,35},{4,36},{5,37},{6,38},{7,39},{8,232},{9... | collective-permute-start | bytes 983048 | tf_op jit(solution)/shard_map/ppermute | solution.py:45
  15.2 2.8 %collective-permute-start.6 = (f32[64,1280]{1,0:T(8,128)S(1)}, f32[64,1280]{1,0:T(8,128)S(1)}, u32[]{:S(2)}, u32[]{:S(2)}) collective-permute-start(f32[64,1280]{1,0:T(8,128)S(1)} %maximum_maximum_fusion.1.refs_3_), channel_id=1, source_target_pairs={{0,32},{1,33},{2,34},{3,35},{4,36},{5,37},{6,38},{7,39},{8,232},{9... | collective-permute-start | bytes 983048 | tf_op jit(solution)/shard_map/ppermute | solution.py:45
  18.0 1.5 %collective-permute-start.18 = (f32[64,1280]{1,0:T(8,128)S(1)}, f32[64,1280]{1,0:T(8,128)S(1)}, u32[]{:S(2)}, u32[]{:S(2)}) collective-permute-start(f32[64,1280]{1,0:T(8,128)S(1)} %collective-permute-done.11.refs_2_), channel_id=1, source_target_pairs={{0,8},{1,9},{2,10},{3,11},{4,12},{5,13},{6,14},{7,15},{8,0},{9,1},... | collective-permute-start | bytes 983048 | tf_op jit(solution)/shard_map/ppermute | solution.py:45
  19.5 1.7 %collective-permute-start.12 = (f32[64,1280]{1,0:T(8,128)S(1)}, f32[64,1280]{1,0:T(8,128)S(1)}, u32[]{:S(2)}, u32[]{:S(2)}) collective-permute-start(f32[64,1280]{1,0:T(8,128)S(1)} %collective-permute-done.11.refs_2_), channel_id=1, source_target_pairs={{0,32},{1,33},{2,34},{3,35},{4,36},{5,37},{6,38},{7,39},{8,232},{9... | collective-permute-start | bytes 983048 | tf_op jit(solution)/shard_map/ppermute | solution.py:45
  25.7 2.1 %collective-permute-start.16 = (f32[64,1280]{1,0:T(8,128)S(1)}, f32[64,1280]{1,0:T(8,128)S(1)}, u32[]{:S(2)}, u32[]{:S(2)}) collective-permute-start(f32[64,1280]{1,0:T(8,128)S(1)} %collective-permute-done.12.refs_2_), channel_id=1, source_target_pairs={{0,8},{1,9},{2,10},{3,11},{4,12},{5,13},{6,14},{7,15},{8,0},{9,1},... | collective-permute-start | bytes 983048 | tf_op jit(solution)/shard_map/ppermute | solution.py:45
  28.7 1.5 %add_texts.10 = (f32[256,128]{1,0:T(8,128)S(1)}, f32[256,512]{1,0:T(8,128)S(1)}, f32[256,512]{1,0:T(8,128)S(1)}) custom-call(f32[256,512]{1,0:T(8,128)S(1)} %convolution_multiply_fusion.refs_0_.refs_1_, f32[256,768]{1,0:T(8,128)S(1)} %broadcast_multiply_fusion.refs_1_.refs_2_, f32[64,1280]{1,0:T(8,128)S(1)} %collective-permute-done.11.refs_2_, ...), custom_call_target="tpu_custom_call" | custom-call | flops 18119393280 | bytes 4194304 | tf_op jit(solution)/shard_map/add_texts/pallas_call | solution.py:152
  30.2 2.0 %collective-permute-start.15 = (f32[64,1280]{1,0:T(8,128)S(1)}, f32[64,1280]{1,0:T(8,128)S(1)}, u32[]{:S(2)}, u32[]{:S(2)}) collective-permute-start(f32[64,1280]{1,0:T(8,128)S(1)} %collective-permute-done.7.refs_2_), channel_id=1, source_target_pairs={{0,8},{1,9},{2,10},{3,11},{4,12},{5,13},{6,14},{7,15},{8,0},{9,1},... | collective-permute-start | bytes 983048 | tf_op jit(solution)/shard_map/ppermute | solution.py:45
  32.7 1.5 %add_texts.11 = (f32[256,128]{1,0:T(8,128)S(1)}, f32[256,512]{1,0:T(8,128)S(1)}, f32[256,512]{1,0:T(8,128)S(1)}) custom-call(f32[256,512]{1,0:T(8,128)S(1)} %convolution_multiply_fusion.refs_0_.refs_1_, f32[256,768]{1,0:T(8,128)S(1)} %broadcast_multiply_fusion.refs_1_.refs_2_, f32[64,1280]{1,0:T(8,128)S(1)} %collective-permute-done.6.refs_2_, ...), custom_call_target="tpu_custom_call" | custom-call | flops 18119393280 | bytes 4194304 | tf_op jit(solution)/shard_map/add_texts/pallas_call | solution.py:152
  34.2 1.7 %collective-permute-start.20 = (f32[32,1280]{1,0:T(8,128)S(1)}, f32[32,1280]{1,0:T(8,128)S(1)}, u32[]{:S(2)}, u32[]{:S(2)}) collective-permute-start(f32[32,1280]{1,0:T(8,128)S(1)} %slice.49), channel_id=1, source_target_pairs={{0,32},{1,33},{2,34},{3,35},{4,36},{5,37},{6,38},{7,39},{8,232},{9... | collective-permute-start | bytes 491528 | tf_op jit(solution)/shard_map/ppermute | solution.py:45
  36.3 1.5 %add_texts.12 = (f32[256,128]{1,0:T(8,128)S(1)}, f32[256,512]{1,0:T(8,128)S(1)}, f32[256,512]{1,0:T(8,128)S(1)}) custom-call(f32[256,512]{1,0:T(8,128)S(1)} %convolution_multiply_fusion.refs_0_.refs_1_, f32[256,768]{1,0:T(8,128)S(1)} %broadcast_multiply_fusion.refs_1_.refs_2_, f32[64,1280]{1,0:T(8,128)S(1)} %collective-permute-done.12.refs_2_, ...), custom_call_target="tpu_custom_call" | custom-call | flops 18119393280 | bytes 4194304 | tf_op jit(solution)/shard_map/add_texts/pallas_call | solution.py:152
  38.4 2.3 %collective-permute-start.9 = (f32[32,1280]{1,0:T(8,128)S(1)}, f32[32,1280]{1,0:T(8,128)S(1)}, u32[]{:S(2)}, u32[]{:S(2)}) collective-permute-start(f32[32,1280]{1,0:T(8,128)S(1)} %slice.48), channel_id=1, source_target_pairs={{0,32},{1,33},{2,34},{3,35},{4,36},{5,37},{6,38},{7,39},{8,232},{9... | collective-permute-start | bytes 491528 | tf_op jit(solution)/shard_map/ppermute | solution.py:45
  40.7 1.5 %add_texts.13 = (f32[256,128]{1,0:T(8,128)S(1)}, f32[256,512]{1,0:T(8,128)S(1)}, f32[256,512]{1,0:T(8,128)S(1)}) custom-call(f32[256,512]{1,0:T(8,128)S(1)} %convolution_multiply_fusion.refs_0_.refs_1_, f32[256,768]{1,0:T(8,128)S(1)} %broadcast_multiply_fusion.refs_1_.refs_2_, f32[64,1280]{1,0:T(8,128)S(1)} %collective-permute-done.7.refs_2_, ...), custom_call_target="tpu_custom_call" | custom-call | flops 18119393280 | bytes 4194304 | tf_op jit(solution)/shard_map/add_texts/pallas_call | solution.py:152
  42.8 1.5 %add_texts.14 = (f32[256,128]{1,0:T(8,128)S(1)}, f32[256,512]{1,0:T(8,128)S(1)}, f32[256,512]{1,0:T(8,128)S(1)}) custom-call(f32[256,512]{1,0:T(8,128)S(1)} %convolution_multiply_fusion.refs_0_.refs_1_, f32[256,768]{1,0:T(8,128)S(1)} %broadcast_multiply_fusion.refs_1_.refs_2_, f32[64,1280]{1,0:T(8,128)S(1)} %collective-permute-done.13.refs_2_, ...), custom_call_target="tpu_custom_call" | custom-call | flops 18119393280 | bytes 4194304 | tf_op jit(solution)/shard_map/add_texts/pallas_call | solution.py:152
  44.3 1.5 %add_texts.15 = (f32[256,128]{1,0:T(8,128)S(1)}, f32[256,512]{1,0:T(8,128)S(1)}, f32[256,512]{1,0:T(8,128)S(1)}) custom-call(f32[256,512]{1,0:T(8,128)S(1)} %convolution_multiply_fusion.refs_0_.refs_1_, f32[256,768]{1,0:T(8,128)S(1)} %broadcast_multiply_fusion.refs_1_.refs_2_, f32[64,1280]{1,0:T(8,128)S(1)} %collective-permute-done.8.refs_2_, ...), custom_call_target="tpu_custom_call" | custom-call | flops 18119393280 | bytes 4194304 | tf_op jit(solution)/shard_map/add_texts/pallas_call | solution.py:152
  47.1 1.5 %add_texts.16 = (f32[256,128]{1,0:T(8,128)S(1)}, f32[256,512]{1,0:T(8,128)S(1)}, f32[256,512]{1,0:T(8,128)S(1)}) custom-call(f32[256,512]{1,0:T(8,128)S(1)} %convolution_multiply_fusion.refs_0_.refs_1_, f32[256,768]{1,0:T(8,128)S(1)} %broadcast_multiply_fusion.refs_1_.refs_2_, f32[32,1280]{1,0:T(8,128)S(1)} %collective-permute-done.20.refs_2_, ...), custom_call_target="tpu_custom_call" | custom-call | flops 9059696640 | bytes 4194304 | tf_op jit(solution)/shard_map/add_texts/pallas_call | solution.py:152
  48.6 2.3 %add_texts.17 = f32[8,264,128]{2,1,0:T(8,128)S(1)} custom-call(s32[8]{0:T(128)S(1)} %iota_xor_fusion.refs_0_, f32[256,512]{1,0:T(8,128)S(1)} %convolution_multiply_fusion.refs_0_.refs_1_, f32[256,768]{1,0:T(8,128)S(1)} %broadcast_multiply_fusion.refs_1_.refs_2_, f32[32,1280]{1,0:T(8,128)S(1)} %collective-permute-done.9.refs_3_, ...), custom_call_target="tpu_custom_call" | custom-call | flops 9059696640 | bytes 4194304 | tf_op jit(solution)/shard_map/add_texts/pallas_call | solution.py:152
  50.9 19.8 %all_to_all.10 = f32[8,264,128]{2,1,0:T(8,128)S(1)} all-to-all(f32[8,264,128]{2,1,0:T(8,128)S(1)} %add_texts.17), channel_id=1, replica_groups=mesh['z'=8,'xh'=2,'core'=2,'xl'=2,'y'=4] {'xl','y'}, dimensions={0} | all-to-all | bytes 2162688 | tf_op jit(solution)/shard_map/all_to_all | solution.py:259
  72.2 1.5 %collective-permute-start.22 = (f32[32,512]{1,0:T(8,128)S(1)}, f32[32,512]{1,0:T(8,128)S(1)}, u32[]{:S(2)}, u32[]{:S(2)}) collective-permute-start(f32[32,512]{1,0:T(8,128)S(1)} %constant_dynamic-slice_fusion), channel_id=1, source_target_pairs={{0,8},{1,9},{2,10},{3,11},{4,12},{5,13},{6,14},{7,15},{8,0},{9,1},... | collective-permute-start | bytes 196616 | tf_op jit(solution)/shard_map/ppermute | solution.py:45
  74.5 2.6 %collective-permute-start.23 = (f32[32,512]{1,0:T(8,128)S(1)}, f32[32,512]{1,0:T(8,128)S(1)}, u32[]{:S(2)}, u32[]{:S(2)}) collective-permute-start(f32[32,512]{1,0:T(8,128)S(1)} %dynamic-slice_add_fusion), channel_id=1, source_target_pairs={{0,20},{1,21},{2,22},{3,23},{4,16},{5,17},{6,18},{7,19},{8,28},{9,... | collective-permute-start | bytes 196616 | tf_op jit(solution)/shard_map/ppermute | solution.py:45
  77.1 1.8 %collective-permute-done.23 = f32[32,512]{1,0:T(8,128)S(1)} collective-permute-done((f32[32,512]{1,0:T(8,128)S(1)}, f32[32,512]{1,0:T(8,128)S(1)}, u32[]{:S(2)}, u32[]{:S(2)}) %collective-permute-start.23) | collective-permute-done | bytes 65568 | tf_op jit(solution)/shard_map/ppermute | solution.py:45
  79.1 3.1 %collective-permute-done.24 = f32[32,512]{1,0:T(8,128)S(1)} collective-permute-done((f32[32,512]{1,0:T(8,128)S(1)}, f32[32,512]{1,0:T(8,128)S(1)}, u32[]{:S(2)}, u32[]{:S(2)}) %collective-permute-start.24) | collective-permute-done | bytes 65568 | tf_op jit(solution)/shard_map/ppermute | solution.py:45
  82.2 2.2 %collective-permute-start.25 = (f32[32,512]{1,0:T(8,128)S(1)}, f32[32,512]{1,0:T(8,128)S(1)}, u32[]{:S(2)}, u32[]{:S(2)}) collective-permute-start(f32[32,512]{1,0:T(8,128)S(1)} %add.14), channel_id=1, source_target_pairs={{0,64},{1,65},{2,66},{3,67},{4,68},{5,69},{6,70},{7,71},{8,72},{9,... | collective-permute-start | bytes 196616 | tf_op jit(solution)/shard_map/ppermute | solution.py:45
  84.4 1.9 %collective-permute-done.25 = f32[32,512]{1,0:T(8,128)S(1)} collective-permute-done((f32[32,512]{1,0:T(8,128)S(1)}, f32[32,512]{1,0:T(8,128)S(1)}, u32[]{:S(2)}, u32[]{:S(2)}) %collective-permute-start.25) | collective-permute-done | bytes 65568 | tf_op jit(solution)/shard_map/ppermute | solution.py:45
  86.3 1.9 %collective-permute-start.26 = (f32[32,512]{1,0:T(8,128)S(1)}, f32[32,512]{1,0:T(8,128)S(1)}, u32[]{:S(2)}, u32[]{:S(2)}) collective-permute-start(f32[32,512]{1,0:T(8,128)S(1)} %add.15.term_ref), channel_id=1, source_target_pairs={{0,192},{1,193},{2,194},{3,195},{4,196},{5,197},{6,198},{7,199},{8... | collective-permute-start | bytes 196616 | tf_op jit(solution)/shard_map/ppermute | solution.py:45
  88.3 3.8 %collective-permute-done.26.received_ref = f32[32,512]{1,0:T(8,128)S(1)} collective-permute-done((f32[32,512]{1,0:T(8,128)S(1)}, f32[32,512]{1,0:T(8,128)S(1)}, u32[]{:S(2)}, u32[]{:S(2)}) %collective-permute-start.26) | collective-permute-done | bytes 65568 | tf_op jit(solution)/shard_map/ppermute | solution.py:45
  92.2 13.3 %all_to_all.11.pieces_ref = f32[8,256,128]{2,1,0:T(8,128)S(1)} all-to-all(f32[8,256,128]{2,1,0:T(8,128)S(1)} %shard_map.68), channel_id=1, replica_groups=mesh['z'=8,'xh'=2,'core'=2,'xl'=2,'y'=4] {'xl','y'}, dimensions={0} | all-to-all | bytes 2097152 | tf_op jit(solution)/shard_map/all_to_all | solution.py:279
  105.5 6.3 %collective-permute-start.27 = (f32[8,128,128]{2,1,0:T(8,128)S(1)}, f32[8,128,128]{2,1,0:T(8,128)S(1)}, u32[]{:S(2)}, u32[]{:S(2)}) collective-permute-start(f32[8,128,128]{2,1,0:T(8,128)S(1)} %slice.59), channel_id=1, source_target_pairs={{0,8},{1,9},{2,10},{3,11},{4,12},{5,13},{6,14},{7,15},{8,0},{9,1},... | collective-permute-start | bytes 1572872 | tf_op jit(solution)/shard_map/ppermute | solution.py:45
  111.9 2.0 %shard_map.69 = f32[256,512]{1,0:T(8,128)} custom-call(s32[2]{0:T(128)S(1)} %pad_add_fusion.where_ref, f32[8,256,128]{2,1,0:T(8,128)S(1)} %all_to_all.11.pieces_ref, f32[512,512]{1,0:T(8,128)S(1)} %copy-done.1), custom_call_target="tpu_custom_call" | custom-call | flops 1024 | bytes 1048576 | tf_op jit(solution)/shard_map/pallas_call | solution.py:174
  113.9 1.6 %shard_map.70 = f32[512,512]{1,0:T(8,128)} custom-call(s32[2]{0:T(128)S(1)} %pad_add_fusion.where_ref, f32[8,256,128]{2,1,0:T(8,128)S(1)} %all_to_all.11.pieces_ref, f32[8,128,128]{2,1,0:T(8,128)S(1)} %collective-permute-done.27.partner_ref), custom_call_target="tpu_custom_call" | custom-call | flops 1024 | bytes 1048576 | tf_op jit(solution)/shard_map/pallas_call | solution.py:174
  (72 shorter events, 15.0 us)
Async XLA Ops:
  0.6 6.4 %copy-start = (f32[256,512]{1,0:T(8,128)S(1)}, f32[256,512]{1,0:T(8,128)}, u32[]{:S(2)}) copy-start(f32[256,512]{1,0:T(8,128)} %param.5) | copy-start | bytes 1572868
  0.6 8.2 %copy-start.2 = (f32[256,768]{1,0:T(8,128)S(1)}, f32[256,768]{1,0:T(8,128)}, u32[]{:S(2)}) copy-start(f32[256,768]{1,0:T(8,128)} %param.6) | copy-start | bytes 2359300
  0.7 8.4 %collective-permute-start.2 = (f32[32,768]{1,0:T(8,128)}, f32[32,768]{1,0:T(8,128)S(1)}, u32[]{:S(2)}, u32[]{:S(2)}) collective-permute-start(f32[32,768]{1,0:T(8,128)} %param.8), channel_id=1, source_target_pairs={{0,8},{1,9},{2,10},{3,11},{4,12},{5,13},{6,14},{7,15},{8,0},{9,1},... | collective-permute-start | bytes 294920 | tf_op jit(solution)/shard_map/ppermute | solution.py:45
  4.0 9.8 %collective-permute-start = (f32[32,768]{1,0:T(8,128)}, f32[32,768]{1,0:T(8,128)S(1)}, u32[]{:S(2)}, u32[]{:S(2)}) collective-permute-start(f32[32,768]{1,0:T(8,128)} %param.8), channel_id=1, source_target_pairs={{0,20},{1,21},{2,22},{3,23},{4,16},{5,17},{6,18},{7,19},{8,28},{9,... | collective-permute-start | bytes 294920 | tf_op jit(solution)/shard_map/ppermute | solution.py:45
  4.7 4.3 %collective-permute-start.3 = (f32[32,512]{1,0:T(8,128)}, f32[32,512]{1,0:T(8,128)S(1)}, u32[]{:S(2)}, u32[]{:S(2)}) collective-permute-start(f32[32,512]{1,0:T(8,128)} %param.7), channel_id=1, source_target_pairs={{0,8},{1,9},{2,10},{3,11},{4,12},{5,13},{6,14},{7,15},{8,0},{9,1},... | collective-permute-start | bytes 196616 | tf_op jit(solution)/shard_map/ppermute | solution.py:45
  5.1 8.6 %collective-permute-start.1 = (f32[32,512]{1,0:T(8,128)}, f32[32,512]{1,0:T(8,128)S(1)}, u32[]{:S(2)}, u32[]{:S(2)}) collective-permute-start(f32[32,512]{1,0:T(8,128)} %param.7), channel_id=1, source_target_pairs={{0,20},{1,21},{2,22},{3,23},{4,16},{5,17},{6,18},{7,19},{8,28},{9,... | collective-permute-start | bytes 196616 | tf_op jit(solution)/shard_map/ppermute | solution.py:45
  8.9 0.9 copy-start.3
  9.8 8.2 %collective-permute-start.11 = (f32[64,1280]{1,0:T(8,128)S(1)}, f32[64,1280]{1,0:T(8,128)S(1)}, u32[]{:S(2)}, u32[]{:S(2)}) collective-permute-start(f32[64,1280]{1,0:T(8,128)S(1)} %maximum_maximum_fusion.refs_2_), channel_id=1, source_target_pairs={{0,32},{1,33},{2,34},{3,35},{4,36},{5,37},{6,38},{7,39},{8,232},{9... | collective-permute-start | bytes 983048 | tf_op jit(solution)/shard_map/ppermute | solution.py:45
  13.7 1.4 %collective-permute-start.4 = (f32[32,768]{1,0:T(8,128)S(1)}, f32[32,768]{1,0:T(8,128)S(1)}, u32[]{:S(2)}, u32[]{:S(2)}) collective-permute-start(f32[32,768]{1,0:T(8,128)S(1)} %collective-permute-done), channel_id=1, source_target_pairs={{0,8},{1,9},{2,10},{3,11},{4,12},{5,13},{6,14},{7,15},{8,0},{9,1},... | collective-permute-start | bytes 294920 | tf_op jit(solution)/shard_map/ppermute | solution.py:45
  13.8 1.4 %collective-permute-start.5 = (f32[32,512]{1,0:T(8,128)S(1)}, f32[32,512]{1,0:T(8,128)S(1)}, u32[]{:S(2)}, u32[]{:S(2)}) collective-permute-start(f32[32,512]{1,0:T(8,128)S(1)} %collective-permute-done.1), channel_id=1, source_target_pairs={{0,8},{1,9},{2,10},{3,11},{4,12},{5,13},{6,14},{7,15},{8,0},{9,1},... | collective-permute-start | bytes 196616 | tf_op jit(solution)/shard_map/ppermute | solution.py:45
  15.2 7.4 %collective-permute-start.6 = (f32[64,1280]{1,0:T(8,128)S(1)}, f32[64,1280]{1,0:T(8,128)S(1)}, u32[]{:S(2)}, u32[]{:S(2)}) collective-permute-start(f32[64,1280]{1,0:T(8,128)S(1)} %maximum_maximum_fusion.1.refs_3_), channel_id=1, source_target_pairs={{0,32},{1,33},{2,34},{3,35},{4,36},{5,37},{6,38},{7,39},{8,232},{9... | collective-permute-start | bytes 983048 | tf_op jit(solution)/shard_map/ppermute | solution.py:45
  18.0 10.7 %collective-permute-start.18 = (f32[64,1280]{1,0:T(8,128)S(1)}, f32[64,1280]{1,0:T(8,128)S(1)}, u32[]{:S(2)}, u32[]{:S(2)}) collective-permute-start(f32[64,1280]{1,0:T(8,128)S(1)} %collective-permute-done.11.refs_2_), channel_id=1, source_target_pairs={{0,8},{1,9},{2,10},{3,11},{4,12},{5,13},{6,14},{7,15},{8,0},{9,1},... | collective-permute-start | bytes 983048 | tf_op jit(solution)/shard_map/ppermute | solution.py:45
  19.5 6.2 %collective-permute-start.12 = (f32[64,1280]{1,0:T(8,128)S(1)}, f32[64,1280]{1,0:T(8,128)S(1)}, u32[]{:S(2)}, u32[]{:S(2)}) collective-permute-start(f32[64,1280]{1,0:T(8,128)S(1)} %collective-permute-done.11.refs_2_), channel_id=1, source_target_pairs={{0,32},{1,33},{2,34},{3,35},{4,36},{5,37},{6,38},{7,39},{8,232},{9... | collective-permute-start | bytes 983048 | tf_op jit(solution)/shard_map/ppermute | solution.py:45
  22.6 10.1 %collective-permute-start.17 = (f32[64,1280]{1,0:T(8,128)S(1)}, f32[64,1280]{1,0:T(8,128)S(1)}, u32[]{:S(2)}, u32[]{:S(2)}) collective-permute-start(f32[64,1280]{1,0:T(8,128)S(1)} %collective-permute-done.6.refs_2_), channel_id=1, source_target_pairs={{0,8},{1,9},{2,10},{3,11},{4,12},{5,13},{6,14},{7,15},{8,0},{9,1},... | collective-permute-start | bytes 983048 | tf_op jit(solution)/shard_map/ppermute | solution.py:45
  23.9 6.3 %collective-permute-start.7 = (f32[64,1280]{1,0:T(8,128)S(1)}, f32[64,1280]{1,0:T(8,128)S(1)}, u32[]{:S(2)}, u32[]{:S(2)}) collective-permute-start(f32[64,1280]{1,0:T(8,128)S(1)} %collective-permute-done.6.refs_2_), channel_id=1, source_target_pairs={{0,32},{1,33},{2,34},{3,35},{4,36},{5,37},{6,38},{7,39},{8,232},{9... | collective-permute-start | bytes 983048 | tf_op jit(solution)/shard_map/ppermute | solution.py:45
  25.7 10.6 %collective-permute-start.16 = (f32[64,1280]{1,0:T(8,128)S(1)}, f32[64,1280]{1,0:T(8,128)S(1)}, u32[]{:S(2)}, u32[]{:S(2)}) collective-permute-start(f32[64,1280]{1,0:T(8,128)S(1)} %collective-permute-done.12.refs_2_), channel_id=1, source_target_pairs={{0,8},{1,9},{2,10},{3,11},{4,12},{5,13},{6,14},{7,15},{8,0},{9,1},... | collective-permute-start | bytes 983048 | tf_op jit(solution)/shard_map/ppermute | solution.py:45
  27.8 6.4 %collective-permute-start.13 = (f32[64,1280]{1,0:T(8,128)S(1)}, f32[64,1280]{1,0:T(8,128)S(1)}, u32[]{:S(2)}, u32[]{:S(2)}) collective-permute-start(f32[64,1280]{1,0:T(8,128)S(1)} %collective-permute-done.12.refs_2_), channel_id=1, source_target_pairs={{0,32},{1,33},{2,34},{3,35},{4,36},{5,37},{6,38},{7,39},{8,232},{9... | collective-permute-start | bytes 983048 | tf_op jit(solution)/shard_map/ppermute | solution.py:45
  30.2 10.5 %collective-permute-start.15 = (f32[64,1280]{1,0:T(8,128)S(1)}, f32[64,1280]{1,0:T(8,128)S(1)}, u32[]{:S(2)}, u32[]{:S(2)}) collective-permute-start(f32[64,1280]{1,0:T(8,128)S(1)} %collective-permute-done.7.refs_2_), channel_id=1, source_target_pairs={{0,8},{1,9},{2,10},{3,11},{4,12},{5,13},{6,14},{7,15},{8,0},{9,1},... | collective-permute-start | bytes 983048 | tf_op jit(solution)/shard_map/ppermute | solution.py:45
  32.2 6.2 %collective-permute-start.8 = (f32[64,1280]{1,0:T(8,128)S(1)}, f32[64,1280]{1,0:T(8,128)S(1)}, u32[]{:S(2)}, u32[]{:S(2)}) collective-permute-start(f32[64,1280]{1,0:T(8,128)S(1)} %collective-permute-done.7.refs_2_), channel_id=1, source_target_pairs={{0,32},{1,33},{2,34},{3,35},{4,36},{5,37},{6,38},{7,39},{8,232},{9... | collective-permute-start | bytes 983048 | tf_op jit(solution)/shard_map/ppermute | solution.py:45
  34.2 8.0 %collective-permute-start.20 = (f32[32,1280]{1,0:T(8,128)S(1)}, f32[32,1280]{1,0:T(8,128)S(1)}, u32[]{:S(2)}, u32[]{:S(2)}) collective-permute-start(f32[32,1280]{1,0:T(8,128)S(1)} %slice.49), channel_id=1, source_target_pairs={{0,32},{1,33},{2,34},{3,35},{4,36},{5,37},{6,38},{7,39},{8,232},{9... | collective-permute-start | bytes 491528 | tf_op jit(solution)/shard_map/ppermute | solution.py:45
  36.0 6.9 %collective-permute-start.14 = (f32[64,1280]{1,0:T(8,128)S(1)}, f32[64,1280]{1,0:T(8,128)S(1)}, u32[]{:S(2)}, u32[]{:S(2)}) collective-permute-start(f32[64,1280]{1,0:T(8,128)S(1)} %collective-permute-done.13.refs_2_), channel_id=1, source_target_pairs={{0,8},{1,9},{2,10},{3,11},{4,12},{5,13},{6,14},{7,15},{8,0},{9,1},... | collective-permute-start | bytes 983048 | tf_op jit(solution)/shard_map/ppermute | solution.py:45
  38.4 7.3 %collective-permute-start.9 = (f32[32,1280]{1,0:T(8,128)S(1)}, f32[32,1280]{1,0:T(8,128)S(1)}, u32[]{:S(2)}, u32[]{:S(2)}) collective-permute-start(f32[32,1280]{1,0:T(8,128)S(1)} %slice.48), channel_id=1, source_target_pairs={{0,32},{1,33},{2,34},{3,35},{4,36},{5,37},{6,38},{7,39},{8,232},{9... | collective-permute-start | bytes 491528 | tf_op jit(solution)/shard_map/ppermute | solution.py:45
  40.7 3.6 %collective-permute-start.10 = (f32[64,1280]{1,0:T(8,128)S(1)}, f32[64,1280]{1,0:T(8,128)S(1)}, u32[]{:S(2)}, u32[]{:S(2)}) collective-permute-start(f32[64,1280]{1,0:T(8,128)S(1)} %collective-permute-done.8.refs_2_), channel_id=1, source_target_pairs={{0,8},{1,9},{2,10},{3,11},{4,12},{5,13},{6,14},{7,15},{8,0},{9,1},... | collective-permute-start | bytes 983048 | tf_op jit(solution)/shard_map/ppermute | solution.py:45
  42.2 4.9 %collective-permute-start.21 = (f32[32,1280]{1,0:T(8,128)S(1)}, f32[32,1280]{1,0:T(8,128)S(1)}, u32[]{:S(2)}, u32[]{:S(2)}) collective-permute-start(f32[32,1280]{1,0:T(8,128)S(1)} %collective-permute-done.20.refs_2_), channel_id=1, source_target_pairs={{0,8},{1,9},{2,10},{3,11},{4,12},{5,13},{6,14},{7,15},{8,0},{9,1},... | collective-permute-start | bytes 491528 | tf_op jit(solution)/shard_map/ppermute | solution.py:45
  45.8 2.8 %collective-permute-start.19 = (f32[32,1280]{1,0:T(8,128)S(1)}, f32[32,1280]{1,0:T(8,128)S(1)}, u32[]{:S(2)}, u32[]{:S(2)}) collective-permute-start(f32[32,1280]{1,0:T(8,128)S(1)} %collective-permute-done.9.refs_3_), channel_id=1, source_target_pairs={{0,8},{1,9},{2,10},{3,11},{4,12},{5,13},{6,14},{7,15},{8,0},{9,1},... | collective-permute-start | bytes 491528 | tf_op jit(solution)/shard_map/ppermute | solution.py:45
  72.2 2.4 %collective-permute-start.22 = (f32[32,512]{1,0:T(8,128)S(1)}, f32[32,512]{1,0:T(8,128)S(1)}, u32[]{:S(2)}, u32[]{:S(2)}) collective-permute-start(f32[32,512]{1,0:T(8,128)S(1)} %constant_dynamic-slice_fusion), channel_id=1, source_target_pairs={{0,8},{1,9},{2,10},{3,11},{4,12},{5,13},{6,14},{7,15},{8,0},{9,1},... | collective-permute-start | bytes 196616 | tf_op jit(solution)/shard_map/ppermute | solution.py:45
  74.5 4.4 %collective-permute-start.23 = (f32[32,512]{1,0:T(8,128)S(1)}, f32[32,512]{1,0:T(8,128)S(1)}, u32[]{:S(2)}, u32[]{:S(2)}) collective-permute-start(f32[32,512]{1,0:T(8,128)S(1)} %dynamic-slice_add_fusion), channel_id=1, source_target_pairs={{0,20},{1,21},{2,22},{3,23},{4,16},{5,17},{6,18},{7,19},{8,28},{9,... | collective-permute-start | bytes 196616 | tf_op jit(solution)/shard_map/ppermute | solution.py:45
  79.0 3.2 %collective-permute-start.24 = (f32[32,512]{1,0:T(8,128)S(1)}, f32[32,512]{1,0:T(8,128)S(1)}, u32[]{:S(2)}, u32[]{:S(2)}) collective-permute-start(f32[32,512]{1,0:T(8,128)S(1)} %add.13), channel_id=1, source_target_pairs={{0,32},{1,33},{2,34},{3,35},{4,36},{5,37},{6,38},{7,39},{8,40},{9,... | collective-permute-start | bytes 196616 | tf_op jit(solution)/shard_map/ppermute | solution.py:45
  82.2 4.1 %collective-permute-start.25 = (f32[32,512]{1,0:T(8,128)S(1)}, f32[32,512]{1,0:T(8,128)S(1)}, u32[]{:S(2)}, u32[]{:S(2)}) collective-permute-start(f32[32,512]{1,0:T(8,128)S(1)} %add.14), channel_id=1, source_target_pairs={{0,64},{1,65},{2,66},{3,67},{4,68},{5,69},{6,70},{7,71},{8,72},{9,... | collective-permute-start | bytes 196616 | tf_op jit(solution)/shard_map/ppermute | solution.py:45
  86.3 5.8 %collective-permute-start.26 = (f32[32,512]{1,0:T(8,128)S(1)}, f32[32,512]{1,0:T(8,128)S(1)}, u32[]{:S(2)}, u32[]{:S(2)}) collective-permute-start(f32[32,512]{1,0:T(8,128)S(1)} %add.15.term_ref), channel_id=1, source_target_pairs={{0,192},{1,193},{2,194},{3,195},{4,196},{5,197},{6,198},{7,199},{8... | collective-permute-start | bytes 196616 | tf_op jit(solution)/shard_map/ppermute | solution.py:45
  92.2 19.7 %copy-start.1 = (f32[512,512]{1,0:T(8,128)S(1)}, f32[512,512]{1,0:T(8,128)}, u32[]{:S(2)}) copy-start(f32[512,512]{1,0:T(8,128)} %head_ref.1) | copy-start | bytes 3145732
  105.5 8.4 %collective-permute-start.27 = (f32[8,128,128]{2,1,0:T(8,128)S(1)}, f32[8,128,128]{2,1,0:T(8,128)S(1)}, u32[]{:S(2)}, u32[]{:S(2)}) collective-permute-start(f32[8,128,128]{2,1,0:T(8,128)S(1)} %slice.59), channel_id=1, source_target_pairs={{0,8},{1,9},{2,10},{3,11},{4,12},{5,13},{6,14},{7,15},{8,0},{9,1},... | collective-permute-start | bytes 1572872 | tf_op jit(solution)/shard_map/ppermute | solution.py:45
  (1 other events, 0.9 us)

commit v6 on v5

--- a/solution.py
+++ b/solution.py
@@ -233,8 +233,6 @@
     scale_t = 4.0 / math.sqrt(DT)
     batch = ROWS * 32
     xh, core = lax.axis_index("xh"), lax.axis_index("core")
-    folded = scale_s * dot(image_student, head, NT)
-    images = scale_t * image_teacher
 
     own = [text_teacher, text_features]
     near = [move(array, CORE) for array in own]
@@ -243,12 +241,18 @@
     *far, _ = lax.optimization_barrier((*far, one))
     last = [move(array, CORE) for array in far]
     two = jnp.concatenate([jnp.concatenate(part, axis=1) for part in (far, last)], axis=0)
+    students, _ = lax.optimization_barrier((image_student, one))
+    folded = scale_s * dot(students, head, NT)
+    images = scale_t * image_teacher
     state = add_texts(folded, images, [one, two])
     for step in range(3):
         one, two = move(one, Z_NEXT), move(two, Z_NEXT)
         state = add_texts(folded, images, [one, move(one, CORE)], state)
+        if step == 2:
+            one = move(one[:SHARD], Z_NEXT)
+            one, *state = lax.optimization_barrier((one, *state))
         state = add_texts(folded, images, [two, move(two, CORE)], state)
-    one, two = move(one[:SHARD], Z_NEXT), move(two[:SHARD], Z_NEXT)
+    two = move(two[:SHARD], Z_NEXT)
     two, *state = lax.optimization_barrier((two, *state))
     state = add_texts(folded, images, [one, move(one, CORE)], state)
     place = jnp.arange(8, dtype=jnp.int32) ^ (4 * xh).astype(jnp.int32)

time: 116 us -> 115 us (level)
  other arithmetic: 1.39 us -> 2.61 us
  matrix products: 2.13 us -> 0.93 us
    mul x1, other arithmetic: 0.07 us -> 1.29 us  [shards(): images = scale_t * image_teacher]
    dot_general x2, matrix products: 2.13 us -> 0.93 us  [dot(): lax.dot_general(a, b, (dims, ((), ())), precision=HIGH, preferred_element...]
  transfers between devices with their start and end apart: 28 -> 28, of which waited for: 8 -> 9; matrix products, arithmetic and copies ran while one was open for 2% -> 2% of each run, Pallas kernels for 12% -> 12%
where the time goes in v6:
time: 115 us
  starting transfers between devices  46 us (40%)
  blocking collectives  33 us (29%)
  Pallas kernels  17.5 us (15%)
  waiting for transfers between devices  13.8 us (12%)
  other arithmetic  2.61 us (2%)
    ppermute x28, starting transfers between devices, move(): return lax.ppermute(array, AXES, pairs)  46 us
    all_to_all x1, blocking collectives, shards(): got = lax.all_to_all(both, ('xl', 'y'), 0, 0, tiled=True)  19.8 us
    pallas_call x9, Pallas kernels, add_texts(): pl.pallas_call(body, out_shape=shapes, in_specs=in_specs, out_specs=[vmem...  13.8 us
    ppermute x28, waiting for transfers between devices, move(): return lax.ppermute(array, AXES, pairs)  13.8 us
    all_to_all x1, blocking collectives, shards(): pieces = lax.all_to_all(packed, ('xl', 'y'), 0, 0, tiled=True)  13.1 us
    pallas_call x3, Pallas kernels, small_call(): pl.pallas_call(body, out_shape=jax.ShapeDtypeStruct(shape, jnp.float32),...  3.66 us
  transfers between devices with their start and end apart: 28, of which 9 were waited for; matrix products, arithmetic and copies ran while one was open for 2% of the time, Pallas kernels for 12%

profile of v6, /device:TPU:1, one launch (start us, length us, event | category | flops | bytes accessed | tf_op | source)
XLA Modules:
  0.0 114.8 jit_solution(15549559658887645856)
XLA Ops:
  0.7 3.3 %collective-permute-start = (f32[32,768]{1,0:T(8,128)}, f32[32,768]{1,0:T(8,128)S(1)}, u32[]{:S(2)}, u32[]{:S(2)}) collective-permute-start(f32[32,768]{1,0:T(8,128)} %param.8), channel_id=1, source_target_pairs={{0,8},{1,9},{2,10},{3,11},{4,12},{5,13},{6,14},{7,15},{8,0},{9,1},... | collective-permute-start | bytes 294920 | tf_op jit(solution)/shard_map/ppermute | solution.py:45
  5.1 1.9 %collective-permute-start.3 = (f32[32,512]{1,0:T(8,128)}, f32[32,512]{1,0:T(8,128)S(1)}, u32[]{:S(2)}, u32[]{:S(2)}) collective-permute-start(f32[32,512]{1,0:T(8,128)} %param.7), channel_id=1, source_target_pairs={{0,20},{1,21},{2,22},{3,23},{4,16},{5,17},{6,18},{7,19},{8,28},{9,... | collective-permute-start | bytes 196616 | tf_op jit(solution)/shard_map/ppermute | solution.py:45
  8.4 3.9 %collective-permute-start.11 = (f32[64,1280]{1,0:T(8,128)S(1)}, f32[64,1280]{1,0:T(8,128)S(1)}, u32[]{:S(2)}, u32[]{:S(2)}) collective-permute-start(f32[64,1280]{1,0:T(8,128)S(1)} %maximum_maximum_fusion.refs_2_), channel_id=1, source_target_pairs={{0,32},{1,33},{2,34},{3,35},{4,36},{5,37},{6,38},{7,39},{8,232},{9... | collective-permute-start | bytes 983048 | tf_op jit(solution)/shard_map/ppermute | solution.py:45
  13.8 4.2 %collective-permute-start.6 = (f32[64,1280]{1,0:T(8,128)S(1)}, f32[64,1280]{1,0:T(8,128)S(1)}, u32[]{:S(2)}, u32[]{:S(2)}) collective-permute-start(f32[64,1280]{1,0:T(8,128)S(1)} %maximum_maximum_fusion.1.refs_3_), channel_id=1, source_target_pairs={{0,32},{1,33},{2,34},{3,35},{4,36},{5,37},{6,38},{7,39},{8,232},{9... | collective-permute-start | bytes 983048 | tf_op jit(solution)/shard_map/ppermute | solution.py:45
  18.1 1.7 %collective-permute-start.12 = (f32[64,1280]{1,0:T(8,128)S(1)}, f32[64,1280]{1,0:T(8,128)S(1)}, u32[]{:S(2)}, u32[]{:S(2)}) collective-permute-start(f32[64,1280]{1,0:T(8,128)S(1)} %collective-permute-done.11.refs_2_), channel_id=1, source_target_pairs={{0,32},{1,33},{2,34},{3,35},{4,36},{5,37},{6,38},{7,39},{8,232},{9... | collective-permute-start | bytes 983048 | tf_op jit(solution)/shard_map/ppermute | solution.py:45
  22.0 1.5 %collective-permute-start.18 = (f32[64,1280]{1,0:T(8,128)S(1)}, f32[64,1280]{1,0:T(8,128)S(1)}, u32[]{:S(2)}, u32[]{:S(2)}) collective-permute-start(f32[64,1280]{1,0:T(8,128)S(1)} %collective-permute-done.6.refs_2_), channel_id=1, source_target_pairs={{0,8},{1,9},{2,10},{3,11},{4,12},{5,13},{6,14},{7,15},{8,0},{9,1},... | collective-permute-start | bytes 983048 | tf_op jit(solution)/shard_map/ppermute | solution.py:45
  23.5 1.7 %collective-permute-start.7 = (f32[64,1280]{1,0:T(8,128)S(1)}, f32[64,1280]{1,0:T(8,128)S(1)}, u32[]{:S(2)}, u32[]{:S(2)}) collective-permute-start(f32[64,1280]{1,0:T(8,128)S(1)} %collective-permute-done.6.refs_2_), channel_id=1, source_target_pairs={{0,32},{1,33},{2,34},{3,35},{4,36},{5,37},{6,38},{7,39},{8,232},{9... | collective-permute-start | bytes 983048 | tf_op jit(solution)/shard_map/ppermute | solution.py:45
  25.5 1.5 %collective-permute-start.17 = (f32[64,1280]{1,0:T(8,128)S(1)}, f32[64,1280]{1,0:T(8,128)S(1)}, u32[]{:S(2)}, u32[]{:S(2)}) collective-permute-start(f32[64,1280]{1,0:T(8,128)S(1)} %collective-permute-done.12.refs_2_), channel_id=1, source_target_pairs={{0,8},{1,9},{2,10},{3,11},{4,12},{5,13},{6,14},{7,15},{8,0},{9,1},... | collective-permute-start | bytes 983048 | tf_op jit(solution)/shard_map/ppermute | solution.py:45
  27.0 1.7 %collective-permute-start.13 = (f32[64,1280]{1,0:T(8,128)S(1)}, f32[64,1280]{1,0:T(8,128)S(1)}, u32[]{:S(2)}, u32[]{:S(2)}) collective-permute-start(f32[64,1280]{1,0:T(8,128)S(1)} %collective-permute-done.12.refs_2_), channel_id=1, source_target_pairs={{0,32},{1,33},{2,34},{3,35},{4,36},{5,37},{6,38},{7,39},{8,232},{9... | collective-permute-start | bytes 983048 | tf_op jit(solution)/shard_map/ppermute | solution.py:45
  28.7 1.5 %add_texts.10 = (f32[256,128]{1,0:T(8,128)S(1)}, f32[256,512]{1,0:T(8,128)S(1)}, f32[256,512]{1,0:T(8,128)S(1)}) custom-call(f32[256,512]{1,0:T(8,128)S(1)} %convolution_multiply_fusion.refs_0_.refs_1_, f32[256,768]{1,0:T(8,128)S(1)} %broadcast_multiply_fusion.refs_1_.refs_2_, f32[64,1280]{1,0:T(8,128)S(1)} %collective-permute-done.11.refs_2_, ...), custom_call_target="tpu_custom_call" | custom-call | flops 18119393280 | bytes 4194304 | tf_op jit(solution)/shard_map/add_texts/pallas_call | solution.py:152
  30.2 1.6 %collective-permute-start.16 = (f32[64,1280]{1,0:T(8,128)S(1)}, f32[64,1280]{1,0:T(8,128)S(1)}, u32[]{:S(2)}, u32[]{:S(2)}) collective-permute-start(f32[64,1280]{1,0:T(8,128)S(1)} %collective-permute-done.7.refs_2_), channel_id=1, source_target_pairs={{0,8},{1,9},{2,10},{3,11},{4,12},{5,13},{6,14},{7,15},{8,0},{9,1},... | collective-permute-start | bytes 983048 | tf_op jit(solution)/shard_map/ppermute | solution.py:45
  32.7 1.5 %add_texts.11 = (f32[256,128]{1,0:T(8,128)S(1)}, f32[256,512]{1,0:T(8,128)S(1)}, f32[256,512]{1,0:T(8,128)S(1)}) custom-call(f32[256,512]{1,0:T(8,128)S(1)} %convolution_multiply_fusion.refs_0_.refs_1_, f32[256,768]{1,0:T(8,128)S(1)} %broadcast_multiply_fusion.refs_1_.refs_2_, f32[64,1280]{1,0:T(8,128)S(1)} %collective-permute-done.6.refs_2_, ...), custom_call_target="tpu_custom_call" | custom-call | flops 18119393280 | bytes 4194304 | tf_op jit(solution)/shard_map/add_texts/pallas_call | solution.py:152
  34.2 1.8 %collective-permute-start.14 = (f32[32,1280]{1,0:T(8,128)S(1)}, f32[32,1280]{1,0:T(8,128)S(1)}, u32[]{:S(2)}, u32[]{:S(2)}) collective-permute-start(f32[32,1280]{1,0:T(8,128)S(1)} %slice.49), channel_id=1, source_target_pairs={{0,32},{1,33},{2,34},{3,35},{4,36},{5,37},{6,38},{7,39},{8,232},{9... | collective-permute-start | bytes 491528 | tf_op jit(solution)/shard_map/ppermute | solution.py:45
  36.0 1.5 %add_texts.12 = (f32[256,128]{1,0:T(8,128)S(1)}, f32[256,512]{1,0:T(8,128)S(1)}, f32[256,512]{1,0:T(8,128)S(1)}) custom-call(f32[256,512]{1,0:T(8,128)S(1)} %convolution_multiply_fusion.refs_0_.refs_1_, f32[256,768]{1,0:T(8,128)S(1)} %broadcast_multiply_fusion.refs_1_.refs_2_, f32[64,1280]{1,0:T(8,128)S(1)} %collective-permute-done.12.refs_2_, ...), custom_call_target="tpu_custom_call" | custom-call | flops 18119393280 | bytes 4194304 | tf_op jit(solution)/shard_map/add_texts/pallas_call | solution.py:152
  38.0 1.9 %collective-permute-start.9 = (f32[32,1280]{1,0:T(8,128)S(1)}, f32[32,1280]{1,0:T(8,128)S(1)}, u32[]{:S(2)}, u32[]{:S(2)}) collective-permute-start(f32[32,1280]{1,0:T(8,128)S(1)} %slice.48), channel_id=1, source_target_pairs={{0,32},{1,33},{2,34},{3,35},{4,36},{5,37},{6,38},{7,39},{8,232},{9... | collective-permute-start | bytes 491528 | tf_op jit(solution)/shard_map/ppermute | solution.py:45
  40.3 1.5 %add_texts.13 = (f32[256,128]{1,0:T(8,128)S(1)}, f32[256,512]{1,0:T(8,128)S(1)}, f32[256,512]{1,0:T(8,128)S(1)}) custom-call(f32[256,512]{1,0:T(8,128)S(1)} %convolution_multiply_fusion.refs_0_.refs_1_, f32[256,768]{1,0:T(8,128)S(1)} %broadcast_multiply_fusion.refs_1_.refs_2_, f32[64,1280]{1,0:T(8,128)S(1)} %collective-permute-done.7.refs_2_, ...), custom_call_target="tpu_custom_call" | custom-call | flops 18119393280 | bytes 4194304 | tf_op jit(solution)/shard_map/add_texts/pallas_call | solution.py:152
  41.7 1.5 %add_texts.14 = (f32[256,128]{1,0:T(8,128)S(1)}, f32[256,512]{1,0:T(8,128)S(1)}, f32[256,512]{1,0:T(8,128)S(1)}) custom-call(f32[256,512]{1,0:T(8,128)S(1)} %convolution_multiply_fusion.refs_0_.refs_1_, f32[256,768]{1,0:T(8,128)S(1)} %broadcast_multiply_fusion.refs_1_.refs_2_, f32[64,1280]{1,0:T(8,128)S(1)} %collective-permute-done.13.refs_2_, ...), custom_call_target="tpu_custom_call" | custom-call | flops 18119393280 | bytes 4194304 | tf_op jit(solution)/shard_map/add_texts/pallas_call | solution.py:152
  43.5 1.5 %add_texts.15 = (f32[256,128]{1,0:T(8,128)S(1)}, f32[256,512]{1,0:T(8,128)S(1)}, f32[256,512]{1,0:T(8,128)S(1)}) custom-call(f32[256,512]{1,0:T(8,128)S(1)} %convolution_multiply_fusion.refs_0_.refs_1_, f32[256,768]{1,0:T(8,128)S(1)} %broadcast_multiply_fusion.refs_1_.refs_2_, f32[64,1280]{1,0:T(8,128)S(1)} %collective-permute-done.8.refs_2_, ...), custom_call_target="tpu_custom_call" | custom-call | flops 18119393280 | bytes 4194304 | tf_op jit(solution)/shard_map/add_texts/pallas_call | solution.py:152
  45.0 1.7 %collective-permute-start.20 = (f32[32,1280]{1,0:T(8,128)S(1)}, f32[32,1280]{1,0:T(8,128)S(1)}, u32[]{:S(2)}, u32[]{:S(2)}) collective-permute-start(f32[32,1280]{1,0:T(8,128)S(1)} %collective-permute-done.9.refs_3_), channel_id=1, source_target_pairs={{0,8},{1,9},{2,10},{3,11},{4,12},{5,13},{6,14},{7,15},{8,0},{9,1},... | collective-permute-start | bytes 491528 | tf_op jit(solution)/shard_map/ppermute | solution.py:45
  48.2 2.3 %add_texts.17 = f32[8,264,128]{2,1,0:T(8,128)S(1)} custom-call(s32[8]{0:T(128)S(1)} %iota_xor_fusion.refs_0_, f32[256,512]{1,0:T(8,128)S(1)} %convolution_multiply_fusion.refs_0_.refs_1_, f32[256,768]{1,0:T(8,128)S(1)} %broadcast_multiply_fusion.refs_1_.refs_2_, f32[32,1280]{1,0:T(8,128)S(1)} %collective-permute-done.9.refs_3_, ...), custom_call_target="tpu_custom_call" | custom-call | flops 9059696640 | bytes 4194304 | tf_op jit(solution)/shard_map/add_texts/pallas_call | solution.py:152
  50.5 19.8 %all_to_all.10 = f32[8,264,128]{2,1,0:T(8,128)S(1)} all-to-all(f32[8,264,128]{2,1,0:T(8,128)S(1)} %add_texts.17), channel_id=1, replica_groups=mesh['z'=8,'xh'=2,'core'=2,'xl'=2,'y'=4] {'xl','y'}, dimensions={0} | all-to-all | bytes 2162688 | tf_op jit(solution)/shard_map/all_to_all | solution.py:263
  74.1 1.8 %collective-permute-start.23 = (f32[32,512]{1,0:T(8,128)S(1)}, f32[32,512]{1,0:T(8,128)S(1)}, u32[]{:S(2)}, u32[]{:S(2)}) collective-permute-start(f32[32,512]{1,0:T(8,128)S(1)} %dynamic-slice_add_fusion), channel_id=1, source_target_pairs={{0,20},{1,21},{2,22},{3,23},{4,16},{5,17},{6,18},{7,19},{8,28},{9,... | collective-permute-start | bytes 196616 | tf_op jit(solution)/shard_map/ppermute | solution.py:45
  75.9 2.6 %collective-permute-done.23 = f32[32,512]{1,0:T(8,128)S(1)} collective-permute-done((f32[32,512]{1,0:T(8,128)S(1)}, f32[32,512]{1,0:T(8,128)S(1)}, u32[]{:S(2)}, u32[]{:S(2)}) %collective-permute-start.23) | collective-permute-done | bytes 65568 | tf_op jit(solution)/shard_map/ppermute | solution.py:45
  78.6 3.1 %collective-permute-done.24 = f32[32,512]{1,0:T(8,128)S(1)} collective-permute-done((f32[32,512]{1,0:T(8,128)S(1)}, f32[32,512]{1,0:T(8,128)S(1)}, u32[]{:S(2)}, u32[]{:S(2)}) %collective-permute-start.24) | collective-permute-done | bytes 65568 | tf_op jit(solution)/shard_map/ppermute | solution.py:45
  81.7 2.6 %collective-permute-start.25 = (f32[32,512]{1,0:T(8,128)S(1)}, f32[32,512]{1,0:T(8,128)S(1)}, u32[]{:S(2)}, u32[]{:S(2)}) collective-permute-start(f32[32,512]{1,0:T(8,128)S(1)} %add.14), channel_id=1, source_target_pairs={{0,64},{1,65},{2,66},{3,67},{4,68},{5,69},{6,70},{7,71},{8,72},{9,... | collective-permute-start | bytes 196616 | tf_op jit(solution)/shard_map/ppermute | solution.py:45
  84.3 1.6 %collective-permute-done.25 = f32[32,512]{1,0:T(8,128)S(1)} collective-permute-done((f32[32,512]{1,0:T(8,128)S(1)}, f32[32,512]{1,0:T(8,128)S(1)}, u32[]{:S(2)}, u32[]{:S(2)}) %collective-permute-start.25) | collective-permute-done | bytes 65568 | tf_op jit(solution)/shard_map/ppermute | solution.py:45
  86.0 2.3 %collective-permute-start.26 = (f32[32,512]{1,0:T(8,128)S(1)}, f32[32,512]{1,0:T(8,128)S(1)}, u32[]{:S(2)}, u32[]{:S(2)}) collective-permute-start(f32[32,512]{1,0:T(8,128)S(1)} %add.15.term_ref), channel_id=1, source_target_pairs={{0,192},{1,193},{2,194},{3,195},{4,196},{5,197},{6,198},{7,199},{8... | collective-permute-start | bytes 196616 | tf_op jit(solution)/shard_map/ppermute | solution.py:45
  88.4 3.5 %collective-permute-done.26.received_ref = f32[32,512]{1,0:T(8,128)S(1)} collective-permute-done((f32[32,512]{1,0:T(8,128)S(1)}, f32[32,512]{1,0:T(8,128)S(1)}, u32[]{:S(2)}, u32[]{:S(2)}) %collective-permute-start.26) | collective-permute-done | bytes 65568 | tf_op jit(solution)/shard_map/ppermute | solution.py:45
  91.9 13.1 %all_to_all.11.pieces_ref = f32[8,256,128]{2,1,0:T(8,128)S(1)} all-to-all(f32[8,256,128]{2,1,0:T(8,128)S(1)} %shard_map.68), channel_id=1, replica_groups=mesh['z'=8,'xh'=2,'core'=2,'xl'=2,'y'=4] {'xl','y'}, dimensions={0} | all-to-all | bytes 2097152 | tf_op jit(solution)/shard_map/all_to_all | solution.py:283
  105.1 6.0 %collective-permute-start.27 = (f32[8,128,128]{2,1,0:T(8,128)S(1)}, f32[8,128,128]{2,1,0:T(8,128)S(1)}, u32[]{:S(2)}, u32[]{:S(2)}) collective-permute-start(f32[8,128,128]{2,1,0:T(8,128)S(1)} %slice.59), channel_id=1, source_target_pairs={{0,8},{1,9},{2,10},{3,11},{4,12},{5,13},{6,14},{7,15},{8,0},{9,1},... | collective-permute-start | bytes 1572872 | tf_op jit(solution)/shard_map/ppermute | solution.py:45
  111.2 2.0 %shard_map.69 = f32[256,512]{1,0:T(8,128)} custom-call(s32[2]{0:T(128)S(1)} %pad_add_fusion.where_ref, f32[8,256,128]{2,1,0:T(8,128)S(1)} %all_to_all.11.pieces_ref, f32[512,512]{1,0:T(8,128)S(1)} %copy-done.1), custom_call_target="tpu_custom_call" | custom-call | flops 1024 | bytes 1048576 | tf_op jit(solution)/shard_map/pallas_call | solution.py:174
  113.2 1.6 %shard_map.70 = f32[512,512]{1,0:T(8,128)} custom-call(s32[2]{0:T(128)S(1)} %pad_add_fusion.where_ref, f32[8,256,128]{2,1,0:T(8,128)S(1)} %all_to_all.11.pieces_ref, f32[8,128,128]{2,1,0:T(8,128)S(1)} %collective-permute-done.27.partner_ref), custom_call_target="tpu_custom_call" | custom-call | flops 1024 | bytes 1048576 | tf_op jit(solution)/shard_map/pallas_call | solution.py:174
  (70 shorter events, 14.2 us)
Async XLA Ops:
  0.6 12.2 %copy-start = (f32[256,512]{1,0:T(8,128)S(1)}, f32[256,512]{1,0:T(8,128)}, u32[]{:S(2)}) copy-start(f32[256,512]{1,0:T(8,128)} %param.5) | copy-start | bytes 1572868
  0.6 7.7 %copy-start.2 = (f32[32,768]{1,0:T(8,128)S(1)}, f32[32,768]{1,0:T(8,128)}, u32[]{:S(2)}) copy-start(f32[32,768]{1,0:T(8,128)} %param.8) | copy-start | bytes 294916
  0.7 7.7 %copy-start.3 = (f32[32,512]{1,0:T(8,128)S(1)}, f32[32,512]{1,0:T(8,128)}, u32[]{:S(2)}) copy-start(f32[32,512]{1,0:T(8,128)} %param.7) | copy-start | bytes 196612
  0.7 7.7 %collective-permute-start = (f32[32,768]{1,0:T(8,128)}, f32[32,768]{1,0:T(8,128)S(1)}, u32[]{:S(2)}, u32[]{:S(2)}) collective-permute-start(f32[32,768]{1,0:T(8,128)} %param.8), channel_id=1, source_target_pairs={{0,8},{1,9},{2,10},{3,11},{4,12},{5,13},{6,14},{7,15},{8,0},{9,1},... | collective-permute-start | bytes 294920 | tf_op jit(solution)/shard_map/ppermute | solution.py:45
  4.0 8.4 %collective-permute-start.2 = (f32[32,768]{1,0:T(8,128)}, f32[32,768]{1,0:T(8,128)S(1)}, u32[]{:S(2)}, u32[]{:S(2)}) collective-permute-start(f32[32,768]{1,0:T(8,128)} %param.8), channel_id=1, source_target_pairs={{0,20},{1,21},{2,22},{3,23},{4,16},{5,17},{6,18},{7,19},{8,28},{9,... | collective-permute-start | bytes 294920 | tf_op jit(solution)/shard_map/ppermute | solution.py:45
  4.8 3.6 %collective-permute-start.1 = (f32[32,512]{1,0:T(8,128)}, f32[32,512]{1,0:T(8,128)S(1)}, u32[]{:S(2)}, u32[]{:S(2)}) collective-permute-start(f32[32,512]{1,0:T(8,128)} %param.7), channel_id=1, source_target_pairs={{0,8},{1,9},{2,10},{3,11},{4,12},{5,13},{6,14},{7,15},{8,0},{9,1},... | collective-permute-start | bytes 196616 | tf_op jit(solution)/shard_map/ppermute | solution.py:45
  5.1 7.2 %collective-permute-start.3 = (f32[32,512]{1,0:T(8,128)}, f32[32,512]{1,0:T(8,128)S(1)}, u32[]{:S(2)}, u32[]{:S(2)}) collective-permute-start(f32[32,512]{1,0:T(8,128)} %param.7), channel_id=1, source_target_pairs={{0,20},{1,21},{2,22},{3,23},{4,16},{5,17},{6,18},{7,19},{8,28},{9,... | collective-permute-start | bytes 196616 | tf_op jit(solution)/shard_map/ppermute | solution.py:45
  7.1 5.8 %copy-start.1 = (f32[512,512]{1,0:T(8,128)S(1)}, f32[512,512]{1,0:T(8,128)}, u32[]{:S(2)}) copy-start(f32[512,512]{1,0:T(8,128)} %head_ref.1) | copy-start | bytes 3145732
  8.4 9.6 %collective-permute-start.11 = (f32[64,1280]{1,0:T(8,128)S(1)}, f32[64,1280]{1,0:T(8,128)S(1)}, u32[]{:S(2)}, u32[]{:S(2)}) collective-permute-start(f32[64,1280]{1,0:T(8,128)S(1)} %maximum_maximum_fusion.refs_2_), channel_id=1, source_target_pairs={{0,32},{1,33},{2,34},{3,35},{4,36},{5,37},{6,38},{7,39},{8,232},{9... | collective-permute-start | bytes 983048 | tf_op jit(solution)/shard_map/ppermute | solution.py:45
  12.4 1.4 %collective-permute-start.4 = (f32[32,768]{1,0:T(8,128)S(1)}, f32[32,768]{1,0:T(8,128)S(1)}, u32[]{:S(2)}, u32[]{:S(2)}) collective-permute-start(f32[32,768]{1,0:T(8,128)S(1)} %collective-permute-done.2), channel_id=1, source_target_pairs={{0,8},{1,9},{2,10},{3,11},{4,12},{5,13},{6,14},{7,15},{8,0},{9,1},... | collective-permute-start | bytes 294920 | tf_op jit(solution)/shard_map/ppermute | solution.py:45
  12.4 1.4 %collective-permute-start.5 = (f32[32,512]{1,0:T(8,128)S(1)}, f32[32,512]{1,0:T(8,128)S(1)}, u32[]{:S(2)}, u32[]{:S(2)}) collective-permute-start(f32[32,512]{1,0:T(8,128)S(1)} %collective-permute-done.3), channel_id=1, source_target_pairs={{0,8},{1,9},{2,10},{3,11},{4,12},{5,13},{6,14},{7,15},{8,0},{9,1},... | collective-permute-start | bytes 196616 | tf_op jit(solution)/shard_map/ppermute | solution.py:45
  13.8 8.2 %collective-permute-start.6 = (f32[64,1280]{1,0:T(8,128)S(1)}, f32[64,1280]{1,0:T(8,128)S(1)}, u32[]{:S(2)}, u32[]{:S(2)}) collective-permute-start(f32[64,1280]{1,0:T(8,128)S(1)} %maximum_maximum_fusion.1.refs_3_), channel_id=1, source_target_pairs={{0,32},{1,33},{2,34},{3,35},{4,36},{5,37},{6,38},{7,39},{8,232},{9... | collective-permute-start | bytes 983048 | tf_op jit(solution)/shard_map/ppermute | solution.py:45
  18.0 10.7 %collective-permute-start.19 = (f32[64,1280]{1,0:T(8,128)S(1)}, f32[64,1280]{1,0:T(8,128)S(1)}, u32[]{:S(2)}, u32[]{:S(2)}) collective-permute-start(f32[64,1280]{1,0:T(8,128)S(1)} %collective-permute-done.11.refs_2_), channel_id=1, source_target_pairs={{0,8},{1,9},{2,10},{3,11},{4,12},{5,13},{6,14},{7,15},{8,0},{9,1},... | collective-permute-start | bytes 983048 | tf_op jit(solution)/shard_map/ppermute | solution.py:45
  18.1 7.4 %collective-permute-start.12 = (f32[64,1280]{1,0:T(8,128)S(1)}, f32[64,1280]{1,0:T(8,128)S(1)}, u32[]{:S(2)}, u32[]{:S(2)}) collective-permute-start(f32[64,1280]{1,0:T(8,128)S(1)} %collective-permute-done.11.refs_2_), channel_id=1, source_target_pairs={{0,32},{1,33},{2,34},{3,35},{4,36},{5,37},{6,38},{7,39},{8,232},{9... | collective-permute-start | bytes 983048 | tf_op jit(solution)/shard_map/ppermute | solution.py:45
  22.0 10.7 %collective-permute-start.18 = (f32[64,1280]{1,0:T(8,128)S(1)}, f32[64,1280]{1,0:T(8,128)S(1)}, u32[]{:S(2)}, u32[]{:S(2)}) collective-permute-start(f32[64,1280]{1,0:T(8,128)S(1)} %collective-permute-done.6.refs_2_), channel_id=1, source_target_pairs={{0,8},{1,9},{2,10},{3,11},{4,12},{5,13},{6,14},{7,15},{8,0},{9,1},... | collective-permute-start | bytes 983048 | tf_op jit(solution)/shard_map/ppermute | solution.py:45
  23.5 6.7 %collective-permute-start.7 = (f32[64,1280]{1,0:T(8,128)S(1)}, f32[64,1280]{1,0:T(8,128)S(1)}, u32[]{:S(2)}, u32[]{:S(2)}) collective-permute-start(f32[64,1280]{1,0:T(8,128)S(1)} %collective-permute-done.6.refs_2_), channel_id=1, source_target_pairs={{0,32},{1,33},{2,34},{3,35},{4,36},{5,37},{6,38},{7,39},{8,232},{9... | collective-permute-start | bytes 983048 | tf_op jit(solution)/shard_map/ppermute | solution.py:45
  25.5 10.4 %collective-permute-start.17 = (f32[64,1280]{1,0:T(8,128)S(1)}, f32[64,1280]{1,0:T(8,128)S(1)}, u32[]{:S(2)}, u32[]{:S(2)}) collective-permute-start(f32[64,1280]{1,0:T(8,128)S(1)} %collective-permute-done.12.refs_2_), channel_id=1, source_target_pairs={{0,8},{1,9},{2,10},{3,11},{4,12},{5,13},{6,14},{7,15},{8,0},{9,1},... | collective-permute-start | bytes 983048 | tf_op jit(solution)/shard_map/ppermute | solution.py:45
  27.0 7.2 %collective-permute-start.13 = (f32[64,1280]{1,0:T(8,128)S(1)}, f32[64,1280]{1,0:T(8,128)S(1)}, u32[]{:S(2)}, u32[]{:S(2)}) collective-permute-start(f32[64,1280]{1,0:T(8,128)S(1)} %collective-permute-done.12.refs_2_), channel_id=1, source_target_pairs={{0,32},{1,33},{2,34},{3,35},{4,36},{5,37},{6,38},{7,39},{8,232},{9... | collective-permute-start | bytes 983048 | tf_op jit(solution)/shard_map/ppermute | solution.py:45
  30.2 10.0 %collective-permute-start.16 = (f32[64,1280]{1,0:T(8,128)S(1)}, f32[64,1280]{1,0:T(8,128)S(1)}, u32[]{:S(2)}, u32[]{:S(2)}) collective-permute-start(f32[64,1280]{1,0:T(8,128)S(1)} %collective-permute-done.7.refs_2_), channel_id=1, source_target_pairs={{0,8},{1,9},{2,10},{3,11},{4,12},{5,13},{6,14},{7,15},{8,0},{9,1},... | collective-permute-start | bytes 983048 | tf_op jit(solution)/shard_map/ppermute | solution.py:45
  31.8 6.2 %collective-permute-start.8 = (f32[64,1280]{1,0:T(8,128)S(1)}, f32[64,1280]{1,0:T(8,128)S(1)}, u32[]{:S(2)}, u32[]{:S(2)}) collective-permute-start(f32[64,1280]{1,0:T(8,128)S(1)} %collective-permute-done.7.refs_2_), channel_id=1, source_target_pairs={{0,32},{1,33},{2,34},{3,35},{4,36},{5,37},{6,38},{7,39},{8,232},{9... | collective-permute-start | bytes 983048 | tf_op jit(solution)/shard_map/ppermute | solution.py:45
  34.2 9.0 %collective-permute-start.14 = (f32[32,1280]{1,0:T(8,128)S(1)}, f32[32,1280]{1,0:T(8,128)S(1)}, u32[]{:S(2)}, u32[]{:S(2)}) collective-permute-start(f32[32,1280]{1,0:T(8,128)S(1)} %slice.49), channel_id=1, source_target_pairs={{0,32},{1,33},{2,34},{3,35},{4,36},{5,37},{6,38},{7,39},{8,232},{9... | collective-permute-start | bytes 491528 | tf_op jit(solution)/shard_map/ppermute | solution.py:45
  36.0 5.8 %collective-permute-start.15 = (f32[64,1280]{1,0:T(8,128)S(1)}, f32[64,1280]{1,0:T(8,128)S(1)}, u32[]{:S(2)}, u32[]{:S(2)}) collective-permute-start(f32[64,1280]{1,0:T(8,128)S(1)} %collective-permute-done.13.refs_2_), channel_id=1, source_target_pairs={{0,8},{1,9},{2,10},{3,11},{4,12},{5,13},{6,14},{7,15},{8,0},{9,1},... | collective-permute-start | bytes 983048 | tf_op jit(solution)/shard_map/ppermute | solution.py:45
  38.0 7.0 %collective-permute-start.9 = (f32[32,1280]{1,0:T(8,128)S(1)}, f32[32,1280]{1,0:T(8,128)S(1)}, u32[]{:S(2)}, u32[]{:S(2)}) collective-permute-start(f32[32,1280]{1,0:T(8,128)S(1)} %slice.48), channel_id=1, source_target_pairs={{0,32},{1,33},{2,34},{3,35},{4,36},{5,37},{6,38},{7,39},{8,232},{9... | collective-permute-start | bytes 491528 | tf_op jit(solution)/shard_map/ppermute | solution.py:45
  39.9 3.6 %collective-permute-start.10 = (f32[64,1280]{1,0:T(8,128)S(1)}, f32[64,1280]{1,0:T(8,128)S(1)}, u32[]{:S(2)}, u32[]{:S(2)}) collective-permute-start(f32[64,1280]{1,0:T(8,128)S(1)} %collective-permute-done.8.refs_2_), channel_id=1, source_target_pairs={{0,8},{1,9},{2,10},{3,11},{4,12},{5,13},{6,14},{7,15},{8,0},{9,1},... | collective-permute-start | bytes 983048 | tf_op jit(solution)/shard_map/ppermute | solution.py:45
  43.2 3.5 %collective-permute-start.21 = (f32[32,1280]{1,0:T(8,128)S(1)}, f32[32,1280]{1,0:T(8,128)S(1)}, u32[]{:S(2)}, u32[]{:S(2)}) collective-permute-start(f32[32,1280]{1,0:T(8,128)S(1)} %collective-permute-done.14.refs_2_), channel_id=1, source_target_pairs={{0,8},{1,9},{2,10},{3,11},{4,12},{5,13},{6,14},{7,15},{8,0},{9,1},... | collective-permute-start | bytes 491528 | tf_op jit(solution)/shard_map/ppermute | solution.py:45
  45.0 3.2 %collective-permute-start.20 = (f32[32,1280]{1,0:T(8,128)S(1)}, f32[32,1280]{1,0:T(8,128)S(1)}, u32[]{:S(2)}, u32[]{:S(2)}) collective-permute-start(f32[32,1280]{1,0:T(8,128)S(1)} %collective-permute-done.9.refs_3_), channel_id=1, source_target_pairs={{0,8},{1,9},{2,10},{3,11},{4,12},{5,13},{6,14},{7,15},{8,0},{9,1},... | collective-permute-start | bytes 491528 | tf_op jit(solution)/shard_map/ppermute | solution.py:45
  71.7 2.3 %collective-permute-start.22 = (f32[32,512]{1,0:T(8,128)S(1)}, f32[32,512]{1,0:T(8,128)S(1)}, u32[]{:S(2)}, u32[]{:S(2)}) collective-permute-start(f32[32,512]{1,0:T(8,128)S(1)} %constant_dynamic-slice_fusion), channel_id=1, source_target_pairs={{0,8},{1,9},{2,10},{3,11},{4,12},{5,13},{6,14},{7,15},{8,0},{9,1},... | collective-permute-start | bytes 196616 | tf_op jit(solution)/shard_map/ppermute | solution.py:45
  74.1 4.4 %collective-permute-start.23 = (f32[32,512]{1,0:T(8,128)S(1)}, f32[32,512]{1,0:T(8,128)S(1)}, u32[]{:S(2)}, u32[]{:S(2)}) collective-permute-start(f32[32,512]{1,0:T(8,128)S(1)} %dynamic-slice_add_fusion), channel_id=1, source_target_pairs={{0,20},{1,21},{2,22},{3,23},{4,16},{5,17},{6,18},{7,19},{8,28},{9,... | collective-permute-start | bytes 196616 | tf_op jit(solution)/shard_map/ppermute | solution.py:45
  78.5 3.2 %collective-permute-start.24 = (f32[32,512]{1,0:T(8,128)S(1)}, f32[32,512]{1,0:T(8,128)S(1)}, u32[]{:S(2)}, u32[]{:S(2)}) collective-permute-start(f32[32,512]{1,0:T(8,128)S(1)} %add.13), channel_id=1, source_target_pairs={{0,32},{1,33},{2,34},{3,35},{4,36},{5,37},{6,38},{7,39},{8,40},{9,... | collective-permute-start | bytes 196616 | tf_op jit(solution)/shard_map/ppermute | solution.py:45
  81.7 4.2 %collective-permute-start.25 = (f32[32,512]{1,0:T(8,128)S(1)}, f32[32,512]{1,0:T(8,128)S(1)}, u32[]{:S(2)}, u32[]{:S(2)}) collective-permute-start(f32[32,512]{1,0:T(8,128)S(1)} %add.14), channel_id=1, source_target_pairs={{0,64},{1,65},{2,66},{3,67},{4,68},{5,69},{6,70},{7,71},{8,72},{9,... | collective-permute-start | bytes 196616 | tf_op jit(solution)/shard_map/ppermute | solution.py:45
  86.0 5.9 %collective-permute-start.26 = (f32[32,512]{1,0:T(8,128)S(1)}, f32[32,512]{1,0:T(8,128)S(1)}, u32[]{:S(2)}, u32[]{:S(2)}) collective-permute-start(f32[32,512]{1,0:T(8,128)S(1)} %add.15.term_ref), channel_id=1, source_target_pairs={{0,192},{1,193},{2,194},{3,195},{4,196},{5,197},{6,198},{7,199},{8... | collective-permute-start | bytes 196616 | tf_op jit(solution)/shard_map/ppermute | solution.py:45
  105.1 8.0 %collective-permute-start.27 = (f32[8,128,128]{2,1,0:T(8,128)S(1)}, f32[8,128,128]{2,1,0:T(8,128)S(1)}, u32[]{:S(2)}, u32[]{:S(2)}) collective-permute-start(f32[8,128,128]{2,1,0:T(8,128)S(1)} %slice.59), channel_id=1, source_target_pairs={{0,8},{1,9},{2,10},{3,11},{4,12},{5,13},{6,14},{7,15},{8,0},{9,1},... | collective-permute-start | bytes 1572872 | tf_op jit(solution)/shard_map/ppermute | solution.py:45

commit v7 on v6

--- a/solution.py
+++ b/solution.py
@@ -276,9 +276,12 @@
 
     piece = jnp.concatenate([gap_text[: ROWS // 2], gap_text[ROWS // 2 :]], axis=1)
     term = halved(dot(gap_text, image_student, ((0,), (0,))), starts, CORE)
-    for pairs in (X_FLIP,) + Z_FOLD[:-1]:
+    for pairs in (X_FLIP, Z_FOLD[0]):
         term = term + move(term, pairs)
-    packed = pack(piece, term, move(term, Z_FOLD[-1]), scale_s / math.sqrt(batch))
+    halves = [term[: SHARD // 2], term[SHARD // 2 :]]
+    halves = [half + move(half, pairs) for half, pairs in zip(halves, Z_FOLD[1:])]
+    received = [move(half, pairs) for half, pairs in zip(halves, Z_FOLD[:0:-1])]
+    packed = pack(piece, jnp.concatenate(halves), jnp.concatenate(received), scale_s / math.sqrt(batch))
 
     pieces = lax.all_to_all(packed, ("xl", "y"), 0, 0, tiled=True)
     partner = move(pieces[:, ROWS // 2 :], CORE)

time: 115 us -> 118 us (1.026)
  starting transfers between devices: 46 us -> 48.7 us
    ppermute x28 -> x30, starting transfers between devices: 46 us -> 48.7 us  [move(): return lax.ppermute(array, AXES, pairs)]
    ppermute x28 -> x30, waiting for transfers between devices: 13.8 us -> 14.9 us  [move(): return lax.ppermute(array, AXES, pairs)]
  transfers between devices with their start and end apart: 28 -> 30, of which waited for: 9 -> 10; matrix products, arithmetic and copies ran while one was open for 2% -> 2% of each run, Pallas kernels for 12% -> 11%
where the time goes in v7:
time: 118 us
  starting transfers between devices  48.7 us (41%)
  blocking collectives  32.6 us (28%)
  Pallas kernels  17.4 us (15%)
  waiting for transfers between devices  14.9 us (13%)
  other arithmetic  2.62 us (2%)
    ppermute x30, starting transfers between devices, move(): return lax.ppermute(array, AXES, pairs)  48.7 us
    all_to_all x1, blocking collectives, shards(): got = lax.all_to_all(both, ('xl', 'y'), 0, 0, tiled=True)  19.8 us
    ppermute x30, waiting for transfers between devices, move(): return lax.ppermute(array, AXES, pairs)  14.9 us
    pallas_call x9, Pallas kernels, add_texts(): pl.pallas_call(body, out_shape=shapes, in_specs=in_specs, out_specs=[vmem...  13.8 us
    all_to_all x1, blocking collectives, shards(): pieces = lax.all_to_all(packed, ('xl', 'y'), 0, 0, tiled=True)  12.7 us
    pallas_call x3, Pallas kernels, small_call(): pl.pallas_call(body, out_shape=jax.ShapeDtypeStruct(shape, jnp.float32),...  3.66 us
  transfers between devices with their start and end apart: 30, of which 10 were waited for; matrix products, arithmetic and copies ran while one was open for 2% of the time, Pallas kernels for 11%

profile of v7, /device:TPU:1, one launch (start us, length us, event | category | flops | bytes accessed | tf_op | source)
XLA Modules:
  0.0 118.3 jit_solution(10819419596584508640)
XLA Ops:
  0.7 3.3 %collective-permute-start = (f32[32,768]{1,0:T(8,128)}, f32[32,768]{1,0:T(8,128)S(1)}, u32[]{:S(2)}, u32[]{:S(2)}) collective-permute-start(f32[32,768]{1,0:T(8,128)} %param.8), channel_id=1, source_target_pairs={{0,8},{1,9},{2,10},{3,11},{4,12},{5,13},{6,14},{7,15},{8,0},{9,1},... | collective-permute-start | bytes 294920 | tf_op jit(solution)/shard_map/ppermute | solution.py:45
  5.1 1.9 %collective-permute-start.3 = (f32[32,512]{1,0:T(8,128)}, f32[32,512]{1,0:T(8,128)S(1)}, u32[]{:S(2)}, u32[]{:S(2)}) collective-permute-start(f32[32,512]{1,0:T(8,128)} %param.7), channel_id=1, source_target_pairs={{0,20},{1,21},{2,22},{3,23},{4,16},{5,17},{6,18},{7,19},{8,28},{9,... | collective-permute-start | bytes 196616 | tf_op jit(solution)/shard_map/ppermute | solution.py:45
  8.4 3.9 %collective-permute-start.11 = (f32[64,1280]{1,0:T(8,128)S(1)}, f32[64,1280]{1,0:T(8,128)S(1)}, u32[]{:S(2)}, u32[]{:S(2)}) collective-permute-start(f32[64,1280]{1,0:T(8,128)S(1)} %maximum_maximum_fusion.refs_2_), channel_id=1, source_target_pairs={{0,32},{1,33},{2,34},{3,35},{4,36},{5,37},{6,38},{7,39},{8,232},{9... | collective-permute-start | bytes 983048 | tf_op jit(solution)/shard_map/ppermute | solution.py:45
  13.8 4.2 %collective-permute-start.6 = (f32[64,1280]{1,0:T(8,128)S(1)}, f32[64,1280]{1,0:T(8,128)S(1)}, u32[]{:S(2)}, u32[]{:S(2)}) collective-permute-start(f32[64,1280]{1,0:T(8,128)S(1)} %maximum_maximum_fusion.1.refs_3_), channel_id=1, source_target_pairs={{0,32},{1,33},{2,34},{3,35},{4,36},{5,37},{6,38},{7,39},{8,232},{9... | collective-permute-start | bytes 983048 | tf_op jit(solution)/shard_map/ppermute | solution.py:45
  18.1 1.7 %collective-permute-start.12 = (f32[64,1280]{1,0:T(8,128)S(1)}, f32[64,1280]{1,0:T(8,128)S(1)}, u32[]{:S(2)}, u32[]{:S(2)}) collective-permute-start(f32[64,1280]{1,0:T(8,128)S(1)} %collective-permute-done.11.refs_2_), channel_id=1, source_target_pairs={{0,32},{1,33},{2,34},{3,35},{4,36},{5,37},{6,38},{7,39},{8,232},{9... | collective-permute-start | bytes 983048 | tf_op jit(solution)/shard_map/ppermute | solution.py:45
  22.0 1.5 %collective-permute-start.18 = (f32[64,1280]{1,0:T(8,128)S(1)}, f32[64,1280]{1,0:T(8,128)S(1)}, u32[]{:S(2)}, u32[]{:S(2)}) collective-permute-start(f32[64,1280]{1,0:T(8,128)S(1)} %collective-permute-done.6.refs_2_), channel_id=1, source_target_pairs={{0,8},{1,9},{2,10},{3,11},{4,12},{5,13},{6,14},{7,15},{8,0},{9,1},... | collective-permute-start | bytes 983048 | tf_op jit(solution)/shard_map/ppermute | solution.py:45
  23.5 1.7 %collective-permute-start.7 = (f32[64,1280]{1,0:T(8,128)S(1)}, f32[64,1280]{1,0:T(8,128)S(1)}, u32[]{:S(2)}, u32[]{:S(2)}) collective-permute-start(f32[64,1280]{1,0:T(8,128)S(1)} %collective-permute-done.6.refs_2_), channel_id=1, source_target_pairs={{0,32},{1,33},{2,34},{3,35},{4,36},{5,37},{6,38},{7,39},{8,232},{9... | collective-permute-start | bytes 983048 | tf_op jit(solution)/shard_map/ppermute | solution.py:45
  25.5 1.5 %collective-permute-start.17 = (f32[64,1280]{1,0:T(8,128)S(1)}, f32[64,1280]{1,0:T(8,128)S(1)}, u32[]{:S(2)}, u32[]{:S(2)}) collective-permute-start(f32[64,1280]{1,0:T(8,128)S(1)} %collective-permute-done.12.refs_2_), channel_id=1, source_target_pairs={{0,8},{1,9},{2,10},{3,11},{4,12},{5,13},{6,14},{7,15},{8,0},{9,1},... | collective-permute-start | bytes 983048 | tf_op jit(solution)/shard_map/ppermute | solution.py:45
  27.0 1.7 %collective-permute-start.13 = (f32[64,1280]{1,0:T(8,128)S(1)}, f32[64,1280]{1,0:T(8,128)S(1)}, u32[]{:S(2)}, u32[]{:S(2)}) collective-permute-start(f32[64,1280]{1,0:T(8,128)S(1)} %collective-permute-done.12.refs_2_), channel_id=1, source_target_pairs={{0,32},{1,33},{2,34},{3,35},{4,36},{5,37},{6,38},{7,39},{8,232},{9... | collective-permute-start | bytes 983048 | tf_op jit(solution)/shard_map/ppermute | solution.py:45
  28.7 1.5 %add_texts.10 = (f32[256,128]{1,0:T(8,128)S(1)}, f32[256,512]{1,0:T(8,128)S(1)}, f32[256,512]{1,0:T(8,128)S(1)}) custom-call(f32[256,512]{1,0:T(8,128)S(1)} %convolution_multiply_fusion.refs_0_.refs_1_, f32[256,768]{1,0:T(8,128)S(1)} %broadcast_multiply_fusion.refs_1_.refs_2_, f32[64,1280]{1,0:T(8,128)S(1)} %collective-permute-done.11.refs_2_, ...), custom_call_target="tpu_custom_call" | custom-call | flops 18119393280 | bytes 4194304 | tf_op jit(solution)/shard_map/add_texts/pallas_call | solution.py:152
  30.2 1.6 %collective-permute-start.16 = (f32[64,1280]{1,0:T(8,128)S(1)}, f32[64,1280]{1,0:T(8,128)S(1)}, u32[]{:S(2)}, u32[]{:S(2)}) collective-permute-start(f32[64,1280]{1,0:T(8,128)S(1)} %collective-permute-done.7.refs_2_), channel_id=1, source_target_pairs={{0,8},{1,9},{2,10},{3,11},{4,12},{5,13},{6,14},{7,15},{8,0},{9,1},... | collective-permute-start | bytes 983048 | tf_op jit(solution)/shard_map/ppermute | solution.py:45
  32.7 1.5 %add_texts.11 = (f32[256,128]{1,0:T(8,128)S(1)}, f32[256,512]{1,0:T(8,128)S(1)}, f32[256,512]{1,0:T(8,128)S(1)}) custom-call(f32[256,512]{1,0:T(8,128)S(1)} %convolution_multiply_fusion.refs_0_.refs_1_, f32[256,768]{1,0:T(8,128)S(1)} %broadcast_multiply_fusion.refs_1_.refs_2_, f32[64,1280]{1,0:T(8,128)S(1)} %collective-permute-done.6.refs_2_, ...), custom_call_target="tpu_custom_call" | custom-call | flops 18119393280 | bytes 4194304 | tf_op jit(solution)/shard_map/add_texts/pallas_call | solution.py:152
  34.2 1.8 %collective-permute-start.14 = (f32[32,1280]{1,0:T(8,128)S(1)}, f32[32,1280]{1,0:T(8,128)S(1)}, u32[]{:S(2)}, u32[]{:S(2)}) collective-permute-start(f32[32,1280]{1,0:T(8,128)S(1)} %slice.57), channel_id=1, source_target_pairs={{0,32},{1,33},{2,34},{3,35},{4,36},{5,37},{6,38},{7,39},{8,232},{9... | collective-permute-start | bytes 491528 | tf_op jit(solution)/shard_map/ppermute | solution.py:45
  36.0 1.5 %add_texts.12 = (f32[256,128]{1,0:T(8,128)S(1)}, f32[256,512]{1,0:T(8,128)S(1)}, f32[256,512]{1,0:T(8,128)S(1)}) custom-call(f32[256,512]{1,0:T(8,128)S(1)} %convolution_multiply_fusion.refs_0_.refs_1_, f32[256,768]{1,0:T(8,128)S(1)} %broadcast_multiply_fusion.refs_1_.refs_2_, f32[64,1280]{1,0:T(8,128)S(1)} %collective-permute-done.12.refs_2_, ...), custom_call_target="tpu_custom_call" | custom-call | flops 18119393280 | bytes 4194304 | tf_op jit(solution)/shard_map/add_texts/pallas_call | solution.py:152
  38.0 1.9 %collective-permute-start.9 = (f32[32,1280]{1,0:T(8,128)S(1)}, f32[32,1280]{1,0:T(8,128)S(1)}, u32[]{:S(2)}, u32[]{:S(2)}) collective-permute-start(f32[32,1280]{1,0:T(8,128)S(1)} %slice.56), channel_id=1, source_target_pairs={{0,32},{1,33},{2,34},{3,35},{4,36},{5,37},{6,38},{7,39},{8,232},{9... | collective-permute-start | bytes 491528 | tf_op jit(solution)/shard_map/ppermute | solution.py:45
  40.3 1.5 %add_texts.13 = (f32[256,128]{1,0:T(8,128)S(1)}, f32[256,512]{1,0:T(8,128)S(1)}, f32[256,512]{1,0:T(8,128)S(1)}) custom-call(f32[256,512]{1,0:T(8,128)S(1)} %convolution_multiply_fusion.refs_0_.refs_1_, f32[256,768]{1,0:T(8,128)S(1)} %broadcast_multiply_fusion.refs_1_.refs_2_, f32[64,1280]{1,0:T(8,128)S(1)} %collective-permute-done.7.refs_2_, ...), custom_call_target="tpu_custom_call" | custom-call | flops 18119393280 | bytes 4194304 | tf_op jit(solution)/shard_map/add_texts/pallas_call | solution.py:152
  41.7 1.5 %add_texts.14 = (f32[256,128]{1,0:T(8,128)S(1)}, f32[256,512]{1,0:T(8,128)S(1)}, f32[256,512]{1,0:T(8,128)S(1)}) custom-call(f32[256,512]{1,0:T(8,128)S(1)} %convolution_multiply_fusion.refs_0_.refs_1_, f32[256,768]{1,0:T(8,128)S(1)} %broadcast_multiply_fusion.refs_1_.refs_2_, f32[64,1280]{1,0:T(8,128)S(1)} %collective-permute-done.13.refs_2_, ...), custom_call_target="tpu_custom_call" | custom-call | flops 18119393280 | bytes 4194304 | tf_op jit(solution)/shard_map/add_texts/pallas_call | solution.py:152
  45.0 1.7 %collective-permute-start.20 = (f32[32,1280]{1,0:T(8,128)S(1)}, f32[32,1280]{1,0:T(8,128)S(1)}, u32[]{:S(2)}, u32[]{:S(2)}) collective-permute-start(f32[32,1280]{1,0:T(8,128)S(1)} %collective-permute-done.9.refs_3_), channel_id=1, source_target_pairs={{0,8},{1,9},{2,10},{3,11},{4,12},{5,13},{6,14},{7,15},{8,0},{9,1},... | collective-permute-start | bytes 491528 | tf_op jit(solution)/shard_map/ppermute | solution.py:45
  48.2 2.3 %add_texts.17 = f32[8,264,128]{2,1,0:T(8,128)S(1)} custom-call(s32[8]{0:T(128)S(1)} %iota_xor_fusion.refs_0_, f32[256,512]{1,0:T(8,128)S(1)} %convolution_multiply_fusion.refs_0_.refs_1_, f32[256,768]{1,0:T(8,128)S(1)} %broadcast_multiply_fusion.refs_1_.refs_2_, f32[32,1280]{1,0:T(8,128)S(1)} %collective-permute-done.9.refs_3_, ...), custom_call_target="tpu_custom_call" | custom-call | flops 9059696640 | bytes 4194304 | tf_op jit(solution)/shard_map/add_texts/pallas_call | solution.py:152
  50.5 19.8 %all_to_all.10 = f32[8,264,128]{2,1,0:T(8,128)S(1)} all-to-all(f32[8,264,128]{2,1,0:T(8,128)S(1)} %add_texts.17), channel_id=1, replica_groups=mesh['z'=8,'xh'=2,'core'=2,'xl'=2,'y'=4] {'xl','y'}, dimensions={0} | all-to-all | bytes 2162688 | tf_op jit(solution)/shard_map/all_to_all | solution.py:263
  74.1 1.8 %collective-permute-start.23 = (f32[32,512]{1,0:T(8,128)S(1)}, f32[32,512]{1,0:T(8,128)S(1)}, u32[]{:S(2)}, u32[]{:S(2)}) collective-permute-start(f32[32,512]{1,0:T(8,128)S(1)} %dynamic-slice_add_fusion), channel_id=1, source_target_pairs={{0,20},{1,21},{2,22},{3,23},{4,16},{5,17},{6,18},{7,19},{8,28},{9,... | collective-permute-start | bytes 196616 | tf_op jit(solution)/shard_map/ppermute | solution.py:45
  75.9 2.6 %collective-permute-done.23 = f32[32,512]{1,0:T(8,128)S(1)} collective-permute-done((f32[32,512]{1,0:T(8,128)S(1)}, f32[32,512]{1,0:T(8,128)S(1)}, u32[]{:S(2)}, u32[]{:S(2)}) %collective-permute-start.23) | collective-permute-done | bytes 65568 | tf_op jit(solution)/shard_map/ppermute | solution.py:45
  78.7 3.1 %collective-permute-done.24 = f32[32,512]{1,0:T(8,128)S(1)} collective-permute-done((f32[32,512]{1,0:T(8,128)S(1)}, f32[32,512]{1,0:T(8,128)S(1)}, u32[]{:S(2)}, u32[]{:S(2)}) %collective-permute-start.24) | collective-permute-done | bytes 65568 | tf_op jit(solution)/shard_map/ppermute | solution.py:45
  81.8 2.6 %collective-permute-start.25 = (f32[16,512]{1,0:T(8,128)S(1)}, f32[16,512]{1,0:T(8,128)S(1)}, u32[]{:S(2)}, u32[]{:S(2)}) collective-permute-start(f32[16,512]{1,0:T(8,128)S(1)} %get-tuple-element.88), channel_id=1, source_target_pairs={{0,64},{1,65},{2,66},{3,67},{4,68},{5,69},{6,70},{7,71},{8,72},{9,... | collective-permute-start | bytes 98312 | tf_op jit(solution)/shard_map/ppermute | solution.py:45
  84.3 2.1 %collective-permute-start.26 = (f32[16,512]{1,0:T(8,128)S(1)}, f32[16,512]{1,0:T(8,128)S(1)}, u32[]{:S(2)}, u32[]{:S(2)}) collective-permute-start(f32[16,512]{1,0:T(8,128)S(1)} %get-tuple-element.89), channel_id=1, source_target_pairs={{0,192},{1,193},{2,194},{3,195},{4,196},{5,197},{6,198},{7,199},{8... | collective-permute-start | bytes 98312 | tf_op jit(solution)/shard_map/ppermute | solution.py:45
  86.5 2.7 %collective-permute-done.26 = f32[16,512]{1,0:T(8,128)S(1)} collective-permute-done((f32[16,512]{1,0:T(8,128)S(1)}, f32[16,512]{1,0:T(8,128)S(1)}, u32[]{:S(2)}, u32[]{:S(2)}) %collective-permute-start.26) | collective-permute-done | bytes 32800 | tf_op jit(solution)/shard_map/ppermute | solution.py:45
  89.2 2.2 %collective-permute-start.27 = (f32[16,512]{1,0:T(8,128)S(1)}, f32[16,512]{1,0:T(8,128)S(1)}, u32[]{:S(2)}, u32[]{:S(2)}) collective-permute-start(f32[16,512]{1,0:T(8,128)S(1)} %get-tuple-element.86), channel_id=1, source_target_pairs={{0,192},{1,193},{2,194},{3,195},{4,196},{5,197},{6,198},{7,199},{8... | collective-permute-start | bytes 98312 | tf_op jit(solution)/shard_map/ppermute | solution.py:45
  91.5 2.7 %collective-permute-done.27 = f32[16,512]{1,0:T(8,128)S(1)} collective-permute-done((f32[16,512]{1,0:T(8,128)S(1)}, f32[16,512]{1,0:T(8,128)S(1)}, u32[]{:S(2)}, u32[]{:S(2)}) %collective-permute-start.27) | collective-permute-done | bytes 32800 | tf_op jit(solution)/shard_map/ppermute | solution.py:45
  95.2 12.7 %all_to_all.11.pieces_ref = f32[8,256,128]{2,1,0:T(8,128)S(1)} all-to-all(f32[8,256,128]{2,1,0:T(8,128)S(1)} %shard_map.68), channel_id=1, replica_groups=mesh['z'=8,'xh'=2,'core'=2,'xl'=2,'y'=4] {'xl','y'}, dimensions={0} | all-to-all | bytes 2097152 | tf_op jit(solution)/shard_map/all_to_all | solution.py:286
  108.0 6.7 %collective-permute-start.29 = (f32[8,128,128]{2,1,0:T(8,128)S(1)}, f32[8,128,128]{2,1,0:T(8,128)S(1)}, u32[]{:S(2)}, u32[]{:S(2)}) collective-permute-start(f32[8,128,128]{2,1,0:T(8,128)S(1)} %slice.69), channel_id=1, source_target_pairs={{0,8},{1,9},{2,10},{3,11},{4,12},{5,13},{6,14},{7,15},{8,0},{9,1},... | collective-permute-start | bytes 1572872 | tf_op jit(solution)/shard_map/ppermute | solution.py:45
  114.7 2.0 %shard_map.69 = f32[256,512]{1,0:T(8,128)} custom-call(s32[2]{0:T(128)S(1)} %pad_add_fusion.where_ref, f32[8,256,128]{2,1,0:T(8,128)S(1)} %all_to_all.11.pieces_ref, f32[512,512]{1,0:T(8,128)S(1)} %copy-done.1), custom_call_target="tpu_custom_call" | custom-call | flops 1024 | bytes 1048576 | tf_op jit(solution)/shard_map/pallas_call | solution.py:174
  116.7 1.6 %shard_map.70 = f32[512,512]{1,0:T(8,128)} custom-call(s32[2]{0:T(128)S(1)} %pad_add_fusion.where_ref, f32[8,256,128]{2,1,0:T(8,128)S(1)} %all_to_all.11.pieces_ref, f32[8,128,128]{2,1,0:T(8,128)S(1)} %collective-permute-done.29.partner_ref), custom_call_target="tpu_custom_call" | custom-call | flops 1024 | bytes 1048576 | tf_op jit(solution)/shard_map/pallas_call | solution.py:174
  (77 shorter events, 16.7 us)
Async XLA Ops:
  0.6 12.2 %copy-start = (f32[256,512]{1,0:T(8,128)S(1)}, f32[256,512]{1,0:T(8,128)}, u32[]{:S(2)}) copy-start(f32[256,512]{1,0:T(8,128)} %param.5) | copy-start | bytes 1572868
  0.6 7.7 %copy-start.2 = (f32[32,768]{1,0:T(8,128)S(1)}, f32[32,768]{1,0:T(8,128)}, u32[]{:S(2)}) copy-start(f32[32,768]{1,0:T(8,128)} %param.8) | copy-start | bytes 294916
  0.7 7.7 %collective-permute-start = (f32[32,768]{1,0:T(8,128)}, f32[32,768]{1,0:T(8,128)S(1)}, u32[]{:S(2)}, u32[]{:S(2)}) collective-permute-start(f32[32,768]{1,0:T(8,128)} %param.8), channel_id=1, source_target_pairs={{0,8},{1,9},{2,10},{3,11},{4,12},{5,13},{6,14},{7,15},{8,0},{9,1},... | collective-permute-start | bytes 294920 | tf_op jit(solution)/shard_map/ppermute | solution.py:45
  4.0 8.4 %collective-permute-start.2 = (f32[32,768]{1,0:T(8,128)}, f32[32,768]{1,0:T(8,128)S(1)}, u32[]{:S(2)}, u32[]{:S(2)}) collective-permute-start(f32[32,768]{1,0:T(8,128)} %param.8), channel_id=1, source_target_pairs={{0,20},{1,21},{2,22},{3,23},{4,16},{5,17},{6,18},{7,19},{8,28},{9,... | collective-permute-start | bytes 294920 | tf_op jit(solution)/shard_map/ppermute | solution.py:45
  4.8 3.6 %collective-permute-start.1 = (f32[32,512]{1,0:T(8,128)}, f32[32,512]{1,0:T(8,128)S(1)}, u32[]{:S(2)}, u32[]{:S(2)}) collective-permute-start(f32[32,512]{1,0:T(8,128)} %param.7), channel_id=1, source_target_pairs={{0,8},{1,9},{2,10},{3,11},{4,12},{5,13},{6,14},{7,15},{8,0},{9,1},... | collective-permute-start | bytes 196616 | tf_op jit(solution)/shard_map/ppermute | solution.py:45
  5.1 7.2 %collective-permute-start.3 = (f32[32,512]{1,0:T(8,128)}, f32[32,512]{1,0:T(8,128)S(1)}, u32[]{:S(2)}, u32[]{:S(2)}) collective-permute-start(f32[32,512]{1,0:T(8,128)} %param.7), channel_id=1, source_target_pairs={{0,20},{1,21},{2,22},{3,23},{4,16},{5,17},{6,18},{7,19},{8,28},{9,... | collective-permute-start | bytes 196616 | tf_op jit(solution)/shard_map/ppermute | solution.py:45
  8.4 9.6 %collective-permute-start.11 = (f32[64,1280]{1,0:T(8,128)S(1)}, f32[64,1280]{1,0:T(8,128)S(1)}, u32[]{:S(2)}, u32[]{:S(2)}) collective-permute-start(f32[64,1280]{1,0:T(8,128)S(1)} %maximum_maximum_fusion.refs_2_), channel_id=1, source_target_pairs={{0,32},{1,33},{2,34},{3,35},{4,36},{5,37},{6,38},{7,39},{8,232},{9... | collective-permute-start | bytes 983048 | tf_op jit(solution)/shard_map/ppermute | solution.py:45
  12.4 1.4 %collective-permute-start.4 = (f32[32,768]{1,0:T(8,128)S(1)}, f32[32,768]{1,0:T(8,128)S(1)}, u32[]{:S(2)}, u32[]{:S(2)}) collective-permute-start(f32[32,768]{1,0:T(8,128)S(1)} %collective-permute-done.2), channel_id=1, source_target_pairs={{0,8},{1,9},{2,10},{3,11},{4,12},{5,13},{6,14},{7,15},{8,0},{9,1},... | collective-permute-start | bytes 294920 | tf_op jit(solution)/shard_map/ppermute | solution.py:45
  12.4 1.4 %collective-permute-start.5 = (f32[32,512]{1,0:T(8,128)S(1)}, f32[32,512]{1,0:T(8,128)S(1)}, u32[]{:S(2)}, u32[]{:S(2)}) collective-permute-start(f32[32,512]{1,0:T(8,128)S(1)} %collective-permute-done.3), channel_id=1, source_target_pairs={{0,8},{1,9},{2,10},{3,11},{4,12},{5,13},{6,14},{7,15},{8,0},{9,1},... | collective-permute-start | bytes 196616 | tf_op jit(solution)/shard_map/ppermute | solution.py:45
  13.8 8.2 %collective-permute-start.6 = (f32[64,1280]{1,0:T(8,128)S(1)}, f32[64,1280]{1,0:T(8,128)S(1)}, u32[]{:S(2)}, u32[]{:S(2)}) collective-permute-start(f32[64,1280]{1,0:T(8,128)S(1)} %maximum_maximum_fusion.1.refs_3_), channel_id=1, source_target_pairs={{0,32},{1,33},{2,34},{3,35},{4,36},{5,37},{6,38},{7,39},{8,232},{9... | collective-permute-start | bytes 983048 | tf_op jit(solution)/shard_map/ppermute | solution.py:45
  18.0 10.7 %collective-permute-start.19 = (f32[64,1280]{1,0:T(8,128)S(1)}, f32[64,1280]{1,0:T(8,128)S(1)}, u32[]{:S(2)}, u32[]{:S(2)}) collective-permute-start(f32[64,1280]{1,0:T(8,128)S(1)} %collective-permute-done.11.refs_2_), channel_id=1, source_target_pairs={{0,8},{1,9},{2,10},{3,11},{4,12},{5,13},{6,14},{7,15},{8,0},{9,1},... | collective-permute-start | bytes 983048 | tf_op jit(solution)/shard_map/ppermute | solution.py:45
  18.1 7.4 %collective-permute-start.12 = (f32[64,1280]{1,0:T(8,128)S(1)}, f32[64,1280]{1,0:T(8,128)S(1)}, u32[]{:S(2)}, u32[]{:S(2)}) collective-permute-start(f32[64,1280]{1,0:T(8,128)S(1)} %collective-permute-done.11.refs_2_), channel_id=1, source_target_pairs={{0,32},{1,33},{2,34},{3,35},{4,36},{5,37},{6,38},{7,39},{8,232},{9... | collective-permute-start | bytes 983048 | tf_op jit(solution)/shard_map/ppermute | solution.py:45
  22.0 10.7 %collective-permute-start.18 = (f32[64,1280]{1,0:T(8,128)S(1)}, f32[64,1280]{1,0:T(8,128)S(1)}, u32[]{:S(2)}, u32[]{:S(2)}) collective-permute-start(f32[64,1280]{1,0:T(8,128)S(1)} %collective-permute-done.6.refs_2_), channel_id=1, source_target_pairs={{0,8},{1,9},{2,10},{3,11},{4,12},{5,13},{6,14},{7,15},{8,0},{9,1},... | collective-permute-start | bytes 983048 | tf_op jit(solution)/shard_map/ppermute | solution.py:45
  23.5 6.7 %collective-permute-start.7 = (f32[64,1280]{1,0:T(8,128)S(1)}, f32[64,1280]{1,0:T(8,128)S(1)}, u32[]{:S(2)}, u32[]{:S(2)}) collective-permute-start(f32[64,1280]{1,0:T(8,128)S(1)} %collective-permute-done.6.refs_2_), channel_id=1, source_target_pairs={{0,32},{1,33},{2,34},{3,35},{4,36},{5,37},{6,38},{7,39},{8,232},{9... | collective-permute-start | bytes 983048 | tf_op jit(solution)/shard_map/ppermute | solution.py:45
  25.5 10.4 %collective-permute-start.17 = (f32[64,1280]{1,0:T(8,128)S(1)}, f32[64,1280]{1,0:T(8,128)S(1)}, u32[]{:S(2)}, u32[]{:S(2)}) collective-permute-start(f32[64,1280]{1,0:T(8,128)S(1)} %collective-permute-done.12.refs_2_), channel_id=1, source_target_pairs={{0,8},{1,9},{2,10},{3,11},{4,12},{5,13},{6,14},{7,15},{8,0},{9,1},... | collective-permute-start | bytes 983048 | tf_op jit(solution)/shard_map/ppermute | solution.py:45
  27.0 7.2 %collective-permute-start.13 = (f32[64,1280]{1,0:T(8,128)S(1)}, f32[64,1280]{1,0:T(8,128)S(1)}, u32[]{:S(2)}, u32[]{:S(2)}) collective-permute-start(f32[64,1280]{1,0:T(8,128)S(1)} %collective-permute-done.12.refs_2_), channel_id=1, source_target_pairs={{0,32},{1,33},{2,34},{3,35},{4,36},{5,37},{6,38},{7,39},{8,232},{9... | collective-permute-start | bytes 983048 | tf_op jit(solution)/shard_map/ppermute | solution.py:45
  30.2 10.0 %collective-permute-start.16 = (f32[64,1280]{1,0:T(8,128)S(1)}, f32[64,1280]{1,0:T(8,128)S(1)}, u32[]{:S(2)}, u32[]{:S(2)}) collective-permute-start(f32[64,1280]{1,0:T(8,128)S(1)} %collective-permute-done.7.refs_2_), channel_id=1, source_target_pairs={{0,8},{1,9},{2,10},{3,11},{4,12},{5,13},{6,14},{7,15},{8,0},{9,1},... | collective-permute-start | bytes 983048 | tf_op jit(solution)/shard_map/ppermute | solution.py:45
  31.8 6.2 %collective-permute-start.8 = (f32[64,1280]{1,0:T(8,128)S(1)}, f32[64,1280]{1,0:T(8,128)S(1)}, u32[]{:S(2)}, u32[]{:S(2)}) collective-permute-start(f32[64,1280]{1,0:T(8,128)S(1)} %collective-permute-done.7.refs_2_), channel_id=1, source_target_pairs={{0,32},{1,33},{2,34},{3,35},{4,36},{5,37},{6,38},{7,39},{8,232},{9... | collective-permute-start | bytes 983048 | tf_op jit(solution)/shard_map/ppermute | solution.py:45
  34.2 9.0 %collective-permute-start.14 = (f32[32,1280]{1,0:T(8,128)S(1)}, f32[32,1280]{1,0:T(8,128)S(1)}, u32[]{:S(2)}, u32[]{:S(2)}) collective-permute-start(f32[32,1280]{1,0:T(8,128)S(1)} %slice.57), channel_id=1, source_target_pairs={{0,32},{1,33},{2,34},{3,35},{4,36},{5,37},{6,38},{7,39},{8,232},{9... | collective-permute-start | bytes 491528 | tf_op jit(solution)/shard_map/ppermute | solution.py:45
  36.0 5.8 %collective-permute-start.15 = (f32[64,1280]{1,0:T(8,128)S(1)}, f32[64,1280]{1,0:T(8,128)S(1)}, u32[]{:S(2)}, u32[]{:S(2)}) collective-permute-start(f32[64,1280]{1,0:T(8,128)S(1)} %collective-permute-done.13.refs_2_), channel_id=1, source_target_pairs={{0,8},{1,9},{2,10},{3,11},{4,12},{5,13},{6,14},{7,15},{8,0},{9,1},... | collective-permute-start | bytes 983048 | tf_op jit(solution)/shard_map/ppermute | solution.py:45
  38.0 7.0 %collective-permute-start.9 = (f32[32,1280]{1,0:T(8,128)S(1)}, f32[32,1280]{1,0:T(8,128)S(1)}, u32[]{:S(2)}, u32[]{:S(2)}) collective-permute-start(f32[32,1280]{1,0:T(8,128)S(1)} %slice.56), channel_id=1, source_target_pairs={{0,32},{1,33},{2,34},{3,35},{4,36},{5,37},{6,38},{7,39},{8,232},{9... | collective-permute-start | bytes 491528 | tf_op jit(solution)/shard_map/ppermute | solution.py:45
  39.9 3.6 %collective-permute-start.10 = (f32[64,1280]{1,0:T(8,128)S(1)}, f32[64,1280]{1,0:T(8,128)S(1)}, u32[]{:S(2)}, u32[]{:S(2)}) collective-permute-start(f32[64,1280]{1,0:T(8,128)S(1)} %collective-permute-done.8.refs_2_), channel_id=1, source_target_pairs={{0,8},{1,9},{2,10},{3,11},{4,12},{5,13},{6,14},{7,15},{8,0},{9,1},... | collective-permute-start | bytes 983048 | tf_op jit(solution)/shard_map/ppermute | solution.py:45
  43.2 3.5 %collective-permute-start.21 = (f32[32,1280]{1,0:T(8,128)S(1)}, f32[32,1280]{1,0:T(8,128)S(1)}, u32[]{:S(2)}, u32[]{:S(2)}) collective-permute-start(f32[32,1280]{1,0:T(8,128)S(1)} %collective-permute-done.14.refs_2_), channel_id=1, source_target_pairs={{0,8},{1,9},{2,10},{3,11},{4,12},{5,13},{6,14},{7,15},{8,0},{9,1},... | collective-permute-start | bytes 491528 | tf_op jit(solution)/shard_map/ppermute | solution.py:45
  45.0 3.2 %collective-permute-start.20 = (f32[32,1280]{1,0:T(8,128)S(1)}, f32[32,1280]{1,0:T(8,128)S(1)}, u32[]{:S(2)}, u32[]{:S(2)}) collective-permute-start(f32[32,1280]{1,0:T(8,128)S(1)} %collective-permute-done.9.refs_3_), channel_id=1, source_target_pairs={{0,8},{1,9},{2,10},{3,11},{4,12},{5,13},{6,14},{7,15},{8,0},{9,1},... | collective-permute-start | bytes 491528 | tf_op jit(solution)/shard_map/ppermute | solution.py:45
  71.7 2.3 %collective-permute-start.22 = (f32[32,512]{1,0:T(8,128)S(1)}, f32[32,512]{1,0:T(8,128)S(1)}, u32[]{:S(2)}, u32[]{:S(2)}) collective-permute-start(f32[32,512]{1,0:T(8,128)S(1)} %constant_dynamic-slice_fusion), channel_id=1, source_target_pairs={{0,8},{1,9},{2,10},{3,11},{4,12},{5,13},{6,14},{7,15},{8,0},{9,1},... | collective-permute-start | bytes 196616 | tf_op jit(solution)/shard_map/ppermute | solution.py:45
  74.1 4.4 %collective-permute-start.23 = (f32[32,512]{1,0:T(8,128)S(1)}, f32[32,512]{1,0:T(8,128)S(1)}, u32[]{:S(2)}, u32[]{:S(2)}) collective-permute-start(f32[32,512]{1,0:T(8,128)S(1)} %dynamic-slice_add_fusion), channel_id=1, source_target_pairs={{0,20},{1,21},{2,22},{3,23},{4,16},{5,17},{6,18},{7,19},{8,28},{9,... | collective-permute-start | bytes 196616 | tf_op jit(solution)/shard_map/ppermute | solution.py:45
  78.5 3.2 %collective-permute-start.24 = (f32[32,512]{1,0:T(8,128)S(1)}, f32[32,512]{1,0:T(8,128)S(1)}, u32[]{:S(2)}, u32[]{:S(2)}) collective-permute-start(f32[32,512]{1,0:T(8,128)S(1)} %add.16), channel_id=1, source_target_pairs={{0,32},{1,33},{2,34},{3,35},{4,36},{5,37},{6,38},{7,39},{8,40},{9,... | collective-permute-start | bytes 196616 | tf_op jit(solution)/shard_map/ppermute | solution.py:45
  81.8 4.8 %collective-permute-start.25 = (f32[16,512]{1,0:T(8,128)S(1)}, f32[16,512]{1,0:T(8,128)S(1)}, u32[]{:S(2)}, u32[]{:S(2)}) collective-permute-start(f32[16,512]{1,0:T(8,128)S(1)} %get-tuple-element.88), channel_id=1, source_target_pairs={{0,64},{1,65},{2,66},{3,67},{4,68},{5,69},{6,70},{7,71},{8,72},{9,... | collective-permute-start | bytes 98312 | tf_op jit(solution)/shard_map/ppermute | solution.py:45
  84.3 4.9 %collective-permute-start.26 = (f32[16,512]{1,0:T(8,128)S(1)}, f32[16,512]{1,0:T(8,128)S(1)}, u32[]{:S(2)}, u32[]{:S(2)}) collective-permute-start(f32[16,512]{1,0:T(8,128)S(1)} %get-tuple-element.89), channel_id=1, source_target_pairs={{0,192},{1,193},{2,194},{3,195},{4,196},{5,197},{6,198},{7,199},{8... | collective-permute-start | bytes 98312 | tf_op jit(solution)/shard_map/ppermute | solution.py:45
  89.2 5.0 %collective-permute-start.27 = (f32[16,512]{1,0:T(8,128)S(1)}, f32[16,512]{1,0:T(8,128)S(1)}, u32[]{:S(2)}, u32[]{:S(2)}) collective-permute-start(f32[16,512]{1,0:T(8,128)S(1)} %get-tuple-element.86), channel_id=1, source_target_pairs={{0,192},{1,193},{2,194},{3,195},{4,196},{5,197},{6,198},{7,199},{8... | collective-permute-start | bytes 98312 | tf_op jit(solution)/shard_map/ppermute | solution.py:45
  91.5 3.7 %collective-permute-start.28 = (f32[16,512]{1,0:T(8,128)S(1)}, f32[16,512]{1,0:T(8,128)S(1)}, u32[]{:S(2)}, u32[]{:S(2)}) collective-permute-start(f32[16,512]{1,0:T(8,128)S(1)} %get-tuple-element.87), channel_id=1, source_target_pairs={{0,64},{1,65},{2,66},{3,67},{4,68},{5,69},{6,70},{7,71},{8,72},{9,... | collective-permute-start | bytes 98312 | tf_op jit(solution)/shard_map/ppermute | solution.py:45
  108.0 8.7 %collective-permute-start.29 = (f32[8,128,128]{2,1,0:T(8,128)S(1)}, f32[8,128,128]{2,1,0:T(8,128)S(1)}, u32[]{:S(2)}, u32[]{:S(2)}) collective-permute-start(f32[8,128,128]{2,1,0:T(8,128)S(1)} %slice.69), channel_id=1, source_target_pairs={{0,8},{1,9},{2,10},{3,11},{4,12},{5,13},{6,14},{7,15},{8,0},{9,1},... | collective-permute-start | bytes 1572872 | tf_op jit(solution)/shard_map/ppermute | solution.py:45
  (2 other events, 13.6 us)

commit v8 on v6

--- a/solution.py
+++ b/solution.py
@@ -215,17 +215,26 @@
 def unpack_head(where, pieces, partner):
     def body(where_ref, pieces_ref, partner_ref, out):
         core = where_ref[1]
-        for k in range(8):
-            block = lax.rem(k + 4 * where_ref[0], 8) * COLS
-            mine = pl.multiple_of(block + core * SHARD, SHARD)
-            other = pl.multiple_of(block + (1 - core) * SHARD, SHARD)
+        for i in range(4):
+            k = lax.rem(4 * (pl.program_id(0) + where_ref[0]) + i, 8)
+            mine = pl.multiple_of(i * COLS + core * SHARD, SHARD)
+            other = pl.multiple_of(i * COLS + (1 - core) * SHARD, SHARD)
             for q in range(4):
                 lanes = slice(128 * q, 128 * (q + 1))
                 here = slice(ROWS // 2 + SHARD * q, ROWS // 2 + SHARD * (q + 1))
                 out[pl.ds(mine, SHARD), lanes] = pieces_ref[k, here]
                 out[pl.ds(other, SHARD), lanes] = partner_ref[k, SHARD * q : SHARD * (q + 1)]
 
-    return small_call(body, (DS, DS), where, pieces, partner, scalars=1)
+    vmem = pl.BlockSpec(memory_space=pltpu.VMEM)
+    return pl.pallas_call(
+        body,
+        out_shape=jax.ShapeDtypeStruct((DS, DS), jnp.float32),
+        grid=(2,),
+        in_specs=[pl.BlockSpec(memory_space=pltpu.SMEM), vmem, vmem],
+        out_specs=pl.BlockSpec((DS // 2, DS), lambda i: (i, 0)),
+        compiler_params=pltpu.CompilerParams(vmem_limit_bytes=VMEM_LIMIT),
+        cost_estimate=pl.CostEstimate(flops=1024, bytes_accessed=1024 * 1024, transcendentals=0),
+    )(where, pieces, partner)
 
 
 def shards(image_student, image_teacher, text_features, text_teacher, head):

time: 115 us -> 115 us (level)
    pallas_call x3 -> x2, Pallas kernels: 3.66 us -> 2.06 us  [small_call(): pl.pallas_call(body, out_shape=jax.ShapeDtypeStruct(shape, jnp.float32),...]
    pallas_call x0 -> x1, Pallas kernels: none -> 1.55 us  [unpack_head(): pl.pallas_call(body, out_shape=jax.ShapeDtypeStruct((DS, DS), jnp.float32...]
where the time goes in v8:
time: 115 us
  starting transfers between devices  46 us (40%)
  blocking collectives  33 us (29%)
  Pallas kernels  17.4 us (15%)
  waiting for transfers between devices  13.8 us (12%)
  other arithmetic  2.61 us (2%)
    ppermute x28, starting transfers between devices, move(): return lax.ppermute(array, AXES, pairs)  46 us
    all_to_all x1, blocking collectives, shards(): got = lax.all_to_all(both, ('xl', 'y'), 0, 0, tiled=True)  19.8 us
    pallas_call x9, Pallas kernels, add_texts(): pl.pallas_call(body, out_shape=shapes, in_specs=in_specs, out_specs=[vmem...  13.8 us
    ppermute x28, waiting for transfers between devices, move(): return lax.ppermute(array, AXES, pairs)  13.8 us
    all_to_all x1, blocking collectives, shards(): pieces = lax.all_to_all(packed, ('xl', 'y'), 0, 0, tiled=True)  13.1 us
  transfers between devices with their start and end apart: 28, of which 9 were waited for; matrix products, arithmetic and copies ran while one was open for 2% of the time, Pallas kernels for 12%

profile of v8, /device:TPU:1, one launch (start us, length us, event | category | flops | bytes accessed | tf_op | source)
XLA Modules:
  0.0 114.7 jit_solution(11153843113689611723)
XLA Ops:
  0.7 3.3 %collective-permute-start = (f32[32,768]{1,0:T(8,128)}, f32[32,768]{1,0:T(8,128)S(1)}, u32[]{:S(2)}, u32[]{:S(2)}) collective-permute-start(f32[32,768]{1,0:T(8,128)} %param.8), channel_id=1, source_target_pairs={{0,8},{1,9},{2,10},{3,11},{4,12},{5,13},{6,14},{7,15},{8,0},{9,1},... | collective-permute-start | bytes 294920 | tf_op jit(solution)/shard_map/ppermute | solution.py:45
  5.1 1.9 %collective-permute-start.3 = (f32[32,512]{1,0:T(8,128)}, f32[32,512]{1,0:T(8,128)S(1)}, u32[]{:S(2)}, u32[]{:S(2)}) collective-permute-start(f32[32,512]{1,0:T(8,128)} %param.7), channel_id=1, source_target_pairs={{0,20},{1,21},{2,22},{3,23},{4,16},{5,17},{6,18},{7,19},{8,28},{9,... | collective-permute-start | bytes 196616 | tf_op jit(solution)/shard_map/ppermute | solution.py:45
  8.4 3.9 %collective-permute-start.11 = (f32[64,1280]{1,0:T(8,128)S(1)}, f32[64,1280]{1,0:T(8,128)S(1)}, u32[]{:S(2)}, u32[]{:S(2)}) collective-permute-start(f32[64,1280]{1,0:T(8,128)S(1)} %maximum_maximum_fusion.refs_2_), channel_id=1, source_target_pairs={{0,32},{1,33},{2,34},{3,35},{4,36},{5,37},{6,38},{7,39},{8,232},{9... | collective-permute-start | bytes 983048 | tf_op jit(solution)/shard_map/ppermute | solution.py:45
  13.8 4.2 %collective-permute-start.6 = (f32[64,1280]{1,0:T(8,128)S(1)}, f32[64,1280]{1,0:T(8,128)S(1)}, u32[]{:S(2)}, u32[]{:S(2)}) collective-permute-start(f32[64,1280]{1,0:T(8,128)S(1)} %maximum_maximum_fusion.1.refs_3_), channel_id=1, source_target_pairs={{0,32},{1,33},{2,34},{3,35},{4,36},{5,37},{6,38},{7,39},{8,232},{9... | collective-permute-start | bytes 983048 | tf_op jit(solution)/shard_map/ppermute | solution.py:45
  18.1 1.7 %collective-permute-start.12 = (f32[64,1280]{1,0:T(8,128)S(1)}, f32[64,1280]{1,0:T(8,128)S(1)}, u32[]{:S(2)}, u32[]{:S(2)}) collective-permute-start(f32[64,1280]{1,0:T(8,128)S(1)} %collective-permute-done.11.refs_2_), channel_id=1, source_target_pairs={{0,32},{1,33},{2,34},{3,35},{4,36},{5,37},{6,38},{7,39},{8,232},{9... | collective-permute-start | bytes 983048 | tf_op jit(solution)/shard_map/ppermute | solution.py:45
  22.0 1.5 %collective-permute-start.18 = (f32[64,1280]{1,0:T(8,128)S(1)}, f32[64,1280]{1,0:T(8,128)S(1)}, u32[]{:S(2)}, u32[]{:S(2)}) collective-permute-start(f32[64,1280]{1,0:T(8,128)S(1)} %collective-permute-done.6.refs_2_), channel_id=1, source_target_pairs={{0,8},{1,9},{2,10},{3,11},{4,12},{5,13},{6,14},{7,15},{8,0},{9,1},... | collective-permute-start | bytes 983048 | tf_op jit(solution)/shard_map/ppermute | solution.py:45
  23.5 1.7 %collective-permute-start.7 = (f32[64,1280]{1,0:T(8,128)S(1)}, f32[64,1280]{1,0:T(8,128)S(1)}, u32[]{:S(2)}, u32[]{:S(2)}) collective-permute-start(f32[64,1280]{1,0:T(8,128)S(1)} %collective-permute-done.6.refs_2_), channel_id=1, source_target_pairs={{0,32},{1,33},{2,34},{3,35},{4,36},{5,37},{6,38},{7,39},{8,232},{9... | collective-permute-start | bytes 983048 | tf_op jit(solution)/shard_map/ppermute | solution.py:45
  25.5 1.5 %collective-permute-start.17 = (f32[64,1280]{1,0:T(8,128)S(1)}, f32[64,1280]{1,0:T(8,128)S(1)}, u32[]{:S(2)}, u32[]{:S(2)}) collective-permute-start(f32[64,1280]{1,0:T(8,128)S(1)} %collective-permute-done.12.refs_2_), channel_id=1, source_target_pairs={{0,8},{1,9},{2,10},{3,11},{4,12},{5,13},{6,14},{7,15},{8,0},{9,1},... | collective-permute-start | bytes 983048 | tf_op jit(solution)/shard_map/ppermute | solution.py:45
  27.0 1.7 %collective-permute-start.13 = (f32[64,1280]{1,0:T(8,128)S(1)}, f32[64,1280]{1,0:T(8,128)S(1)}, u32[]{:S(2)}, u32[]{:S(2)}) collective-permute-start(f32[64,1280]{1,0:T(8,128)S(1)} %collective-permute-done.12.refs_2_), channel_id=1, source_target_pairs={{0,32},{1,33},{2,34},{3,35},{4,36},{5,37},{6,38},{7,39},{8,232},{9... | collective-permute-start | bytes 983048 | tf_op jit(solution)/shard_map/ppermute | solution.py:45
  28.7 1.5 %add_texts.10 = (f32[256,128]{1,0:T(8,128)S(1)}, f32[256,512]{1,0:T(8,128)S(1)}, f32[256,512]{1,0:T(8,128)S(1)}) custom-call(f32[256,512]{1,0:T(8,128)S(1)} %convolution_multiply_fusion.refs_0_.refs_1_, f32[256,768]{1,0:T(8,128)S(1)} %broadcast_multiply_fusion.refs_1_.refs_2_, f32[64,1280]{1,0:T(8,128)S(1)} %collective-permute-done.11.refs_2_, ...), custom_call_target="tpu_custom_call" | custom-call | flops 18119393280 | bytes 4194304 | tf_op jit(solution)/shard_map/add_texts/pallas_call | solution.py:152
  30.2 1.6 %collective-permute-start.16 = (f32[64,1280]{1,0:T(8,128)S(1)}, f32[64,1280]{1,0:T(8,128)S(1)}, u32[]{:S(2)}, u32[]{:S(2)}) collective-permute-start(f32[64,1280]{1,0:T(8,128)S(1)} %collective-permute-done.7.refs_2_), channel_id=1, source_target_pairs={{0,8},{1,9},{2,10},{3,11},{4,12},{5,13},{6,14},{7,15},{8,0},{9,1},... | collective-permute-start | bytes 983048 | tf_op jit(solution)/shard_map/ppermute | solution.py:45
  32.7 1.5 %add_texts.11 = (f32[256,128]{1,0:T(8,128)S(1)}, f32[256,512]{1,0:T(8,128)S(1)}, f32[256,512]{1,0:T(8,128)S(1)}) custom-call(f32[256,512]{1,0:T(8,128)S(1)} %convolution_multiply_fusion.refs_0_.refs_1_, f32[256,768]{1,0:T(8,128)S(1)} %broadcast_multiply_fusion.refs_1_.refs_2_, f32[64,1280]{1,0:T(8,128)S(1)} %collective-permute-done.6.refs_2_, ...), custom_call_target="tpu_custom_call" | custom-call | flops 18119393280 | bytes 4194304 | tf_op jit(solution)/shard_map/add_texts/pallas_call | solution.py:152
  34.2 1.8 %collective-permute-start.14 = (f32[32,1280]{1,0:T(8,128)S(1)}, f32[32,1280]{1,0:T(8,128)S(1)}, u32[]{:S(2)}, u32[]{:S(2)}) collective-permute-start(f32[32,1280]{1,0:T(8,128)S(1)} %slice.49), channel_id=1, source_target_pairs={{0,32},{1,33},{2,34},{3,35},{4,36},{5,37},{6,38},{7,39},{8,232},{9... | collective-permute-start | bytes 491528 | tf_op jit(solution)/shard_map/ppermute | solution.py:45
  36.0 1.5 %add_texts.12 = (f32[256,128]{1,0:T(8,128)S(1)}, f32[256,512]{1,0:T(8,128)S(1)}, f32[256,512]{1,0:T(8,128)S(1)}) custom-call(f32[256,512]{1,0:T(8,128)S(1)} %convolution_multiply_fusion.refs_0_.refs_1_, f32[256,768]{1,0:T(8,128)S(1)} %broadcast_multiply_fusion.refs_1_.refs_2_, f32[64,1280]{1,0:T(8,128)S(1)} %collective-permute-done.12.refs_2_, ...), custom_call_target="tpu_custom_call" | custom-call | flops 18119393280 | bytes 4194304 | tf_op jit(solution)/shard_map/add_texts/pallas_call | solution.py:152
  38.0 1.9 %collective-permute-start.9 = (f32[32,1280]{1,0:T(8,128)S(1)}, f32[32,1280]{1,0:T(8,128)S(1)}, u32[]{:S(2)}, u32[]{:S(2)}) collective-permute-start(f32[32,1280]{1,0:T(8,128)S(1)} %slice.48), channel_id=1, source_target_pairs={{0,32},{1,33},{2,34},{3,35},{4,36},{5,37},{6,38},{7,39},{8,232},{9... | collective-permute-start | bytes 491528 | tf_op jit(solution)/shard_map/ppermute | solution.py:45
  40.3 1.5 %add_texts.13 = (f32[256,128]{1,0:T(8,128)S(1)}, f32[256,512]{1,0:T(8,128)S(1)}, f32[256,512]{1,0:T(8,128)S(1)}) custom-call(f32[256,512]{1,0:T(8,128)S(1)} %convolution_multiply_fusion.refs_0_.refs_1_, f32[256,768]{1,0:T(8,128)S(1)} %broadcast_multiply_fusion.refs_1_.refs_2_, f32[64,1280]{1,0:T(8,128)S(1)} %collective-permute-done.7.refs_2_, ...), custom_call_target="tpu_custom_call" | custom-call | flops 18119393280 | bytes 4194304 | tf_op jit(solution)/shard_map/add_texts/pallas_call | solution.py:152
  41.7 1.5 %add_texts.14 = (f32[256,128]{1,0:T(8,128)S(1)}, f32[256,512]{1,0:T(8,128)S(1)}, f32[256,512]{1,0:T(8,128)S(1)}) custom-call(f32[256,512]{1,0:T(8,128)S(1)} %convolution_multiply_fusion.refs_0_.refs_1_, f32[256,768]{1,0:T(8,128)S(1)} %broadcast_multiply_fusion.refs_1_.refs_2_, f32[64,1280]{1,0:T(8,128)S(1)} %collective-permute-done.13.refs_2_, ...), custom_call_target="tpu_custom_call" | custom-call | flops 18119393280 | bytes 4194304 | tf_op jit(solution)/shard_map/add_texts/pallas_call | solution.py:152
  43.5 1.5 %add_texts.15 = (f32[256,128]{1,0:T(8,128)S(1)}, f32[256,512]{1,0:T(8,128)S(1)}, f32[256,512]{1,0:T(8,128)S(1)}) custom-call(f32[256,512]{1,0:T(8,128)S(1)} %convolution_multiply_fusion.refs_0_.refs_1_, f32[256,768]{1,0:T(8,128)S(1)} %broadcast_multiply_fusion.refs_1_.refs_2_, f32[64,1280]{1,0:T(8,128)S(1)} %collective-permute-done.8.refs_2_, ...), custom_call_target="tpu_custom_call" | custom-call | flops 18119393280 | bytes 4194304 | tf_op jit(solution)/shard_map/add_texts/pallas_call | solution.py:152
  45.0 1.7 %collective-permute-start.20 = (f32[32,1280]{1,0:T(8,128)S(1)}, f32[32,1280]{1,0:T(8,128)S(1)}, u32[]{:S(2)}, u32[]{:S(2)}) collective-permute-start(f32[32,1280]{1,0:T(8,128)S(1)} %collective-permute-done.9.refs_3_), channel_id=1, source_target_pairs={{0,8},{1,9},{2,10},{3,11},{4,12},{5,13},{6,14},{7,15},{8,0},{9,1},... | collective-permute-start | bytes 491528 | tf_op jit(solution)/shard_map/ppermute | solution.py:45
  48.2 2.3 %add_texts.17 = f32[8,264,128]{2,1,0:T(8,128)S(1)} custom-call(s32[8]{0:T(128)S(1)} %iota_xor_fusion.refs_0_, f32[256,512]{1,0:T(8,128)S(1)} %convolution_multiply_fusion.refs_0_.refs_1_, f32[256,768]{1,0:T(8,128)S(1)} %broadcast_multiply_fusion.refs_1_.refs_2_, f32[32,1280]{1,0:T(8,128)S(1)} %collective-permute-done.9.refs_3_, ...), custom_call_target="tpu_custom_call" | custom-call | flops 9059696640 | bytes 4194304 | tf_op jit(solution)/shard_map/add_texts/pallas_call | solution.py:152
  50.5 19.8 %all_to_all.10 = f32[8,264,128]{2,1,0:T(8,128)S(1)} all-to-all(f32[8,264,128]{2,1,0:T(8,128)S(1)} %add_texts.17), channel_id=1, replica_groups=mesh['z'=8,'xh'=2,'core'=2,'xl'=2,'y'=4] {'xl','y'}, dimensions={0} | all-to-all | bytes 2162688 | tf_op jit(solution)/shard_map/all_to_all | solution.py:272
  74.1 1.8 %collective-permute-start.23 = (f32[32,512]{1,0:T(8,128)S(1)}, f32[32,512]{1,0:T(8,128)S(1)}, u32[]{:S(2)}, u32[]{:S(2)}) collective-permute-start(f32[32,512]{1,0:T(8,128)S(1)} %dynamic-slice_add_fusion), channel_id=1, source_target_pairs={{0,20},{1,21},{2,22},{3,23},{4,16},{5,17},{6,18},{7,19},{8,28},{9,... | collective-permute-start | bytes 196616 | tf_op jit(solution)/shard_map/ppermute | solution.py:45
  75.9 2.6 %collective-permute-done.23 = f32[32,512]{1,0:T(8,128)S(1)} collective-permute-done((f32[32,512]{1,0:T(8,128)S(1)}, f32[32,512]{1,0:T(8,128)S(1)}, u32[]{:S(2)}, u32[]{:S(2)}) %collective-permute-start.23) | collective-permute-done | bytes 65568 | tf_op jit(solution)/shard_map/ppermute | solution.py:45
  78.6 3.1 %collective-permute-done.24 = f32[32,512]{1,0:T(8,128)S(1)} collective-permute-done((f32[32,512]{1,0:T(8,128)S(1)}, f32[32,512]{1,0:T(8,128)S(1)}, u32[]{:S(2)}, u32[]{:S(2)}) %collective-permute-start.24) | collective-permute-done | bytes 65568 | tf_op jit(solution)/shard_map/ppermute | solution.py:45
  81.7 2.6 %collective-permute-start.25 = (f32[32,512]{1,0:T(8,128)S(1)}, f32[32,512]{1,0:T(8,128)S(1)}, u32[]{:S(2)}, u32[]{:S(2)}) collective-permute-start(f32[32,512]{1,0:T(8,128)S(1)} %add.14), channel_id=1, source_target_pairs={{0,64},{1,65},{2,66},{3,67},{4,68},{5,69},{6,70},{7,71},{8,72},{9,... | collective-permute-start | bytes 196616 | tf_op jit(solution)/shard_map/ppermute | solution.py:45
  84.3 1.6 %collective-permute-done.25 = f32[32,512]{1,0:T(8,128)S(1)} collective-permute-done((f32[32,512]{1,0:T(8,128)S(1)}, f32[32,512]{1,0:T(8,128)S(1)}, u32[]{:S(2)}, u32[]{:S(2)}) %collective-permute-start.25) | collective-permute-done | bytes 65568 | tf_op jit(solution)/shard_map/ppermute | solution.py:45
  86.0 2.3 %collective-permute-start.26 = (f32[32,512]{1,0:T(8,128)S(1)}, f32[32,512]{1,0:T(8,128)S(1)}, u32[]{:S(2)}, u32[]{:S(2)}) collective-permute-start(f32[32,512]{1,0:T(8,128)S(1)} %add.15.term_ref), channel_id=1, source_target_pairs={{0,192},{1,193},{2,194},{3,195},{4,196},{5,197},{6,198},{7,199},{8... | collective-permute-start | bytes 196616 | tf_op jit(solution)/shard_map/ppermute | solution.py:45
  88.4 3.5 %collective-permute-done.26.received_ref = f32[32,512]{1,0:T(8,128)S(1)} collective-permute-done((f32[32,512]{1,0:T(8,128)S(1)}, f32[32,512]{1,0:T(8,128)S(1)}, u32[]{:S(2)}, u32[]{:S(2)}) %collective-permute-start.26) | collective-permute-done | bytes 65568 | tf_op jit(solution)/shard_map/ppermute | solution.py:45
  91.9 13.1 %all_to_all.11.pieces_ref = f32[8,256,128]{2,1,0:T(8,128)S(1)} all-to-all(f32[8,256,128]{2,1,0:T(8,128)S(1)} %shard_map.68), channel_id=1, replica_groups=mesh['z'=8,'xh'=2,'core'=2,'xl'=2,'y'=4] {'xl','y'}, dimensions={0} | all-to-all | bytes 2097152 | tf_op jit(solution)/shard_map/all_to_all | solution.py:292
  105.1 6.0 %collective-permute-start.27 = (f32[8,128,128]{2,1,0:T(8,128)S(1)}, f32[8,128,128]{2,1,0:T(8,128)S(1)}, u32[]{:S(2)}, u32[]{:S(2)}) collective-permute-start(f32[8,128,128]{2,1,0:T(8,128)S(1)} %slice.59), channel_id=1, source_target_pairs={{0,8},{1,9},{2,10},{3,11},{4,12},{5,13},{6,14},{7,15},{8,0},{9,1},... | collective-permute-start | bytes 1572872 | tf_op jit(solution)/shard_map/ppermute | solution.py:45
  111.2 2.0 %shard_map.69 = f32[256,512]{1,0:T(8,128)} custom-call(s32[2]{0:T(128)S(1)} %pad_add_fusion.where_ref, f32[8,256,128]{2,1,0:T(8,128)S(1)} %all_to_all.11.pieces_ref, f32[512,512]{1,0:T(8,128)S(1)} %copy-done.1), custom_call_target="tpu_custom_call" | custom-call | flops 1024 | bytes 1048576 | tf_op jit(solution)/shard_map/pallas_call | solution.py:174
  113.2 1.6 %shard_map.70 = f32[512,512]{1,0:T(8,128)} custom-call(s32[2]{0:T(128)S(1)} %pad_add_fusion.where_ref, f32[8,256,128]{2,1,0:T(8,128)S(1)} %all_to_all.11.pieces_ref, f32[8,128,128]{2,1,0:T(8,128)S(1)} %collective-permute-done.27.partner_ref), custom_call_target="tpu_custom_call" | custom-call | flops 1024 | bytes 1048576 | tf_op jit(solution)/shard_map/pallas_call | solution.py:229
  (70 shorter events, 14.2 us)
Async XLA Ops:
  0.6 12.2 %copy-start = (f32[256,512]{1,0:T(8,128)S(1)}, f32[256,512]{1,0:T(8,128)}, u32[]{:S(2)}) copy-start(f32[256,512]{1,0:T(8,128)} %param.5) | copy-start | bytes 1572868
  0.6 7.7 %copy-start.2 = (f32[32,768]{1,0:T(8,128)S(1)}, f32[32,768]{1,0:T(8,128)}, u32[]{:S(2)}) copy-start(f32[32,768]{1,0:T(8,128)} %param.8) | copy-start | bytes 294916
  0.7 7.7 %copy-start.3 = (f32[32,512]{1,0:T(8,128)S(1)}, f32[32,512]{1,0:T(8,128)}, u32[]{:S(2)}) copy-start(f32[32,512]{1,0:T(8,128)} %param.7) | copy-start | bytes 196612
  0.7 7.7 %collective-permute-start = (f32[32,768]{1,0:T(8,128)}, f32[32,768]{1,0:T(8,128)S(1)}, u32[]{:S(2)}, u32[]{:S(2)}) collective-permute-start(f32[32,768]{1,0:T(8,128)} %param.8), channel_id=1, source_target_pairs={{0,8},{1,9},{2,10},{3,11},{4,12},{5,13},{6,14},{7,15},{8,0},{9,1},... | collective-permute-start | bytes 294920 | tf_op jit(solution)/shard_map/ppermute | solution.py:45
  4.0 8.4 %collective-permute-start.2 = (f32[32,768]{1,0:T(8,128)}, f32[32,768]{1,0:T(8,128)S(1)}, u32[]{:S(2)}, u32[]{:S(2)}) collective-permute-start(f32[32,768]{1,0:T(8,128)} %param.8), channel_id=1, source_target_pairs={{0,20},{1,21},{2,22},{3,23},{4,16},{5,17},{6,18},{7,19},{8,28},{9,... | collective-permute-start | bytes 294920 | tf_op jit(solution)/shard_map/ppermute | solution.py:45
  4.8 3.6 %collective-permute-start.1 = (f32[32,512]{1,0:T(8,128)}, f32[32,512]{1,0:T(8,128)S(1)}, u32[]{:S(2)}, u32[]{:S(2)}) collective-permute-start(f32[32,512]{1,0:T(8,128)} %param.7), channel_id=1, source_target_pairs={{0,8},{1,9},{2,10},{3,11},{4,12},{5,13},{6,14},{7,15},{8,0},{9,1},... | collective-permute-start | bytes 196616 | tf_op jit(solution)/shard_map/ppermute | solution.py:45
  5.1 7.2 %collective-permute-start.3 = (f32[32,512]{1,0:T(8,128)}, f32[32,512]{1,0:T(8,128)S(1)}, u32[]{:S(2)}, u32[]{:S(2)}) collective-permute-start(f32[32,512]{1,0:T(8,128)} %param.7), channel_id=1, source_target_pairs={{0,20},{1,21},{2,22},{3,23},{4,16},{5,17},{6,18},{7,19},{8,28},{9,... | collective-permute-start | bytes 196616 | tf_op jit(solution)/shard_map/ppermute | solution.py:45
  7.1 5.8 %copy-start.1 = (f32[512,512]{1,0:T(8,128)S(1)}, f32[512,512]{1,0:T(8,128)}, u32[]{:S(2)}) copy-start(f32[512,512]{1,0:T(8,128)} %head_ref.1) | copy-start | bytes 3145732
  8.4 9.6 %collective-permute-start.11 = (f32[64,1280]{1,0:T(8,128)S(1)}, f32[64,1280]{1,0:T(8,128)S(1)}, u32[]{:S(2)}, u32[]{:S(2)}) collective-permute-start(f32[64,1280]{1,0:T(8,128)S(1)} %maximum_maximum_fusion.refs_2_), channel_id=1, source_target_pairs={{0,32},{1,33},{2,34},{3,35},{4,36},{5,37},{6,38},{7,39},{8,232},{9... | collective-permute-start | bytes 983048 | tf_op jit(solution)/shard_map/ppermute | solution.py:45
  12.4 1.4 %collective-permute-start.4 = (f32[32,768]{1,0:T(8,128)S(1)}, f32[32,768]{1,0:T(8,128)S(1)}, u32[]{:S(2)}, u32[]{:S(2)}) collective-permute-start(f32[32,768]{1,0:T(8,128)S(1)} %collective-permute-done.2), channel_id=1, source_target_pairs={{0,8},{1,9},{2,10},{3,11},{4,12},{5,13},{6,14},{7,15},{8,0},{9,1},... | collective-permute-start | bytes 294920 | tf_op jit(solution)/shard_map/ppermute | solution.py:45
  12.4 1.4 %collective-permute-start.5 = (f32[32,512]{1,0:T(8,128)S(1)}, f32[32,512]{1,0:T(8,128)S(1)}, u32[]{:S(2)}, u32[]{:S(2)}) collective-permute-start(f32[32,512]{1,0:T(8,128)S(1)} %collective-permute-done.3), channel_id=1, source_target_pairs={{0,8},{1,9},{2,10},{3,11},{4,12},{5,13},{6,14},{7,15},{8,0},{9,1},... | collective-permute-start | bytes 196616 | tf_op jit(solution)/shard_map/ppermute | solution.py:45
  13.8 8.2 %collective-permute-start.6 = (f32[64,1280]{1,0:T(8,128)S(1)}, f32[64,1280]{1,0:T(8,128)S(1)}, u32[]{:S(2)}, u32[]{:S(2)}) collective-permute-start(f32[64,1280]{1,0:T(8,128)S(1)} %maximum_maximum_fusion.1.refs_3_), channel_id=1, source_target_pairs={{0,32},{1,33},{2,34},{3,35},{4,36},{5,37},{6,38},{7,39},{8,232},{9... | collective-permute-start | bytes 983048 | tf_op jit(solution)/shard_map/ppermute | solution.py:45
  18.0 10.7 %collective-permute-start.19 = (f32[64,1280]{1,0:T(8,128)S(1)}, f32[64,1280]{1,0:T(8,128)S(1)}, u32[]{:S(2)}, u32[]{:S(2)}) collective-permute-start(f32[64,1280]{1,0:T(8,128)S(1)} %collective-permute-done.11.refs_2_), channel_id=1, source_target_pairs={{0,8},{1,9},{2,10},{3,11},{4,12},{5,13},{6,14},{7,15},{8,0},{9,1},... | collective-permute-start | bytes 983048 | tf_op jit(solution)/shard_map/ppermute | solution.py:45
  18.1 7.4 %collective-permute-start.12 = (f32[64,1280]{1,0:T(8,128)S(1)}, f32[64,1280]{1,0:T(8,128)S(1)}, u32[]{:S(2)}, u32[]{:S(2)}) collective-permute-start(f32[64,1280]{1,0:T(8,128)S(1)} %collective-permute-done.11.refs_2_), channel_id=1, source_target_pairs={{0,32},{1,33},{2,34},{3,35},{4,36},{5,37},{6,38},{7,39},{8,232},{9... | collective-permute-start | bytes 983048 | tf_op jit(solution)/shard_map/ppermute | solution.py:45
  22.0 10.7 %collective-permute-start.18 = (f32[64,1280]{1,0:T(8,128)S(1)}, f32[64,1280]{1,0:T(8,128)S(1)}, u32[]{:S(2)}, u32[]{:S(2)}) collective-permute-start(f32[64,1280]{1,0:T(8,128)S(1)} %collective-permute-done.6.refs_2_), channel_id=1, source_target_pairs={{0,8},{1,9},{2,10},{3,11},{4,12},{5,13},{6,14},{7,15},{8,0},{9,1},... | collective-permute-start | bytes 983048 | tf_op jit(solution)/shard_map/ppermute | solution.py:45
  23.5 6.7 %collective-permute-start.7 = (f32[64,1280]{1,0:T(8,128)S(1)}, f32[64,1280]{1,0:T(8,128)S(1)}, u32[]{:S(2)}, u32[]{:S(2)}) collective-permute-start(f32[64,1280]{1,0:T(8,128)S(1)} %collective-permute-done.6.refs_2_), channel_id=1, source_target_pairs={{0,32},{1,33},{2,34},{3,35},{4,36},{5,37},{6,38},{7,39},{8,232},{9... | collective-permute-start | bytes 983048 | tf_op jit(solution)/shard_map/ppermute | solution.py:45
  25.5 10.4 %collective-permute-start.17 = (f32[64,1280]{1,0:T(8,128)S(1)}, f32[64,1280]{1,0:T(8,128)S(1)}, u32[]{:S(2)}, u32[]{:S(2)}) collective-permute-start(f32[64,1280]{1,0:T(8,128)S(1)} %collective-permute-done.12.refs_2_), channel_id=1, source_target_pairs={{0,8},{1,9},{2,10},{3,11},{4,12},{5,13},{6,14},{7,15},{8,0},{9,1},... | collective-permute-start | bytes 983048 | tf_op jit(solution)/shard_map/ppermute | solution.py:45
  27.0 7.2 %collective-permute-start.13 = (f32[64,1280]{1,0:T(8,128)S(1)}, f32[64,1280]{1,0:T(8,128)S(1)}, u32[]{:S(2)}, u32[]{:S(2)}) collective-permute-start(f32[64,1280]{1,0:T(8,128)S(1)} %collective-permute-done.12.refs_2_), channel_id=1, source_target_pairs={{0,32},{1,33},{2,34},{3,35},{4,36},{5,37},{6,38},{7,39},{8,232},{9... | collective-permute-start | bytes 983048 | tf_op jit(solution)/shard_map/ppermute | solution.py:45
  30.2 10.0 %collective-permute-start.16 = (f32[64,1280]{1,0:T(8,128)S(1)}, f32[64,1280]{1,0:T(8,128)S(1)}, u32[]{:S(2)}, u32[]{:S(2)}) collective-permute-start(f32[64,1280]{1,0:T(8,128)S(1)} %collective-permute-done.7.refs_2_), channel_id=1, source_target_pairs={{0,8},{1,9},{2,10},{3,11},{4,12},{5,13},{6,14},{7,15},{8,0},{9,1},... | collective-permute-start | bytes 983048 | tf_op jit(solution)/shard_map/ppermute | solution.py:45
  31.8 6.2 %collective-permute-start.8 = (f32[64,1280]{1,0:T(8,128)S(1)}, f32[64,1280]{1,0:T(8,128)S(1)}, u32[]{:S(2)}, u32[]{:S(2)}) collective-permute-start(f32[64,1280]{1,0:T(8,128)S(1)} %collective-permute-done.7.refs_2_), channel_id=1, source_target_pairs={{0,32},{1,33},{2,34},{3,35},{4,36},{5,37},{6,38},{7,39},{8,232},{9... | collective-permute-start | bytes 983048 | tf_op jit(solution)/shard_map/ppermute | solution.py:45
  34.2 9.0 %collective-permute-start.14 = (f32[32,1280]{1,0:T(8,128)S(1)}, f32[32,1280]{1,0:T(8,128)S(1)}, u32[]{:S(2)}, u32[]{:S(2)}) collective-permute-start(f32[32,1280]{1,0:T(8,128)S(1)} %slice.49), channel_id=1, source_target_pairs={{0,32},{1,33},{2,34},{3,35},{4,36},{5,37},{6,38},{7,39},{8,232},{9... | collective-permute-start | bytes 491528 | tf_op jit(solution)/shard_map/ppermute | solution.py:45
  36.0 5.8 %collective-permute-start.15 = (f32[64,1280]{1,0:T(8,128)S(1)}, f32[64,1280]{1,0:T(8,128)S(1)}, u32[]{:S(2)}, u32[]{:S(2)}) collective-permute-start(f32[64,1280]{1,0:T(8,128)S(1)} %collective-permute-done.13.refs_2_), channel_id=1, source_target_pairs={{0,8},{1,9},{2,10},{3,11},{4,12},{5,13},{6,14},{7,15},{8,0},{9,1},... | collective-permute-start | bytes 983048 | tf_op jit(solution)/shard_map/ppermute | solution.py:45
  38.0 7.0 %collective-permute-start.9 = (f32[32,1280]{1,0:T(8,128)S(1)}, f32[32,1280]{1,0:T(8,128)S(1)}, u32[]{:S(2)}, u32[]{:S(2)}) collective-permute-start(f32[32,1280]{1,0:T(8,128)S(1)} %slice.48), channel_id=1, source_target_pairs={{0,32},{1,33},{2,34},{3,35},{4,36},{5,37},{6,38},{7,39},{8,232},{9... | collective-permute-start | bytes 491528 | tf_op jit(solution)/shard_map/ppermute | solution.py:45
  39.9 3.6 %collective-permute-start.10 = (f32[64,1280]{1,0:T(8,128)S(1)}, f32[64,1280]{1,0:T(8,128)S(1)}, u32[]{:S(2)}, u32[]{:S(2)}) collective-permute-start(f32[64,1280]{1,0:T(8,128)S(1)} %collective-permute-done.8.refs_2_), channel_id=1, source_target_pairs={{0,8},{1,9},{2,10},{3,11},{4,12},{5,13},{6,14},{7,15},{8,0},{9,1},... | collective-permute-start | bytes 983048 | tf_op jit(solution)/shard_map/ppermute | solution.py:45
  43.2 3.5 %collective-permute-start.21 = (f32[32,1280]{1,0:T(8,128)S(1)}, f32[32,1280]{1,0:T(8,128)S(1)}, u32[]{:S(2)}, u32[]{:S(2)}) collective-permute-start(f32[32,1280]{1,0:T(8,128)S(1)} %collective-permute-done.14.refs_2_), channel_id=1, source_target_pairs={{0,8},{1,9},{2,10},{3,11},{4,12},{5,13},{6,14},{7,15},{8,0},{9,1},... | collective-permute-start | bytes 491528 | tf_op jit(solution)/shard_map/ppermute | solution.py:45
  45.0 3.2 %collective-permute-start.20 = (f32[32,1280]{1,0:T(8,128)S(1)}, f32[32,1280]{1,0:T(8,128)S(1)}, u32[]{:S(2)}, u32[]{:S(2)}) collective-permute-start(f32[32,1280]{1,0:T(8,128)S(1)} %collective-permute-done.9.refs_3_), channel_id=1, source_target_pairs={{0,8},{1,9},{2,10},{3,11},{4,12},{5,13},{6,14},{7,15},{8,0},{9,1},... | collective-permute-start | bytes 491528 | tf_op jit(solution)/shard_map/ppermute | solution.py:45
  71.7 2.3 %collective-permute-start.22 = (f32[32,512]{1,0:T(8,128)S(1)}, f32[32,512]{1,0:T(8,128)S(1)}, u32[]{:S(2)}, u32[]{:S(2)}) collective-permute-start(f32[32,512]{1,0:T(8,128)S(1)} %constant_dynamic-slice_fusion), channel_id=1, source_target_pairs={{0,8},{1,9},{2,10},{3,11},{4,12},{5,13},{6,14},{7,15},{8,0},{9,1},... | collective-permute-start | bytes 196616 | tf_op jit(solution)/shard_map/ppermute | solution.py:45
  74.1 4.4 %collective-permute-start.23 = (f32[32,512]{1,0:T(8,128)S(1)}, f32[32,512]{1,0:T(8,128)S(1)}, u32[]{:S(2)}, u32[]{:S(2)}) collective-permute-start(f32[32,512]{1,0:T(8,128)S(1)} %dynamic-slice_add_fusion), channel_id=1, source_target_pairs={{0,20},{1,21},{2,22},{3,23},{4,16},{5,17},{6,18},{7,19},{8,28},{9,... | collective-permute-start | bytes 196616 | tf_op jit(solution)/shard_map/ppermute | solution.py:45
  78.5 3.2 %collective-permute-start.24 = (f32[32,512]{1,0:T(8,128)S(1)}, f32[32,512]{1,0:T(8,128)S(1)}, u32[]{:S(2)}, u32[]{:S(2)}) collective-permute-start(f32[32,512]{1,0:T(8,128)S(1)} %add.13), channel_id=1, source_target_pairs={{0,32},{1,33},{2,34},{3,35},{4,36},{5,37},{6,38},{7,39},{8,40},{9,... | collective-permute-start | bytes 196616 | tf_op jit(solution)/shard_map/ppermute | solution.py:45
  81.7 4.2 %collective-permute-start.25 = (f32[32,512]{1,0:T(8,128)S(1)}, f32[32,512]{1,0:T(8,128)S(1)}, u32[]{:S(2)}, u32[]{:S(2)}) collective-permute-start(f32[32,512]{1,0:T(8,128)S(1)} %add.14), channel_id=1, source_target_pairs={{0,64},{1,65},{2,66},{3,67},{4,68},{5,69},{6,70},{7,71},{8,72},{9,... | collective-permute-start | bytes 196616 | tf_op jit(solution)/shard_map/ppermute | solution.py:45
  86.0 5.9 %collective-permute-start.26 = (f32[32,512]{1,0:T(8,128)S(1)}, f32[32,512]{1,0:T(8,128)S(1)}, u32[]{:S(2)}, u32[]{:S(2)}) collective-permute-start(f32[32,512]{1,0:T(8,128)S(1)} %add.15.term_ref), channel_id=1, source_target_pairs={{0,192},{1,193},{2,194},{3,195},{4,196},{5,197},{6,198},{7,199},{8... | collective-permute-start | bytes 196616 | tf_op jit(solution)/shard_map/ppermute | solution.py:45
  105.1 8.0 %collective-permute-start.27 = (f32[8,128,128]{2,1,0:T(8,128)S(1)}, f32[8,128,128]{2,1,0:T(8,128)S(1)}, u32[]{:S(2)}, u32[]{:S(2)}) collective-permute-start(f32[8,128,128]{2,1,0:T(8,128)S(1)} %slice.59), channel_id=1, source_target_pairs={{0,8},{1,9},{2,10},{3,11},{4,12},{5,13},{6,14},{7,15},{8,0},{9,1},... | collective-permute-start | bytes 1572872 | tf_op jit(solution)/shard_map/ppermute | solution.py:45
